TPU v7x, 32 devices: a whole 2x2x4 slice. The times are simulated.
32 devices in a mesh: section: 2 (over core), dp: 4 (over z), tensor: 4 (over y, x).
Axes of the slice: x: 2, y: 2, z: 4, core: 2. Of those that a mesh axis runs over, the one named last changes fastest.
Arguments:
- inputs: bfloat16 [16, 512, 768], P('dp', 'tensor'), may hold values from -6 to 6
- cls_pos: int32 [16, 4], P('dp'), may hold values from 0 to 496, as said below
- w_qkv: bfloat16 [2, 768, 3, 768], P('section', 'dp', None, 'tensor'), may hold values from -0.21875 to 0.21875
- qv_bias: bfloat16 [2, 2, 4, 192], P('section', None, 'tensor', 'dp'), may hold values from -3 to 3
- w_out: bfloat16 [2, 768, 768], P('section', 'tensor', 'dp'), may hold values from -0.875 to 0.875
- w_in: bfloat16 [2, 768, 3072], P('section', 'dp', 'tensor'), may hold values from -0.21875 to 0.21875
- in_bias: bfloat16 [2, 4, 768], P('section', 'tensor', 'dp'), may hold values from -3 to 3
- w_ffn_out: bfloat16 [2, 3072, 768], P('section', 'tensor', 'dp'), may hold values from -0.109375 to 0.109375
- layer_gains: bfloat16 [2, 2, 768], P('section', None, ('dp', 'tensor')), may hold values from 0.5 to 1.5
- shifts: bfloat16 [2, 4, 768], P('section', None, ('dp', 'tensor')), may hold values from -3 to 3
- queries: bfloat16 [64, 768], P(('dp', 'tensor')), may hold values from -0.59765625 to 0.59765625
- positive: int32 [64], P(('dp', 'tensor')), may hold values from 0 to 63
- token_grad: bfloat16 [16, 512, 768], P('dp', 'tensor'), may hold values from -6 to 6
Outputs:
- grad_qkv: float32 [2, 768, 3, 768], P('section', 'dp', None, 'tensor')
- grad_qv_bias: float32 [2, 2, 4, 192], P('section', None, 'tensor', 'dp')
- grad_out: float32 [2, 768, 768], P('section', 'tensor', 'dp')
- grad_in: float32 [2, 768, 3072], P('section', 'dp', 'tensor')
- grad_in_bias: float32 [2, 4, 768], P('section', 'tensor', 'dp')
- grad_ffn_out: float32 [2, 3072, 768], P('section', 'tensor', 'dp')
- grad_gains: float32 [2, 2, 768], P('section', None, ('dp', 'tensor'))
- grad_shifts: float32 [2, 4, 768], P('section', None, ('dp', 'tensor'))
- boundary: float32 [2, 16, 512, 768], P('section', 'dp', 'tensor')
- mean_loss: float32 [], replicated
Inputs may be any that keep to these rules, and one draw needn't show every extreme that they name: `cls_pos`: in each row the entries rise and the first is 0; each passage (up to the next entry, the last up to 512) has 16 tokens or more.
All inputs are finite; a program needn't handle non-finite values.
Results may differ from a plain program's by a relative error of at most 0.02.
Values may be sent and summed in bfloat16 or wider, within the bound.
No kernel may reach another device: no remote copies, remote signals or barrier semaphores. Data moves between devices by JAX's collectives and lax.ppermute only.
A program may use at most 192 MiB of HBM per device.

v0:
```python
import jax
import jax.numpy as jnp
from jax import lax
from jax.experimental import pallas as pl
from jax.experimental.pallas import tpu as pltpu
from jax.sharding import PartitionSpec as P

HD = 64
PARTNER = 1
CROSS = 2
BF16 = jnp.bfloat16
F32 = jnp.float32


def mm(left, right, dims):
    return lax.dot_general(left, right, (dims, ((), ())), preferred_element_type=F32)


def nn(left, right):
    return mm(left, right, ((1,), (0,)))


def nt(left, right):
    return mm(left, right, ((1,), (1,)))


def after(block, *earlier):
    return lax.optimization_barrier((block, *earlier))[0]


def swap_cores(block):
    return lax.ppermute(block, "section", [(0, 1), (1, 0)])


def hop(block, axis, flip):
    return lax.ppermute(block, axis, [(i, i ^ flip) for i in range(lax.axis_size(axis))])


def core_hop(block, axis, flip, core):
    size = lax.axis_size(axis)
    route = [(core * size + i, core * size + (i ^ flip)) for i in range(size)]
    return lax.ppermute(block, ("section", axis), route)


def cross_hop(block, source):
    size = lax.axis_size("tensor")
    route = [(source * size + i, (1 - source) * size + (i ^ CROSS)) for i in range(size)]
    return lax.ppermute(block, ("section", "tensor"), route)


def direct_dp():
    return lax.axis_size("dp") == 4


def dp_order():
    size = lax.axis_size("dp")
    if direct_dp():
        return lax.axis_index("dp") ^ jnp.arange(size, dtype=jnp.int32)
    return jnp.arange(size, dtype=jnp.int32)


def spread_dp(block):
    if direct_dp():
        return jnp.stack([block] + [hop(block, "dp", k) for k in range(1, 4)])
    return lax.all_gather(block, "dp", axis=0, tiled=False)


def spread_tensor(block):
    return jnp.stack([block] + [hop(block, "tensor", k) for k in range(1, 4)])


def double(block, axis):
    pair = jnp.stack([block, hop(block, axis, 1)])
    return jnp.concatenate([pair, hop(pair, axis, 2)])


def exchange_rows(blocks):
    first = hop(jnp.stack([blocks[1], blocks[3]]), "tensor", 1)
    second = hop(jnp.stack([blocks[2], first[1]]), "tensor", 2)
    return [blocks[0], first[0], second[0], second[1]]


def cross_all(block):
    size = lax.axis_size("tensor")
    route = [(s * size + i, (1 - s) * size + (i ^ CROSS)) for s in range(2) for i in range(size)]
    return lax.ppermute(block, ("section", "tensor"), route)


def rest_dp(own):
    return [hop(own, "dp", k) for k in range(1, 4)]


def gather_own(own):
    near, far = hop(own, "tensor", PARTNER), cross_all(own)
    return near, far


def gather_own_both(near, far):
    half = near.shape[1] // 2
    return cross_all(near[:, :half]), hop(far[:, half:], "tensor", PARTNER)


def gather_near(rest):
    a, b = rest
    near_a, far_b = hop(a, "tensor", PARTNER), cross_all(b)
    near_b, far_a = hop(b, "tensor", PARTNER), cross_all(a)
    return near_a, near_b, far_a, far_b


def gather_both(near_a, far_b):
    return cross_all(near_a), hop(far_b, "tensor", PARTNER)


def add_low(*items):
    total = items[0].astype(F32)
    for item in items[1:]:
        total = total + item.astype(F32)
    return total.astype(BF16)


class Reduction:
    def __init__(self, grads, core):
        self.core = core
        self.pair, self.next_b, self.own_b = grads
        self.got = cross_hop(self.pair, 1 - core)
        self.near_b = hop(self.next_b, "tensor", PARTNER)

    def first(self, *earlier):
        half = self.next_b.shape[0]
        self.parts = pair, own_b, got, near_b = after((self.pair, self.own_b, self.got, self.near_b), *earlier)
        self.added = add_low(pair[:half], got[:half]), add_low(own_b, near_b)
        self.near_a = core_hop(self.added[0], "tensor", PARTNER, self.core)
        self.far_b = cross_hop(self.added[1], 1 - self.core)
        return self.added

    def sum_halves(self, *earlier):
        half = self.next_b.shape[0]
        near_a, far_b, (pair, own_b, got, near_b) = after((self.near_a, self.far_b, self.parts), *earlier)
        return add_low(pair[half:], got[half:], near_a), add_low(own_b, near_b, far_b)

    def scatter(self):
        whole = jnp.concatenate(self.sums).reshape(-1, self.own_b.shape[2])
        return [lax.psum_scatter(whole, "dp", scatter_dimension=0, tiled=True)]

    def second_direct(self, *earlier):
        a, b = self.sums = self.sum_halves(*earlier)
        if direct_dp():
            self.hops = [
                core_hop(block, "dp", k, self.core) for k, block in ((1, a[1]), (2, b[0]), (3, b[1]))
            ]
        return self.sums

    def third_direct(self, *earlier):
        if not direct_dp():
            return sum(p.astype(F32) for p in self.scatter())
        return sum(p.astype(F32) for p in after([self.sums[0][0], *self.hops], *earlier))

    def second(self, *earlier):
        self.sums = self.sum_halves(*earlier)
        if direct_dp():
            self.across = core_hop(self.sums[1], "dp", 2, self.core)
        return self.sums

    def third(self, *earlier):
        if not direct_dp():
            self.pieces = self.scatter()
            return self.pieces
        a, across = after((self.sums[0], self.across), *earlier)
        self.pieces = [add_low(a[k], across[k]) for k in range(2)]
        return self.pieces


def last_dp(reductions, *earlier):
    if not direct_dp():
        return [r.pieces for r in reductions]
    high = max(r.pieces[0].shape[0] for r in reductions)
    block = [jnp.pad(r.pieces[1], ((0, high - r.pieces[1].shape[0]), (0, 0))) for r in reductions]
    got = core_hop(after(jnp.concatenate(block, 1), *earlier), "dp", 1, reductions[0].core)
    at, out = 0, []
    for r in reductions:
        rows, width = r.pieces[0].shape
        out.append([r.pieces[0], got[:rows, at : at + width]])
        at += width
    return out


VMEM_LIMIT = 48 * 1024 * 1024
CHUNK = 128


def takes(micros):
    return pl.CostEstimate(flops=int(micros * 1.1e9), bytes_accessed=0, transcendentals=0)


def params():
    return pltpu.CompilerParams(vmem_limit_bytes=VMEM_LIMIT)


ANY = pl.BlockSpec(memory_space=pl.ANY)
VM = pl.BlockSpec(memory_space=pltpu.VMEM)
SM = pl.BlockSpec(memory_space=pltpu.SMEM)


def sds(shape, dtype):
    return jax.ShapeDtypeStruct(shape, dtype)


def chunks(length, step=CHUNK):
    return [slice(i, i + step) for i in range(0, length, step)]


def norm_rows(z):
    centre = z - jnp.mean(z, -1, keepdims=True)
    spread = jnp.mean(centre * centre, -1, keepdims=True)
    scale = lax.rsqrt(spread + 1e-05)
    return centre * scale, scale


def norm_back_rows(d_out, gain, xhat, scale):
    g = d_out * gain
    m1 = jnp.mean(g, -1, keepdims=True)
    m2 = jnp.mean(g * xhat, -1, keepdims=True)
    return scale * (g - m1 - xhat * m2)


def gelu_parts(x):
    e = jnp.exp(-0.5 * x * x)
    t = 1.0 / (1.0 + 0.2316418882 * jnp.abs(x))
    poly = t * (
        0.127414796 + t * (-0.142248368 + t * (0.7107068705 + t * (-0.7265760135 + t * 0.5307027145)))
    )
    tail = poly * e
    cdf = jnp.where(x < 0.0, tail, 1.0 - tail)
    return x * cdf, cdf + x * e * 0.3989422804014327


def zrows(meta, k, rz):
    return pl.ds(pl.multiple_of(meta[1 + k], 64), rz)


def cut(start, width, at):
    if start < at < start + width:
        return [(start, at - start), (at, start + width - at)]
    return [(start, width)]


def load_weights(meta, pieces, base, places, sems):
    own, near0, far0, a0, b0, *halves = pieces
    rest, near, far, both = halves[0:2], halves[2:4], halves[4:6], halves[6:8]
    split0, split, count = a0.shape[1], both[0].shape[2], rest[0].shape[0]
    home = meta[0] == 1
    lists = [[] for _ in places]
    at = 0
    for j in range(2):
        for k in range(count + 1):
            rows = zrows(meta, k, own.shape[0])
            for n, (start, width, place) in enumerate(places):
                offset = 0 if k else base
                for g, w in cut(offset + start, width, split if k else split0):
                    side, column = divmod(g, split if k else split0)
                    if k == 0:
                        mine = (near0 if j else own).at[:, pl.ds(g, w)]
                        other = (a0, b0)[side].at[:, pl.ds(column, w)] if j else far0.at[:, pl.ds(g, w)]
                    else:
                        mine, other = (
                            v[side].at[k - 1, :, pl.ds(g if v[0].shape[2] > split else column, w)]
                            for v in ((near, both) if j else (rest, far))
                        )
                    dst = place(j, rows, g - offset - start, w)
                    first = pltpu.make_async_copy(mine, dst, sems.at[at])
                    second = pltpu.make_async_copy(other, dst, sems.at[at])
                    at += 1

                    @pl.when(home)
                    def _():
                        first.start()

                    @pl.when(jnp.logical_not(home))
                    def _():
                        second.start()

                    lists[n].append(first)
    return lists


def copies_of(rest):
    return 2 * 3 * (1 + rest.shape[0])


def wait_all(waits):
    for made in waits:
        made.wait()


def load_a(meta, pieces, w_a, sems):
    width = w_a.shape[2]
    return load_weights(
        meta, pieces, 0, [(0, width, lambda j, rows, c, w: w_a.at[j, rows, pl.ds(c, w)])], sems
    )[0]


def load_b(meta, pieces, w_i, w_f, sems):
    one = w_i.shape[1] // 2
    base = pieces[0].shape[1] - 2 * one
    return load_weights(
        meta,
        pieces,
        base,
        [
            (0, one, lambda j, rows, c, w: w_i.at[rows, pl.ds(j * one + c, w)]),
            (one, one, lambda j, rows, c, w: w_f.at[rows, pl.ds(j * one + c, w)]),
        ],
        sems,
    )


def attn_forward(level, meta, x_or_mid, parts, norms, pieces, bias, seg_col, seg_row, cols):
    four = 4 * cols
    length, width = x_or_mid.shape
    three = 3 * cols
    heads = 2 * cols // HD

    def body(meta, *refs):
        refs = list(refs)
        src = refs.pop(0)
        if level:
            own, other, gain, shift = (refs.pop(0) for _ in range(4))
        pieces = [refs.pop(0) for _ in range(13)]
        bias, sc, sr = (refs.pop(0) for _ in range(3))
        part_out, qkv_out, probs_out, ctx_out = (refs.pop(0) for _ in range(4))
        if level:
            x_out, xhat_out, scale_out = (refs.pop(0) for _ in range(3))
        w_a, sems = refs
        waits = load_a(meta, pieces, w_a, sems)
        if level:
            for rows in chunks(length):
                z = src[rows, :] + (own[rows, :].astype(F32) + other[rows, :].astype(F32)) + shift[2:3, :]
                xhat, scale = norm_rows(z)
                x_out[rows, :] = (xhat * gain[1:2, :] + shift[3:4, :]).astype(BF16)
                xhat_out[rows, :] = xhat.astype(BF16)
                scale_out[rows, :] = scale
            x_ref = x_out
        else:
            x_ref = src
        wait_all(waits)
        for j in range(2):
            c = slice(j * three, (j + 1) * three)
            for rows in chunks(length, 256):
                qkv_out[rows, c] = (nn(x_ref[rows, :], w_a[j, :, :three]) + bias[:, c]).astype(BF16)
        v_t = jnp.concatenate(
            [qkv_out[:, j * three + 2 * cols : (j + 1) * three].astype(F32) for j in range(2)], 1
        ).T.astype(BF16)
        for queries in chunks(length, 256):
            same = sc[...] == sr[:, queries]
            outs = []
            for h in range(heads):
                j, i = divmod(h, cols // HD)
                at = j * three + i * HD
                q = qkv_out[queries, at : at + HD]
                k = qkv_out[:, at + cols : at + cols + HD]
                st = jnp.where(same, nt(k, q) * 0.125, -1e30)
                p = jnp.exp(st - jnp.max(st, 0, keepdims=True))
                p = (p * (1.0 / jnp.sum(p, 0, keepdims=True))).astype(BF16)
                probs_out[h, :, queries] = p
                outs.append(nn(v_t[h * HD : (h + 1) * HD], p))
            ctx = jnp.concatenate(outs, 0).T.astype(BF16)
            ctx_out[queries, :] = ctx
            part_out[queries, :] = (
                nt(ctx[:, :cols], w_a[0, :, three:]) + nt(ctx[:, cols:], w_a[1, :, three:])
            ).astype(BF16)

    outs = [
        sds((length, width), BF16), sds((length, 2 * three), BF16),
        sds((heads, length, length), BF16), sds((length, 2 * cols), BF16),
    ]
    args = [meta, x_or_mid]
    if level:
        args += [*parts, *norms]
        outs += [sds((length, width), BF16), sds((length, width), BF16), sds((length, 1), F32)]
    specs = [SM] + [VM] * (len(args) - 1) + [ANY] * 13 + [VM] * 3
    args += [*pieces, bias, seg_col, seg_row]
    return pl.pallas_call(
        body,
        out_shape=outs,
        in_specs=specs,
        out_specs=[VM] * len(outs),
        scratch_shapes=[pltpu.VMEM((2, width, four), BF16), pltpu.SemaphoreType.DMA((copies_of(pieces[5]),))],
        compiler_params=params(),
        cost_estimate=takes(13),
        name="attn_forward",
    )(*args)


def ffn_forward(meta, x, parts, gains, shifts, pieces, bias_in, half):
    units = 2 * half
    length, width = x.shape

    def body(meta, x, own, other, gain, shift, p0, p1, p2, p3, p4, p5, p6, p7, p8, p9, p10, p11, p12, bias,
             part_out, mid_out, xhat_out, scale_out, act_out, slope_out, w_i, w_f, low, sems):
        first, second = load_b(meta, (p0, p1, p2, p3, p4, p5, p6, p7, p8, p9, p10, p11, p12), w_i, w_f, sems)
        for rows in chunks(length):
            z = x[rows, :].astype(F32) + (own[rows, :].astype(F32) + other[rows, :].astype(F32)) + shift[0:1, :]
            xhat, scale = norm_rows(z)
            mid = xhat * gain[0:1, :] + shift[1:2, :]
            mid_out[rows, :] = mid
            low[rows, :] = mid.astype(BF16)
            xhat_out[rows, :] = xhat.astype(BF16)
            scale_out[rows, :] = scale
        wait_all(first)
        for rows in chunks(length, 256):
            for c in chunks(units, 512):
                pre = nn(low[rows, :], w_i[:, c]) + bias[:, c]
                act, slope = gelu_parts(pre)
                act_out[rows, c] = act.astype(BF16)
                slope_out[rows, c] = slope.astype(BF16)
        wait_all(second)
        for rows in chunks(length, 256):
            part_out[rows, :] = nt(act_out[rows, :], w_f[...]).astype(BF16)

    return pl.pallas_call(
        body,
        out_shape=[
            sds((length, width), BF16), sds((length, width), F32), sds((length, width), BF16),
            sds((length, 1), F32), sds((length, units), BF16), sds((length, units), BF16),
        ],
        in_specs=[SM] + [VM] * 5 + [ANY] * 13 + [VM],
        out_specs=[VM] * 6,
        scratch_shapes=[
            pltpu.VMEM((width, units), BF16), pltpu.VMEM((width, units), BF16),
            pltpu.VMEM((length, width), BF16), pltpu.SemaphoreType.DMA((copies_of(pieces[5]),)),
        ],
        compiler_params=params(),
        cost_estimate=takes(9),
        name="ffn_forward",
    )(meta, x, *parts, gains, shifts, *pieces, bias_in)


def last_norm(mid, parts, gains, shifts, tok_row, cls_pos):
    length, width = mid.shape
    n_cls = cls_pos.shape[0]

    def body(cls, mid, own, other, gain, shift, tok, y_out, xhat_out, scale_out, cls_out):
        for rows in chunks(length):
            z = mid[rows, :] + (own[rows, :].astype(F32) + other[rows, :].astype(F32)) + shift[2:3, :]
            xhat, scale = norm_rows(z)
            y_out[rows, :] = (xhat * gain[1:2, :] + shift[3:4, :]).astype(BF16)
            xhat_out[rows, :] = xhat.astype(BF16)
            scale_out[rows, :] = scale
        which = lax.broadcasted_iota(jnp.int32, (16, length), 0)
        hot = jnp.zeros((16, length), F32)
        for p in range(n_cls):
            hot = jnp.where(jnp.logical_and(which == p, tok[...] == cls[p]), 1.0, hot)
        cls_out[...] = nn(hot.astype(BF16), y_out[...])[:n_cls].astype(BF16)

    return pl.pallas_call(
        body,
        out_shape=[
            sds((length, width), BF16), sds((length, width), BF16), sds((length, 1), F32),
            sds((n_cls, width), BF16),
        ],
        in_specs=[SM] + [VM] * 6,
        out_specs=[VM] * 4,
        compiler_params=params(),
        cost_estimate=takes(2),
        name="last_norm",
    )(cls_pos, mid, *parts, gains, shifts, tok_row)


def ffn_backward(level, meta, sources, xhat, scale, gains, slope, pieces, half):
    units = 2 * half
    length, width = xhat.shape
    n_cls = sources[3].shape[0] if level else 0

    def body(meta, *refs):
        refs = list(refs)
        if level:
            cls, grad, d_cls, tok = (refs.pop(0) for _ in range(4))
        else:
            d_above, own, other = (refs.pop(0) for _ in range(3))
        xhat, scale, gain, slope = (refs.pop(0) for _ in range(4))
        pieces = [refs.pop(0) for _ in range(13)]
        part_out, second_out, low_out, pre_out, vec_out, inb_out, w_i, w_f, sems = refs
        first, second = load_b(meta, pieces, w_i, w_f, sems)
        sums = [jnp.zeros((1, width), F32) for _ in range(3)]
        for rows in chunks(length):
            if level:
                d_out = grad[rows, :].astype(F32)
                for p in range(n_cls):
                    d_out = d_out + jnp.where(tok[rows, :] == cls[p], 1.0, 0.0) * d_cls[p : p + 1, :]
            else:
                d_out = d_above[rows, :] + (own[rows, :].astype(F32) + other[rows, :].astype(F32))
                d_out = d_out.astype(BF16).astype(F32)
            hat = xhat[rows, :].astype(F32)
            d_second = norm_back_rows(d_out, gain[1:2, :], hat, scale[rows, :])
            second_out[rows, :] = d_second
            low_out[rows, :] = d_second.astype(BF16)
            for n, item in enumerate((d_out * hat, d_out, d_second)):
                sums[n] = sums[n] + jnp.sum(item, 0, keepdims=True)
        for n in range(3):
            vec_out[n : n + 1, :] = sums[n]
        wait_all(second)
        for n, rows in enumerate(chunks(length, 256)):
            for c in chunks(units, units // 4):
                d_act = nn(low_out[rows, :], w_f[:, c])
                d_pre = (slope[rows, c].astype(F32) * d_act).astype(BF16)
                pre_out[rows, c] = d_pre
                j, at = divmod(c.start, units // 2)
                at = slice(at, at + c.stop - c.start)
                total = jnp.sum(d_pre.astype(F32), 0, keepdims=True)
                inb_out[j : j + 1, at] = total if n == 0 else inb_out[j : j + 1, at] + total
        wait_all(first)
        for rows in chunks(length, 256):
            part_out[rows, :] = nt(pre_out[rows, :], w_i[...]).astype(BF16)

    if level:
        token_grad, d_cls, tok_col, cls_pos = sources
        args, specs = [meta, cls_pos, token_grad, d_cls, tok_col], [SM, SM, VM, VM, VM]
    else:
        args, specs = [meta, *sources], [SM, VM, VM, VM]
    args += [xhat, scale, gains, slope, *pieces]
    specs += [VM] * 4 + [ANY] * 13
    return pl.pallas_call(
        body,
        out_shape=[
            sds((length, width), BF16), sds((length, width), F32), sds((length, width), BF16),
            sds((length, units), BF16), sds((3, width), F32), sds((2, units // 2), F32),
        ],
        in_specs=specs,
        out_specs=[VM] * 6,
        scratch_shapes=[
            pltpu.VMEM((width, units), BF16), pltpu.VMEM((width, units), BF16),
            pltpu.SemaphoreType.DMA((copies_of(pieces[5]),)),
        ],
        compiler_params=params(),
        cost_estimate=takes(9),
        name="ffn_backward",
    )(*args)


def grads_of(nz, rz, width):
    half = nz // 2
    return [sds((nz, rz, width), BF16), sds((half, rz, width), BF16), sds((half, rz, width), BF16)]


def put_grad(outs, j, k, nz, column, value, first=0):
    half, (height, width) = nz // 2, value.shape
    if k < half:
        out, at = outs[0], k + (half if j == 0 else 0)
    else:
        out, at = outs[2 if j == 0 else 1], k - half
    out[at, first : first + height, column : column + width] = value.astype(BF16)


def ffn_grads(meta, mid, d_pre, d_ffn, act, nz):
    length, width = mid.shape
    units = d_pre.shape[1]
    one = units // 2
    rz = width // nz

    def body(meta, mid, d_pre, d_ffn, act, *refs):
        outs, (mid_t, ffn_t) = refs[:3], refs[3:]
        mid_t[...] = mid[...].T.astype(BF16)
        ffn_t[...] = d_ffn[...].astype(F32).T.astype(BF16)
        for j in range(2):
            c = slice(j * one, (j + 1) * one)
            for k in range(nz):
                rows = zrows(meta, k, rz)
                put_grad(outs, j, k, nz, 0, nn(mid_t[rows, :], d_pre[:, c]))
                put_grad(outs, j, k, nz, one, nn(ffn_t[rows, :], act[:, c]))

    return pl.pallas_call(
        body,
        out_shape=grads_of(nz, rz, units),
        in_specs=[SM] + [VM] * 4,
        out_specs=[VM] * 3,
        scratch_shapes=[pltpu.VMEM((width, length), BF16)] * 2,
        compiler_params=params(),
        cost_estimate=takes(7),
        name="ffn_grads",
    )(meta, mid, d_pre, d_ffn, act)


def attn_backward(meta, d_second, parts, xhat, scale, gains, qkv, probs, pieces, cols):
    four = 4 * cols
    length, width = d_second.shape
    three = 3 * cols
    heads = 2 * cols // HD

    def body(meta, d_second, own, other, xhat, scale, gain, qkv, probs, p0, p1, p2, p3, p4, p5, p6, p7, p8, p9, p10, p11, p12,
             part_out, first_out, low_out, dqkv_out, vec_out, sum_out,
             w_a, d_ctx, acc_v, acc_k, sems):
        waits = load_a(meta, (p0, p1, p2, p3, p4, p5, p6, p7, p8, p9, p10, p11, p12), w_a, sems)
        sums = [jnp.zeros((1, width), F32) for _ in range(3)]
        for rows in chunks(length):
            d_mid = d_second[rows, :] + (own[rows, :].astype(F32) + other[rows, :].astype(F32))
            hat = xhat[rows, :].astype(F32)
            d_first = norm_back_rows(d_mid, gain[0:1, :], hat, scale[rows, :])
            first_out[rows, :] = d_first
            low_out[rows, :] = d_first.astype(BF16)
            for n, item in enumerate((d_mid * hat, d_mid, d_first)):
                sums[n] = sums[n] + jnp.sum(item, 0, keepdims=True)
        for n in range(3):
            vec_out[n : n + 1, :] = sums[n]
        wait_all(waits)
        for j in range(2):
            for rows in chunks(length, 256):
                d_ctx[rows, j * cols : (j + 1) * cols] = nn(low_out[rows, :], w_a[j, :, three:]).astype(BF16)
        k_t = jnp.concatenate(
            [qkv[:, j * three + cols : j * three + 2 * cols].astype(F32) for j in range(2)], 1
        ).T.astype(BF16)
        for h in range(heads):
            j, i = divmod(h, cols // HD)
            at = j * three + i * HD
            q_cols, k_cols, v_cols = (slice(at + n * cols, at + n * cols + HD) for n in range(3))
            for n, queries in enumerate(chunks(length, 256)):
                d_o = d_ctx[queries, h * HD : (h + 1) * HD]
                d_p = nt(qkv[:, v_cols], d_o)
                p = probs[h, :, queries]
                wide = p.astype(F32)
                d_s = (wide * (d_p - jnp.sum(wide * d_p, 0, keepdims=True))).astype(BF16)
                d_v = nn(p, d_o)
                d_k = nn(d_s, qkv[queries, q_cols])
                acc_v[...] = d_v if n == 0 else acc_v[...] + d_v
                acc_k[...] = d_k if n == 0 else acc_k[...] + d_k
                d_q = nn(k_t[h * HD : (h + 1) * HD], d_s)
                dqkv_out[queries, q_cols] = (d_q.T * 0.125).astype(BF16)
            dqkv_out[:, v_cols] = acc_v[...].astype(BF16)
            dqkv_out[:, k_cols] = (acc_k[...] * 0.125).astype(BF16)
        for j in range(2):
            sum_out[j : j + 1, :] = jnp.sum(
                dqkv_out[:, j * three : (j + 1) * three].astype(F32), 0, keepdims=True
            )
        for rows in chunks(length, 256):
            part_out[rows, :] = (
                nt(dqkv_out[rows, :three], w_a[0, :, :three]) + nt(dqkv_out[rows, three:], w_a[1, :, :three])
            ).astype(BF16)

    return pl.pallas_call(
        body,
        out_shape=[
            sds((length, width), BF16), sds((length, width), F32), sds((length, width), BF16),
            sds((length, 2 * three), BF16), sds((3, width), F32), sds((2, three), F32),
        ],
        in_specs=[SM] + [VM] * 8 + [ANY] * 13,
        out_specs=[VM] * 6,
        scratch_shapes=[
            pltpu.VMEM((2, width, four), BF16), pltpu.VMEM((length, 2 * cols), BF16),
            pltpu.VMEM((length, HD), F32), pltpu.VMEM((length, HD), F32),
            pltpu.SemaphoreType.DMA((copies_of(pieces[5]),)),
        ],
        compiler_params=params(),
        cost_estimate=takes(15),
        name="attn_backward",
    )(meta, d_second, *parts, xhat, scale, gains, qkv, probs, *pieces)


def attn_grads(meta, places, x, d_attn, d_qkv, ctx, vectors, nz, extra):
    length, width = x.shape
    three = d_qkv.shape[1] // 2
    cols = ctx.shape[1] // 2
    rz = width // nz

    def body(meta, places, x, d_attn, d_qkv, ctx, vec1, vec2, sum_qkv, sum_inb, *refs):
        outs, (x_t, a_t, norm_rows_, qv_rows, inb_rows) = refs[:3], refs[3:]
        x_t[...] = x[...].astype(F32).T.astype(BF16)
        a_t[...] = d_attn[...].astype(F32).T.astype(BF16)
        for j in range(2):
            for k in range(nz):
                rows = zrows(meta, k, rz)
                grad = nn(x_t[rows, :], d_qkv[:, j * three : (j + 1) * three])
                put_grad(outs, j, k, nz, 0, grad)
                put_grad(outs, j, k, nz, three, nn(a_t[rows, :], ctx[:, j * cols : (j + 1) * cols]))
        if not extra:
            return
        piece, part = width // (4 * nz), cols // nz
        units = sum_inb.shape[1] // nz
        norm_rows_[...] = jnp.zeros_like(norm_rows_)
        norm_rows_[0:3, :] = vec1[...]
        norm_rows_[3:6, :] = vec2[...]
        for j in range(2):
            qv_rows[...] = jnp.zeros_like(qv_rows)
            qv_rows[0:1, :cols] = sum_qkv[j : j + 1, :cols]
            qv_rows[1:2, :cols] = sum_qkv[j : j + 1, 2 * cols : three]
            inb_rows[...] = jnp.zeros_like(inb_rows)
            inb_rows[0:1, :] = sum_inb[j : j + 1, :]
            for k in range(nz):
                d = places[2 + k]
                from_norm = pltpu.roll(norm_rows_[...], width - (d * 4 + places[j]) * piece, 1)
                from_qv = pltpu.roll(qv_rows[...], width - d * part, 1)
                from_inb = pltpu.roll(inb_rows[...], width - d * units, 1)
                lane = lax.broadcasted_iota(jnp.int32, (8, 2 * cols), 1)
                upper = jnp.where(lane < piece, from_norm[:, : 2 * cols], 0.0)
                lower = jnp.where(lane < part, from_qv[:, : 2 * cols], 0.0)
                shifted = pltpu.roll(from_inb, 128, 1)[:, : 2 * cols]
                inside = jnp.logical_and(lane >= 128, lane < 128 + units)
                lower = jnp.where(inside, shifted, lower)
                put_grad(outs, j, k, nz, 0, jnp.concatenate([upper, lower], 0), rz)
                put_grad(outs, j, k, nz, 2 * cols, jnp.zeros((extra, 2 * cols), F32), rz)

    return pl.pallas_call(
        body,
        out_shape=grads_of(nz, rz + extra, three + cols),
        in_specs=[SM, SM] + [VM] * 8,
        out_specs=[VM] * 3,
        scratch_shapes=[pltpu.VMEM((width, length), BF16)] * 2 + [pltpu.VMEM((8, width), F32)] * 3,
        compiler_params=params(),
        cost_estimate=takes(4),
        name="attn_grads",
    )(meta, places, x, d_attn, d_qkv, ctx, *vectors)


def loss_kernel(own, perm, slots, queries, positive_col, n_own):
    n_q, width = queries.shape
    n_p = slots.shape[0]

    def body(own, perm, slots, queries, pos, loss_out, d_out):
        passages = nn(perm[...], slots[...]).astype(BF16)
        logits = nt(queries[...], passages)
        top = jnp.max(logits, -1, keepdims=True)
        log_total = top + jnp.log(jnp.sum(jnp.exp(logits - top), -1, keepdims=True))
        index = lax.broadcasted_iota(jnp.int32, (n_q, n_p), 1)
        hits = pos[...] == index
        chosen = jnp.sum(jnp.where(hits, logits, 0.0), -1, keepdims=True)
        loss_out[...] = jnp.sum(log_total - chosen, 0, keepdims=True) / n_q
        d_logits = (16.0 * (jnp.exp(logits - log_total) - jnp.where(hits, 1.0, 0.0))).astype(BF16)
        pick = jnp.where(
            lax.broadcasted_iota(jnp.int32, (n_p, 128), 0)
            == lax.broadcasted_iota(jnp.int32, (n_p, 128), 1) + own[0],
            1.0, 0.0,
        ).astype(BF16)
        cols = nn(d_logits, pick)
        d_out[...] = nn(cols.T.astype(BF16), queries[...])[:n_own]

    return pl.pallas_call(
        body,
        out_shape=[sds((1, 1), F32), sds((n_own, width), F32)],
        in_specs=[SM] + [VM] * 4,
        out_specs=[VM] * 2,
        compiler_params=params(),
        cost_estimate=takes(1),
        name="contrast",
    )(own, perm, slots, queries, positive_col)


def on_device(
    inputs, cls_pos, w_qkv, qv_bias, w_out, w_in, in_bias, w_ffn_out,
    layer_gains, shifts, queries, positive, token_grad,
):
    core = lax.axis_index("section")
    dp = lax.axis_index("dp")
    me = lax.axis_index("tensor")
    n_dp = lax.axis_size("dp")
    n_t = lax.axis_size("tensor")
    first_core = core == 0
    rows_dev, share, width = inputs.shape
    cols = w_qkv.shape[3]
    units = w_in.shape[2]
    length = n_t * share
    n_chips = n_dp * n_t
    piece = width // n_chips
    order = dp_order()
    direct = direct_dp()
    nz, extra = (4, 16) if direct else (2, 0)
    t_ids = jnp.arange(n_t, dtype=jnp.int32)

    vec = jnp.concatenate(
        [layer_gains.reshape(-1), shifts.reshape(-1), qv_bias.reshape(-1), in_bias.reshape(-1)]
    )
    n_gain, n_shift, n_qv, n_inb = layer_gains.size, shifts.size, qv_bias.size, in_bias.size
    n_vec = vec.shape[0]
    flat = jnp.concatenate(
        [vec, queries.reshape(-1), (positive // 16).astype(BF16), (positive % 16).astype(BF16)]
    )
    flat = jnp.pad(flat, (0, -flat.shape[0] % 2048)).reshape(-1, 128)

    def spread_rows(block):
        blocks = [lax.dynamic_index_in_dim(block, me ^ k, 0, keepdims=False) for k in range(n_t)]
        return jnp.concatenate(exchange_rows(blocks), 0)

    pack = jnp.concatenate(
        [w_qkv[0, :, 0], w_qkv[0, :, 1], w_qkv[0, :, 2], w_out[0].T, w_in[0], w_ffn_out[0].T], 1
    )
    message = spread_dp(flat)
    if direct:
        own = pack
        z_a = rest_dp(after(pack[:, :width], message))
    else:
        pack = lax.all_gather(pack, "dp", axis=0, tiled=True)
        own, other_rows = pack[: width // 2], pack[width // 2 :][None]
    message = spread_tensor(message)
    near0, far0 = gather_own(after(own, message))
    both0 = gather_own_both(near0, far0)
    owns = [own, near0, far0, *both0]

    def halves_of(blocks, first, size, *earlier):
        half = size // 2
        if not direct:
            blocks = other_rows[:, :, first : first + size]
            return blocks[:, :, :half], blocks[:, :, half:]
        blocks = after(blocks, *earlier)
        return jnp.stack([b[:, :half] for b in blocks]), jnp.stack([b[:, half:] for b in blocks])

    rest_a = jnp.stack(after(z_a, near0, far0)) if direct else other_rows[:, :, :width]
    near_a, far_a = gather_own(rest_a)
    if direct:
        z_b = rest_dp(after(pack[:, width:], rest_a))
    rows_in = spread_rows(after(jnp.where(first_core, inputs, token_grad), near_a))
    near_a, far_a = after((near_a, far_a), both0, z_b[:2] if direct else near_a)
    both_a = gather_both(near_a[:, :, : width // 2], far_a[:, :, width // 2 :])
    rows_got = swap_cores(rows_in)
    x_low = jnp.where(first_core, rows_in, rows_got)
    tokens = jnp.where(first_core, rows_got, rows_in)
    rest_b = halves_of(z_b if direct else None, width, 2 * units, both_a)
    near_b = gather_near(rest_b)
    pieces_a = [*owns, rest_a, rest_a, near_a, near_a, far_a, far_a, *both_a]

    zrow = order * (width // n_dp) if direct else jnp.arange(2, dtype=jnp.int32) * (width // 2)
    metas = [
        jnp.concatenate([(core == level)[None].astype(jnp.int32), zrow.astype(jnp.int32)])
        for level in range(2)
    ]
    slots = [me ^ (2 * (core != level) + jnp.arange(2, dtype=jnp.int32)) for level in range(2)]
    places = [jnp.concatenate([s, order[:nz]]).astype(jnp.int32) for s in slots]
    hots = [(s[:, None] == t_ids[None, :]).astype(F32) for s in slots]

    positions = jnp.concatenate(
        [(me ^ k) * share + jnp.arange(share, dtype=jnp.int32) for k in range(n_t)]
    )
    cls_row = lax.dynamic_index_in_dim(cls_pos, me, 0, keepdims=False)
    segments = jnp.sum((positions[:, None] >= cls_row[None, :]).astype(jnp.int32), -1)
    seg_col, seg_row = segments[:, None], segments[None, :]
    tok_col, tok_row = positions[:, None], positions[None, :]

    slot_ids = (order[None, :] * n_t + (me ^ t_ids)[:, None]).reshape(-1)
    to_natural = (jnp.arange(n_chips, dtype=jnp.int32)[:, None] == slot_ids[None, :]).astype(BF16)
    table = nn(to_natural, message.reshape(n_chips, -1))
    own_table = table[:, :n_vec].astype(BF16)
    other_table = swap_cores(own_table)
    tables = jnp.where(
        first_core, jnp.stack([own_table, other_table]), jnp.stack([other_table, own_table])
    ).astype(F32)
    at = 0
    gains = tables[:, :, at : at + n_gain].reshape(2, n_chips, 2, piece).transpose(0, 2, 1, 3).reshape(2, 2, width)
    at += n_gain
    shift = tables[:, :, at : at + n_shift].reshape(2, n_chips, 4, piece).transpose(0, 2, 1, 3).reshape(2, 4, width)
    at += n_shift
    qv = tables[:, :, at : at + n_qv].reshape(2, n_dp, n_t, 2, cols // n_dp)
    qv = qv.transpose(0, 3, 2, 1, 4).reshape(2, 2, n_t, cols)
    at += n_qv
    inb = tables[:, :, at : at + n_inb].reshape(2, n_dp, n_t, n_inb).transpose(0, 2, 1, 3).reshape(2, n_t, units)
    vectors = []
    for level in range(2):
        bias = jnp.sum(hots[level][None, :, :, None] * qv[level][:, None], 2)
        bias = jnp.stack([bias[0], jnp.zeros_like(bias[0]), bias[1]], 1).reshape(1, -1)
        bias_in = jnp.sum(hots[level][:, :, None] * inb[level][None], 1).reshape(1, -1)
        vectors.append((gains[level], shift[level], bias, bias_in))
    at = n_vec
    q_dev = queries.shape[0]
    all_q = table[:, at : at + q_dev * width].reshape(-1, width).astype(BF16)
    at += q_dev * width
    all_pos = table[:, at : at + q_dev] * 16.0 + table[:, at + q_dev : at + 2 * q_dev]
    all_pos = all_pos.astype(jnp.int32).reshape(-1, 1)
    n_cls = cls_row.shape[0]
    perm = jnp.repeat(jnp.repeat(to_natural, n_cls, 0), n_cls, 1)
    perm = perm * jnp.tile(jnp.eye(n_cls, dtype=BF16), (n_chips, n_chips))

    vectors, all_q, all_pos, perm, x_low = lax.optimization_barrier(
        (vectors, all_q, all_pos, perm, x_low)
    )
    saved = []
    source, parts, norms = x_low, None, None
    for level in range(2):
        gain, shift, bias, bias_in = vectors[level]
        outs = attn_forward(
            level, metas[level], source, parts, norms, pieces_a, bias, seg_col, seg_row, cols
        )
        part, qkv, probs, ctx = outs[:4]
        if level == 0:
            pieces_b = [*owns, *rest_b, *near_b, *gather_both(near_b[0], after(near_b[3], part))]
        if level:
            x, xhat2, scale2 = outs[4:]
            saved[0]["second"] = (xhat2, scale2)
        else:
            x = x_low
        part, mid, xhat1, scale1, act, slope = ffn_forward(
            metas[level], x, (part, swap_cores(part)), gain, shift, pieces_b, bias_in, units
        )
        saved.append(
            dict(x=x, qkv=qkv, probs=probs, ctx=ctx, mid=mid, xhat1=xhat1, scale1=scale1, act=act, slope=slope)
        )
        source, parts, norms = mid, (part, swap_cores(part)), (gain, shift)
    y, xhat2, scale2, cls_own = last_norm(source, parts, *norms, tok_row, cls_row)
    saved[1]["second"] = (xhat2, scale2)

    cls_slots = spread_tensor(spread_dp(cls_own)).reshape(n_chips * n_cls, width)
    first_own = ((dp * n_t + me) * n_cls).astype(jnp.int32)[None]
    mean_loss, d_cls = loss_kernel(first_own, perm, cls_slots, all_q, all_pos, n_cls)

    vector_rows = [None, None]
    sources = (tokens, d_cls, tok_col, cls_row)
    sums_a, sums_b = [None, None], [None, None]
    for level in (1, 0):
        gain = vectors[level][0]
        kept = saved[level]
        meta = metas[level]
        xhat2, scale2 = kept["second"]
        if level == 0:
            sources = (after(sources[0], sums_b[1].first(grads_a[1])), *sources[1:])
        part, d_second, d_ffn, d_pre, vec2, sum_inb = ffn_backward(
            level, meta, sources, xhat2, scale2, gain, kept["slope"], pieces_b, units
        )
        other = swap_cores(part)
        if level == 0:
            d_ffn = after(d_ffn, sums_a[1].first(part))
        grads_b = ffn_grads(meta, kept["mid"], d_pre, d_ffn, kept["act"], nz)
        sums_b[level] = Reduction(grads_b, level)
        d_second = after(d_second, grads_b[1])
        if level == 0:
            d_second = after(d_second, sums_b[1].second(grads_b[1]))
        part, d_first, d_attn, d_qkv, vec1, sum_qkv = attn_backward(
            meta, d_second, (part, other), kept["xhat1"], kept["scale1"], gain,
            kept["qkv"], kept["probs"], pieces_a, cols,
        )
        other = swap_cores(part)
        if level == 0:
            d_attn = after(d_attn, sums_b[0].first(sums_a[1].second(part)))
        grads_a = attn_grads(
            meta, places[level], kept["x"], d_attn, d_qkv, kept["ctx"], (vec1, vec2, sum_qkv, sum_inb), nz, extra
        )
        sums_a[level] = Reduction(grads_a, level)
        vector_rows[level] = (vec1, vec2, sum_qkv, sum_inb)
        sources = (d_first, part, other)
    sums_b[1].third(grads_a[1])
    sums_b[0].second_direct(sums_b[1].pieces)
    sums_a[1].third(sums_b[0].sums)
    sums_a[0].first(sums_a[1].pieces, sums_b[0].hops[1:2] if direct else sums_b[0].sums)
    sums_a[0].second_direct(sums_a[0].added)
    last_a1, last_b1 = last_dp([sums_a[1], sums_b[1]], sums_a[0].sums)
    total_b0 = sums_b[0].third_direct()
    d_hidden = d_first + (part.astype(F32) + other.astype(F32))
    outgoing = jnp.where(first_core, d_hidden, y.astype(F32))
    low = after(outgoing.astype(BF16), sums_a[0].added).reshape(n_t, share, width)
    incoming = [outgoing[:share]] + [b.astype(F32) for b in exchange_rows([low[k] for k in range(n_t)])[1:]]
    boundary = jnp.zeros((n_t, share, width), F32)
    for k in range(n_t):
        boundary = lax.dynamic_update_index_in_dim(boundary, incoming[k], me ^ k, 0)
    tot_b, tot_a = (
        jnp.where(first_core, low, sum(p.astype(F32) for p in high))
        for low, high in ((total_b0, last_b1), (sums_a[0].third_direct(), last_a1))
    )
    if direct:
        end = width // n_dp
        own = tot_a[end : end + 6, :piece]
        qv = tot_a[end + 8 : end + 10, : qv_bias.shape[3]]
        grad_inb = tot_a[end + 8 : end + 9, 128 : 128 + n_inb]
        tot_a = tot_a[:end]
    else:
        tables = []
        for level in range(2):
            vec1, vec2, sum_qkv, sum_inb = vector_rows[level]
            by_t = lax.dot_general(
                hots[level], jnp.concatenate([sum_qkv, sum_inb], 1), (((0,), (0,)), ((), ())),
                precision=lax.Precision.HIGHEST,
            )
            whole = 0.5 * jnp.concatenate([vec1, vec2])
            whole = jnp.pad(whole, ((0, 0), (0, by_t.shape[1] - width)))
            tables.append(jnp.concatenate([whole, by_t]))
        tables = lax.psum(jnp.stack(tables), ("section", "dp", "tensor"))
        flat = jnp.where(first_core, tables[0], tables[1])
        own = lax.dynamic_slice_in_dim(flat[:6, :width], (dp * n_t + me) * piece, piece, 1)
        by_t = lax.dynamic_slice_in_dim(flat, 6 + me, 1, 0)
        qv = jnp.concatenate([by_t[:, :cols], by_t[:, 2 * cols : 3 * cols]])
        qv = lax.dynamic_slice_in_dim(qv, dp * qv_bias.shape[3], qv_bias.shape[3], 1)
        grad_inb = lax.dynamic_slice_in_dim(by_t[:, 3 * cols :], dp * n_inb, n_inb, 1)
    grad_gains = jnp.concatenate([own[0:1], own[3:4]]).reshape(layer_gains.shape)
    grad_shifts = jnp.concatenate([own[2:3], own[1:2], own[5:6], own[4:5]]).reshape(shifts.shape)
    grad_qv, grad_inb = qv.reshape(qv_bias.shape), grad_inb.reshape(in_bias.shape)

    grad_qkv = jnp.stack([tot_a[:, n * cols : (n + 1) * cols] for n in range(3)], 1)[None]
    grad_out = tot_a[:, 3 * cols :].T[None]
    grad_in = tot_b[:, :units][None]
    grad_ffn = tot_b[:, units:].T[None]
    return (
        grad_qkv, grad_qv, grad_out, grad_in, grad_inb, grad_ffn,
        grad_gains, grad_shifts, boundary[None], mean_loss.reshape(()),
    )


def solution(mesh):
    return jax.shard_map(
        on_device,
        mesh=mesh,
        in_specs=(
            P("dp", "tensor", None),
            P("dp", None),
            P("section", "dp", None, "tensor"),
            P("section", None, "tensor", "dp"),
            P("section", "tensor", "dp"),
            P("section", "dp", "tensor"),
            P("section", "tensor", "dp"),
            P("section", "tensor", "dp"),
            P("section", None, ("dp", "tensor")),
            P("section", None, ("dp", "tensor")),
            P(("dp", "tensor"), None),
            P(("dp", "tensor")),
            P("dp", "tensor", None),
        ),
        out_specs=(
            P("section", "dp", None, "tensor"),
            P("section", None, "tensor", "dp"),
            P("section", "tensor", "dp"),
            P("section", "dp", "tensor"),
            P("section", "tensor", "dp"),
            P("section", "tensor", "dp"),
            P("section", None, ("dp", "tensor")),
            P("section", None, ("dp", "tensor")),
            P("section", "dp", "tensor", None),
            P(),
        ),
        check_vma=False,
    )
```

profile of v0, /device:TPU:0, one launch (start us, length us, event | category | flops | bytes accessed | tf_op | source)
XLA Modules:
  0.0 473.2 jit_solution(17734513259504538111)
XLA Ops:
  5.2 3.1 collective-permute-start
  29.4 3.5 collective-permute-start.8
  34.4 9.1 %collective-permute-done.7 = bf16[192,768]{1,0:T(8,128)(2,1)S(1)} collective-permute-done((bf16[192,768]{1,0:T(8,128)(2,1)}, bf16[192,768]{1,0:T(8,128)(2,1)S(1)}, u32[]{:S(2)}, u32[]{:S(2)}) %collective-permute-start.7) | collective-permute-done | bytes 294944 | tf_op jit(solution)/shard_map/ppermute | solution.py:36
  43.5 10.2 %collective-permute-done.8 = bf16[192,768]{1,0:T(8,128)(2,1)S(1)} collective-permute-done((bf16[192,768]{1,0:T(8,128)(2,1)}, bf16[192,768]{1,0:T(8,128)(2,1)S(1)}, u32[]{:S(2)}, u32[]{:S(2)}) %collective-permute-start.8) | collective-permute-done | bytes 294944 | tf_op jit(solution)/shard_map/ppermute | solution.py:36
  58.0 6.2 %collective-permute-start.19 = (bf16[192,1536]{1,0:T(8,128)(2,1)}, bf16[192,1536]{1,0:T(8,128)(2,1)S(1)}, u32[]{:S(2)}, u32[]{:S(2)}) collective-permute-start(bf16[192,1536]{1,0:T(8,128)(2,1)} %pad_maximum_fusion.4), channel_id=1, source_target_pairs={{0,4},{4,0},{8,12},{12,8},{1,5},{5,1},{9,13},{13,9},{2,6},{6,2},{1... | collective-permute-start | bytes 1769480 | tf_op jit(solution)/shard_map/ppermute | solution.py:36
  69.1 7.0 %collective-permute-done.12.refs_8_.refs_9_.refs_12_.refs_13_.p7.p8 = bf16[3,192,768]{2,1,0:T(8,128)(2,1)} collective-permute-done((bf16[3,192,768]{2,1,0:T(8,128)(2,1)}, bf16[3,192,768]{2,1,0:T(8,128)(2,1)}, u32[]{:S(2)}, u32[]{:S(2)}) %collective-permute-start.12) | collective-permute-done | bytes 884768 | tf_op jit(solution)/shard_map/ppermute | solution.py:36
  80.5 8.8 %collective-permute-done.16.refs_4_.p3.refs_8_.refs_11_.refs_10_ = bf16[192,1152]{1,0:T(8,128)(2,1)S(1)} collective-permute-done((bf16[192,1152]{1,0:T(8,128)(2,1)}, bf16[192,1152]{1,0:T(8,128)(2,1)S(1)}, u32[]{:S(2)}, u32[]{:S(2)}) %collective-permute-start.16) | collective-permute-done | bytes 442400 | tf_op jit(solution)/shard_map/ppermute | solution.py:86
  98.5 4.6 collective-permute-done.13
  105.2 9.4 %collective-permute-start.14 = (bf16[2,128,768]{2,1,0:T(8,128)(2,1)S(1)}, bf16[2,128,768]{2,1,0:T(8,128)(2,1)S(1)}, u32[]{:S(2)}, u32[]{:S(2)}) collective-permute-start(bf16[2,128,768]{2,1,0:T(8,128)(2,1)S(1)} %pad_maximum_fusion.6), channel_id=1, source_target_pairs={{0,2},{1,3},{2,0},{3,1},{4,6},{5,7},{6,4},{7,5},{8,10},{9,11},{10,... | collective-permute-start | bytes 1179656 | tf_op jit(solution)/shard_map/ppermute | solution.py:36
  120.1 3.7 collective-permute-done.14
  130.0 7.8 %collective-permute-done.25.p7.refs_15_.refs_14_ = bf16[3,192,768]{2,1,0:T(8,128)(2,1)} collective-permute-done((bf16[3,192,768]{2,1,0:T(8,128)(2,1)}, bf16[3,192,768]{2,1,0:T(8,128)(2,1)}, u32[]{:S(2)}, u32[]{:S(2)}) %collective-permute-start.25) | collective-permute-done | bytes 884768 | tf_op jit(solution)/shard_map/ppermute | solution.py:36
  139.4 12.1 %attn_forward.2 = (bf16[512,768]{1,0:T(8,128)(2,1)S(1)}, bf16[512,1152]{1,0:T(8,128)(2,1)}, bf16[6,512,512]{2,1,0:T(8,128)(2,1)}, bf16[512,384]{1,0:T(8,128)(2,1)S(1)}) custom-call(s32[5]{0:T(128)S(1)} %get-tuple-element.426.meta, bf16[512,768]{1,0:T(8,128)(2,1)S(1)} %get-tuple-element.166.refs_0_.x, ...), custom_call_target="tpu_custom_call" | custom-call | flops 14300000256 | tf_op jit(solution)/shard_map/attn_forward/pallas_call | solution.py:382
  154.0 6.7 %collective-permute-start.23 = (bf16[512,768]{1,0:T(8,128)(2,1)S(1)}, bf16[512,768]{1,0:T(8,128)(2,1)S(1)}, u32[]{:S(2)}, u32[]{:S(2)}) collective-permute-start(bf16[512,768]{1,0:T(8,128)(2,1)S(1)} %get-tuple-element.172.own), channel_id=1, source_target_pairs={{0,16},{16,0},{1,17},{17,1},{2,18},{18,2},{3,19},{19,3},{4,20},{20... | collective-permute-start | bytes 2359304 | tf_op jit(solution)/shard_map/ppermute | solution.py:32
  160.7 7.1 %collective-permute-done.27.p9.refs_17_.refs_16_ = bf16[3,192,768]{2,1,0:T(8,128)(2,1)S(1)} collective-permute-done((bf16[3,192,768]{2,1,0:T(8,128)(2,1)}, bf16[3,192,768]{2,1,0:T(8,128)(2,1)S(1)}, u32[]{:S(2)}, u32[]{:S(2)}) %collective-permute-start.27) | collective-permute-done | bytes 884768 | tf_op jit(solution)/shard_map/ppermute | solution.py:86
  167.8 19.0 %collective-permute-done.29.p11.refs_19_.refs_18_ = bf16[3,192,768]{2,1,0:T(8,128)(2,1)S(1)} collective-permute-done((bf16[3,192,768]{2,1,0:T(8,128)(2,1)}, bf16[3,192,768]{2,1,0:T(8,128)(2,1)S(1)}, u32[]{:S(2)}, u32[]{:S(2)}) %collective-permute-start.29) | collective-permute-done | bytes 884768 | tf_op jit(solution)/shard_map/ppermute | solution.py:86
  188.6 8.9 %ffn_forward.2 = (bf16[512,768]{1,0:T(8,128)(2,1)S(1)}, f32[512,768]{1,0:T(8,128)}, bf16[512,768]{1,0:T(8,128)(2,1)S(1)}, f32[512,1]{1,0:T(8,128)S(1)}, bf16[512...) custom-call(s32[5]{0:T(128)S(1)} %get-tuple-element.426.meta, bf16[512,768]{1,0:T(8,128)(2,1)S(1)} %get-tuple-element.166.refs_0_.x, ...), custom_call_target="tpu_custom_call" | custom-call | flops 9900000256 | tf_op jit(solution)/shard_map/ffn_forward/pallas_call | solution.py:420
  202.3 13.2 %attn_forward.3 = (bf16[512,768]{1,0:T(8,128)(2,1)S(1)}, bf16[512,1152]{1,0:T(8,128)(2,1)}, bf16[6,512,512]{2,1,0:T(8,128)(2,1)}, bf16[512,384]{1,0:T(8,128)(2,1...) custom-call(s32[5]{0:T(128)S(1)} %get-tuple-element.427.meta, ...), custom_call_target="tpu_custom_call" | custom-call | flops 14300000256 | tf_op jit(solution)/shard_map/attn_forward/pallas_call | solution.py:382
  218.9 8.9 %ffn_forward.3 = (bf16[512,768]{1,0:T(8,128)(2,1)S(1)}, f32[512,768]{1,0:T(8,128)}, bf16[512,768]{1,0:T(8,128)(2,1)S(1)}, f32[512,1]{1,0:T(8,128)S(1)}, bf16[512...) custom-call(s32[5]{0:T(128)S(1)} %get-tuple-element.427.meta, bf16[512,768]{1,0:T(8,128)(2,1)S(1)} %get-tuple-element.183.x, ...), custom_call_target="tpu_custom_call" | custom-call | flops 9900000256 | tf_op jit(solution)/shard_map/ffn_forward/pallas_call | solution.py:420
  236.1 5.8 %collective-permute-start.35 = (bf16[4,768]{1,0:T(4,128)(2,1)S(1)}, bf16[4,768]{1,0:T(4,128)(2,1)}, u32[]{:S(2)}, u32[]{:S(2)}) collective-permute-start(bf16[4,768]{1,0:T(4,128)(2,1)S(1)} %get-tuple-element.190), channel_id=1, source_target_pairs={{0,8},{4,12},{8,0},{12,4},{1,9},{5,13},{9,1},{13,5},{2,10},{6,14},... | collective-permute-start | bytes 18440 | tf_op jit(solution)/shard_map/ppermute | solution.py:36
  243.7 3.8 collective-permute-done.36
  262.1 8.6 %ffn_backward.2 = (bf16[512,768]{1,0:T(8,128)(2,1)S(1)}, f32[512,768]{1,0:T(8,128)}, bf16[512,768]{1,0:T(8,128)(2,1)S(1)}, bf16[512,1536]{1,0:T(8,128)(2,1)}, f3...) custom-call(s32[5]{0:T(128)S(1)} %copy-done.17, s32[4]{0:T(128)S(1)} %copy-done.15, ...), custom_call_target="tpu_custom_call" | custom-call | flops 9900000256 | tf_op jit(solution)/shard_map/ffn_backward/pallas_call | solution.py:522
  270.8 6.0 %ffn_grads.2 = (bf16[4,192,1536]{2,1,0:T(8,128)(2,1)}, bf16[2,192,1536]{2,1,0:T(8,128)(2,1)S(1)}, bf16[2,192,1536]{2,1,0:T(8,128)(2,1)S(1)}) custom-call(s32[5]{0:T(128)S(1)} %copy-done.17, f32[512,768]{1,0:T(8,128)S(1)} %copy-done.31, bf16[512,1536]{1,0:T(8,128)(2,1)} %get-tuple-element.198.d_pre, bf16[512,768]{1,0:T(8,128)(2,1)S(1)} %get-tuple-element.199.d_ffn, ...), custom_call_target="tpu_custom_call" | custom-call | flops 7699999744 | tf_op jit(solution)/shard_map/ffn_grads/pallas_call | solution.py:571
  276.8 4.3 collective-permute-start.41
  281.9 12.8 %attn_backward.2 = (bf16[512,768]{1,0:T(8,128)(2,1)S(1)}, f32[512,768]{1,0:T(8,128)}, bf16[512,768]{1,0:T(8,128)(2,1)S(1)}, bf16[512,1152]{1,0:T(8,128)(2,1)}, f...) custom-call(s32[5]{0:T(128)S(1)} %copy-done.17, f32[512,768]{1,0:T(8,128)} %get-tuple-element.202.d_second, ...), custom_call_target="tpu_custom_call" | custom-call | flops 16499999744 | tf_op jit(solution)/shard_map/attn_backward/pallas_call | solution.py:638
  296.2 2.9 attn_grads.2
  299.0 5.1 %collective-permute-start.44 = (bf16[4,208,768]{2,1,0:T(8,128)(2,1)S(1)}, bf16[4,208,768]{2,1,0:T(8,128)(2,1)}, u32[]{:S(2)}, u32[]{:S(2)}) collective-permute-start(bf16[4,208,768]{2,1,0:T(8,128)(2,1)S(1)} %get-tuple-element.257), channel_id=1, source_target_pairs={{0,18},{1,19},{2,16},{3,17},{4,22},{5,23},{6,20},{7,21},{8,26},{9,... | collective-permute-start | bytes 3833864 | tf_op jit(solution)/shard_map/ppermute | solution.py:48
  304.7 4.9 %collective-permute-done.42 = bf16[2,192,1536]{2,1,0:T(8,128)(2,1)S(1)} collective-permute-done((bf16[2,192,1536]{2,1,0:T(8,128)(2,1)S(1)}, bf16[2,192,1536]{2,1,0:T(8,128)(2,1)S(1)}, u32[]{:S(2)}, u32[]{:S(2)}) %collective-permute-start.42) | collective-permute-done | bytes 1179680 | tf_op jit(solution)/shard_map/ppermute | solution.py:36
  317.9 8.4 %ffn_backward.3 = (bf16[512,768]{1,0:T(8,128)(2,1)S(1)}, f32[512,768]{1,0:T(8,128)}, bf16[512,768]{1,0:T(8,128)(2,1)S(1)}, bf16[512,1536]{1,0:T(8,128)(2,1)}, f3...) custom-call(s32[5]{0:T(128)S(1)} %copy-done.13, f32[512,768]{1,0:T(8,128)} %get-tuple-element.223.refs_0_, ...), custom_call_target="tpu_custom_call" | custom-call | flops 9900000256 | tf_op jit(solution)/shard_map/ffn_backward/pallas_call | solution.py:522
  328.2 3.6 collective-permute-start.52
  335.4 5.8 %ffn_grads.3 = (bf16[4,192,1536]{2,1,0:T(8,128)(2,1)}, bf16[2,192,1536]{2,1,0:T(8,128)(2,1)S(1)}, bf16[2,192,1536]{2,1,0:T(8,128)(2,1)S(1)}) custom-call(s32[5]{0:T(128)S(1)} %copy-done.13, f32[512,768]{1,0:T(8,128)S(1)} %copy-done.40, bf16[512,1536]{1,0:T(8,128)(2,1)} %get-tuple-element.229.d_pre, bf16[512,768]{1,0:T(8,128)(2,1)S(1)} %get-tuple-element.238.d_ffn, ...), custom_call_target="tpu_custom_call" | custom-call | flops 7699999744 | tf_op jit(solution)/shard_map/ffn_grads/pallas_call | solution.py:571
  344.2 2.7 add_convert_fusion.4
  350.8 12.9 %attn_backward.3 = (bf16[512,768]{1,0:T(8,128)(2,1)S(1)}, f32[512,768]{1,0:T(8,128)}, bf16[512,768]{1,0:T(8,128)(2,1)S(1)}, bf16[512,1152]{1,0:T(8,128)(2,1)}, f...) custom-call(s32[5]{0:T(128)S(1)} %copy-done.13, f32[512,768]{1,0:T(8,128)} %get-tuple-element.248.d_second, ...), custom_call_target="tpu_custom_call" | custom-call | flops 16499999744 | tf_op jit(solution)/shard_map/attn_backward/pallas_call | solution.py:638
  363.7 3.5 collective-permute-start.68
  376.1 2.6 add_convert_fusion.3
  378.7 2.7 collective-permute-start.56
  382.7 2.9 attn_grads.3
  390.0 2.7 collective-permute-done.57
  392.7 10.8 %collective-permute-done.56 = bf16[2,192,1536]{2,1,0:T(8,128)(2,1)} collective-permute-done((bf16[2,192,1536]{2,1,0:T(8,128)(2,1)}, bf16[2,192,1536]{2,1,0:T(8,128)(2,1)}, u32[]{:S(2)}, u32[]{:S(2)}) %collective-permute-start.56) | collective-permute-done | bytes 1179680 | tf_op jit(solution)/shard_map/ppermute | solution.py:42
  405.3 4.1 collective-permute-start.59
  413.5 3.2 collective-permute-start.66
  417.9 12.0 %collective-permute-done.59 = bf16[192,1536]{1,0:T(8,128)(2,1)S(1)} collective-permute-done((bf16[192,1536]{1,0:T(8,128)(2,1)S(1)}, bf16[192,1536]{1,0:T(8,128)(2,1)S(1)}, u32[]{:S(2)}, u32[]{:S(2)}) %collective-permute-start.59) | collective-permute-done | bytes 589856 | tf_op jit(solution)/shard_map/ppermute | solution.py:42
  432.8 3.0 collective-permute-start.60
  439.0 5.5 %collective-permute-done.61 = bf16[2,208,768]{2,1,0:T(8,128)(2,1)S(1)} collective-permute-done((bf16[2,208,768]{2,1,0:T(8,128)(2,1)S(1)}, bf16[2,208,768]{2,1,0:T(8,128)(2,1)S(1)}, u32[]{:S(2)}, u32[]{:S(2)}) %collective-permute-start.61) | collective-permute-done | bytes 639008 | tf_op jit(solution)/shard_map/ppermute | solution.py:48
  448.4 2.7 collective-permute-start.64
  451.1 4.6 collective-permute-start.62
  455.8 4.0 collective-permute-done.63
  459.8 4.6 collective-permute-done.64
  464.4 2.7 collective-permute-done.62
  (434 shorter events, 162.4 us)
Async XLA Ops:
  25.8 27.8 %collective-permute-start.10 = (bf16[192,2304]{1,0:T(8,128)(2,1)S(1)}, bf16[192,2304]{1,0:T(8,128)(2,1)S(1)}, u32[]{:S(2)}, u32[]{:S(2)}) collective-permute-start(bf16[192,2304]{1,0:T(8,128)(2,1)S(1)} %concatenate.43.refs_1_.p0.refs_5_.refs_8_.refs_7_), channel_id=1, source_target_pairs={{0,1},{1,0},{2,3},{3,2},{4,5},{5,4},{6,7},{7,6},{8,9},{9,8},{10,11... | collective-permute-start | bytes 2654216 | tf_op jit(solution)/shard_map/ppermute | solution.py:36
  26.4 27.2 %collective-permute-start.11 = (bf16[192,2304]{1,0:T(8,128)(2,1)S(1)}, bf16[192,2304]{1,0:T(8,128)(2,1)}, u32[]{:S(2)}, u32[]{:S(2)}) collective-permute-start(bf16[192,2304]{1,0:T(8,128)(2,1)S(1)} %concatenate.43.refs_1_.p0.refs_5_.refs_8_.refs_7_), channel_id=1, source_target_pairs={{0,18},{1,19},{2,16},{3,17},{16,2},{17,3},{18,0},{19,1},{4,22},{5,... | collective-permute-start | bytes 2654216 | tf_op jit(solution)/shard_map/ppermute | solution.py:86
  28.5 15.0 %collective-permute-start.7 = (bf16[192,768]{1,0:T(8,128)(2,1)}, bf16[192,768]{1,0:T(8,128)(2,1)S(1)}, u32[]{:S(2)}, u32[]{:S(2)}) collective-permute-start(bf16[192,768]{1,0:T(8,128)(2,1)} %pad_maximum_fusion.9), channel_id=1, source_target_pairs={{0,4},{4,0},{8,12},{12,8},{1,5},{5,1},{9,13},{13,9},{2,6},{6,2},{1... | collective-permute-start | bytes 884744 | tf_op jit(solution)/shard_map/ppermute | solution.py:36
  29.4 24.3 %collective-permute-start.8 = (bf16[192,768]{1,0:T(8,128)(2,1)}, bf16[192,768]{1,0:T(8,128)(2,1)S(1)}, u32[]{:S(2)}, u32[]{:S(2)}) collective-permute-start(bf16[192,768]{1,0:T(8,128)(2,1)} %pad_maximum_fusion.9), channel_id=1, source_target_pairs={{0,8},{4,12},{8,0},{12,4},{1,9},{5,13},{9,1},{13,5},{2,10},{6,14},... | collective-permute-start | bytes 884744 | tf_op jit(solution)/shard_map/ppermute | solution.py:36
  33.7 20.0 %collective-permute-start.9 = (bf16[192,768]{1,0:T(8,128)(2,1)}, bf16[192,768]{1,0:T(8,128)(2,1)}, u32[]{:S(2)}, u32[]{:S(2)}) collective-permute-start(bf16[192,768]{1,0:T(8,128)(2,1)} %pad_maximum_fusion.9), channel_id=1, source_target_pairs={{0,12},{4,8},{8,4},{12,0},{1,13},{5,9},{9,5},{13,1},{2,14},{6,10},... | collective-permute-start | bytes 884744 | tf_op jit(solution)/shard_map/ppermute | solution.py:36
  55.9 20.2 %collective-permute-start.12 = (bf16[3,192,768]{2,1,0:T(8,128)(2,1)}, bf16[3,192,768]{2,1,0:T(8,128)(2,1)}, u32[]{:S(2)}, u32[]{:S(2)}) collective-permute-start(bf16[3,192,768]{2,1,0:T(8,128)(2,1)} %pad_maximum_fusion.refs_6_.refs_7_.refs_10_.refs_11_.p5.p6), channel_id=1, source_target_pairs={{0,1},{1,0},{2,3},{3,2},{4,5},{5,4},{6,7},{7,6},{8,9},{9,8},{10,11... | collective-permute-start | bytes 2654216 | tf_op jit(solution)/shard_map/ppermute | solution.py:36
  57.8 36.2 %collective-permute-start.18 = (bf16[3,192,768]{2,1,0:T(8,128)(2,1)}, bf16[3,192,768]{2,1,0:T(8,128)(2,1)}, u32[]{:S(2)}, u32[]{:S(2)}) collective-permute-start(bf16[3,192,768]{2,1,0:T(8,128)(2,1)} %pad_maximum_fusion.refs_6_.refs_7_.refs_10_.refs_11_.p5.p6), channel_id=1, source_target_pairs={{0,18},{1,19},{2,16},{3,17},{16,2},{17,3},{18,0},{19,1},{4,22},{5,... | collective-permute-start | bytes 2654216 | tf_op jit(solution)/shard_map/ppermute | solution.py:86
  58.0 34.3 %collective-permute-start.19 = (bf16[192,1536]{1,0:T(8,128)(2,1)}, bf16[192,1536]{1,0:T(8,128)(2,1)S(1)}, u32[]{:S(2)}, u32[]{:S(2)}) collective-permute-start(bf16[192,1536]{1,0:T(8,128)(2,1)} %pad_maximum_fusion.4), channel_id=1, source_target_pairs={{0,4},{4,0},{8,12},{12,8},{1,5},{5,1},{9,13},{13,9},{2,6},{6,2},{1... | collective-permute-start | bytes 1769480 | tf_op jit(solution)/shard_map/ppermute | solution.py:36
  64.1 29.8 %collective-permute-start.20 = (bf16[192,1536]{1,0:T(8,128)(2,1)}, bf16[192,1536]{1,0:T(8,128)(2,1)}, u32[]{:S(2)}, u32[]{:S(2)}) collective-permute-start(bf16[192,1536]{1,0:T(8,128)(2,1)} %pad_maximum_fusion.4), channel_id=1, source_target_pairs={{0,8},{4,12},{8,0},{12,4},{1,9},{5,13},{9,1},{13,5},{2,10},{6,14},... | collective-permute-start | bytes 1769480 | tf_op jit(solution)/shard_map/ppermute | solution.py:36
  65.9 23.5 %collective-permute-start.16 = (bf16[192,1152]{1,0:T(8,128)(2,1)}, bf16[192,1152]{1,0:T(8,128)(2,1)S(1)}, u32[]{:S(2)}, u32[]{:S(2)}) collective-permute-start(bf16[192,1152]{1,0:T(8,128)(2,1)} %slice.434), channel_id=1, source_target_pairs={{0,18},{1,19},{2,16},{3,17},{16,2},{17,3},{18,0},{19,1},{4,22},{5,... | collective-permute-start | bytes 1327112 | tf_op jit(solution)/shard_map/ppermute | solution.py:86
  76.1 15.6 %collective-permute-start.17 = (bf16[192,1152]{1,0:T(8,128)(2,1)}, bf16[192,1152]{1,0:T(8,128)(2,1)S(1)}, u32[]{:S(2)}, u32[]{:S(2)}) collective-permute-start(bf16[192,1152]{1,0:T(8,128)(2,1)} %slice.435), channel_id=1, source_target_pairs={{0,1},{1,0},{2,3},{3,2},{4,5},{5,4},{6,7},{7,6},{8,9},{9,8},{10,11... | collective-permute-start | bytes 1327112 | tf_op jit(solution)/shard_map/ppermute | solution.py:36
  89.3 25.3 %collective-permute-start.24 = (bf16[192,1536]{1,0:T(8,128)(2,1)}, bf16[192,1536]{1,0:T(8,128)(2,1)}, u32[]{:S(2)}, u32[]{:S(2)}) collective-permute-start(bf16[192,1536]{1,0:T(8,128)(2,1)} %pad_maximum_fusion.4), channel_id=1, source_target_pairs={{0,12},{4,8},{8,4},{12,0},{1,13},{5,9},{9,5},{13,1},{2,14},{6,10},... | collective-permute-start | bytes 1769480 | tf_op jit(solution)/shard_map/ppermute | solution.py:36
  95.8 18.9 %collective-permute-start.21 = (bf16[3,192,384]{2,1,0:T(8,128)(2,1)}, bf16[3,192,384]{2,1,0:T(8,128)(2,1)S(1)}, u32[]{:S(2)}, u32[]{:S(2)}) collective-permute-start(bf16[3,192,384]{2,1,0:T(8,128)(2,1)} %slice.343), channel_id=1, source_target_pairs={{0,18},{1,19},{2,16},{3,17},{16,2},{17,3},{18,0},{19,1},{4,22},{5,... | collective-permute-start | bytes 1327112 | tf_op jit(solution)/shard_map/ppermute | solution.py:86
  97.6 17.1 %collective-permute-start.22 = (bf16[3,192,384]{2,1,0:T(8,128)(2,1)}, bf16[3,192,384]{2,1,0:T(8,128)(2,1)S(1)}, u32[]{:S(2)}, u32[]{:S(2)}) collective-permute-start(bf16[3,192,384]{2,1,0:T(8,128)(2,1)} %slice.344), channel_id=1, source_target_pairs={{0,1},{1,0},{2,3},{3,2},{4,5},{5,4},{6,7},{7,6},{8,9},{9,8},{10,11... | collective-permute-start | bytes 1327112 | tf_op jit(solution)/shard_map/ppermute | solution.py:36
  105.2 18.5 %collective-permute-start.14 = (bf16[2,128,768]{2,1,0:T(8,128)(2,1)S(1)}, bf16[2,128,768]{2,1,0:T(8,128)(2,1)S(1)}, u32[]{:S(2)}, u32[]{:S(2)}) collective-permute-start(bf16[2,128,768]{2,1,0:T(8,128)(2,1)S(1)} %pad_maximum_fusion.6), channel_id=1, source_target_pairs={{0,2},{1,3},{2,0},{3,1},{4,6},{5,7},{6,4},{7,5},{8,10},{9,11},{10,... | collective-permute-start | bytes 1179656 | tf_op jit(solution)/shard_map/ppermute | solution.py:36
  118.6 19.2 %collective-permute-start.25 = (bf16[3,192,768]{2,1,0:T(8,128)(2,1)}, bf16[3,192,768]{2,1,0:T(8,128)(2,1)}, u32[]{:S(2)}, u32[]{:S(2)}) collective-permute-start(bf16[3,192,768]{2,1,0:T(8,128)(2,1)} %pad_maximum_fusion.1.p5.refs_13_.refs_12_), channel_id=1, source_target_pairs={{0,1},{1,0},{2,3},{3,2},{4,5},{5,4},{6,7},{7,6},{8,9},{9,8},{10,11... | collective-permute-start | bytes 2654216 | tf_op jit(solution)/shard_map/ppermute | solution.py:36
  127.0 24.5 %collective-permute-start.28 = (bf16[3,192,768]{2,1,0:T(8,128)(2,1)S(1)}, bf16[3,192,768]{2,1,0:T(8,128)(2,1)S(1)}, u32[]{:S(2)}, u32[]{:S(2)}) collective-permute-start(bf16[3,192,768]{2,1,0:T(8,128)(2,1)S(1)} %pad_maximum_fusion.2.p6.refs_14_.refs_13_), channel_id=1, source_target_pairs={{0,18},{1,19},{2,16},{3,17},{16,2},{17,3},{18,0},{19,1},{4,22},{5,... | collective-permute-start | bytes 2654216 | tf_op jit(solution)/shard_map/ppermute | solution.py:86
  128.3 32.3 %collective-permute-start.26 = (bf16[3,192,768]{2,1,0:T(8,128)(2,1)S(1)}, bf16[3,192,768]{2,1,0:T(8,128)(2,1)S(1)}, u32[]{:S(2)}, u32[]{:S(2)}) collective-permute-start(bf16[3,192,768]{2,1,0:T(8,128)(2,1)S(1)} %pad_maximum_fusion.2.p6.refs_14_.refs_13_), channel_id=1, source_target_pairs={{0,1},{1,0},{2,3},{3,2},{4,5},{5,4},{6,7},{7,6},{8,9},{9,8},{10,11... | collective-permute-start | bytes 2654216 | tf_op jit(solution)/shard_map/ppermute | solution.py:36
  129.6 38.2 %collective-permute-start.27 = (bf16[3,192,768]{2,1,0:T(8,128)(2,1)}, bf16[3,192,768]{2,1,0:T(8,128)(2,1)S(1)}, u32[]{:S(2)}, u32[]{:S(2)}) collective-permute-start(bf16[3,192,768]{2,1,0:T(8,128)(2,1)} %pad_maximum_fusion.1.p5.refs_13_.refs_12_), channel_id=1, source_target_pairs={{0,18},{1,19},{2,16},{3,17},{16,2},{17,3},{18,0},{19,1},{4,22},{5,... | collective-permute-start | bytes 2654216 | tf_op jit(solution)/shard_map/ppermute | solution.py:86
  137.8 48.9 %collective-permute-start.29 = (bf16[3,192,768]{2,1,0:T(8,128)(2,1)}, bf16[3,192,768]{2,1,0:T(8,128)(2,1)S(1)}, u32[]{:S(2)}, u32[]{:S(2)}) collective-permute-start(bf16[3,192,768]{2,1,0:T(8,128)(2,1)} %collective-permute-done.25.p7.refs_15_.refs_14_), channel_id=1, source_target_pairs={{0,18},{1,19},{2,16},{3,17},{16,2},{17,3},{18,0},{19,1},{4,22},{5,... | collective-permute-start | bytes 2654216 | tf_op jit(solution)/shard_map/ppermute | solution.py:86
  151.5 35.2 %collective-permute-start.30 = (bf16[3,192,768]{2,1,0:T(8,128)(2,1)S(1)}, bf16[3,192,768]{2,1,0:T(8,128)(2,1)S(1)}, u32[]{:S(2)}, u32[]{:S(2)}) collective-permute-start(bf16[3,192,768]{2,1,0:T(8,128)(2,1)S(1)} %collective-permute-done.28.p10.refs_18_.refs_17_), channel_id=1, source_target_pairs={{0,1},{1,0},{2,3},{3,2},{4,5},{5,4},{6,7},{7,6},{8,9},{9,8},{10,11... | collective-permute-start | bytes 2654216 | tf_op jit(solution)/shard_map/ppermute | solution.py:36
  154.0 32.7 %collective-permute-start.23 = (bf16[512,768]{1,0:T(8,128)(2,1)S(1)}, bf16[512,768]{1,0:T(8,128)(2,1)S(1)}, u32[]{:S(2)}, u32[]{:S(2)}) collective-permute-start(bf16[512,768]{1,0:T(8,128)(2,1)S(1)} %get-tuple-element.172.own), channel_id=1, source_target_pairs={{0,16},{16,0},{1,17},{17,1},{2,18},{18,2},{3,19},{19,3},{4,20},{20... | collective-permute-start | bytes 2359304 | tf_op jit(solution)/shard_map/ppermute | solution.py:32
  276.8 32.8 %collective-permute-start.41 = (bf16[4,192,1536]{2,1,0:T(8,128)(2,1)}, bf16[4,192,1536]{2,1,0:T(8,128)(2,1)}, u32[]{:S(2)}, u32[]{:S(2)}) collective-permute-start(bf16[4,192,1536]{2,1,0:T(8,128)(2,1)} %get-tuple-element.242), channel_id=1, source_target_pairs={{0,18},{1,19},{2,16},{3,17},{4,22},{5,23},{6,20},{7,21},{8,26},{9,... | collective-permute-start | bytes 7077896 | tf_op jit(solution)/shard_map/ppermute | solution.py:48
  281.2 28.4 %collective-permute-start.42 = (bf16[2,192,1536]{2,1,0:T(8,128)(2,1)S(1)}, bf16[2,192,1536]{2,1,0:T(8,128)(2,1)S(1)}, u32[]{:S(2)}, u32[]{:S(2)}) collective-permute-start(bf16[2,192,1536]{2,1,0:T(8,128)(2,1)S(1)} %get-tuple-element.201), channel_id=1, source_target_pairs={{0,1},{1,0},{2,3},{3,2},{4,5},{5,4},{6,7},{7,6},{8,9},{9,8},{10,11... | collective-permute-start | bytes 3538952 | tf_op jit(solution)/shard_map/ppermute | solution.py:36
  294.8 23.1 %collective-permute-start.43 = (bf16[512,768]{1,0:T(8,128)(2,1)S(1)}, bf16[512,768]{1,0:T(8,128)(2,1)S(1)}, u32[]{:S(2)}, u32[]{:S(2)}) collective-permute-start(bf16[512,768]{1,0:T(8,128)(2,1)S(1)} %get-tuple-element.224.refs_1_), channel_id=1, source_target_pairs={{0,16},{16,0},{1,17},{17,1},{2,18},{18,2},{3,19},{19,3},{4,20},{20... | collective-permute-start | bytes 2359304 | tf_op jit(solution)/shard_map/ppermute | solution.py:32
  299.0 27.3 %collective-permute-start.44 = (bf16[4,208,768]{2,1,0:T(8,128)(2,1)S(1)}, bf16[4,208,768]{2,1,0:T(8,128)(2,1)}, u32[]{:S(2)}, u32[]{:S(2)}) collective-permute-start(bf16[4,208,768]{2,1,0:T(8,128)(2,1)S(1)} %get-tuple-element.257), channel_id=1, source_target_pairs={{0,18},{1,19},{2,16},{3,17},{4,22},{5,23},{6,20},{7,21},{8,26},{9,... | collective-permute-start | bytes 3833864 | tf_op jit(solution)/shard_map/ppermute | solution.py:48
  304.1 22.2 %collective-permute-start.45 = (bf16[2,208,768]{2,1,0:T(8,128)(2,1)S(1)}, bf16[2,208,768]{2,1,0:T(8,128)(2,1)S(1)}, u32[]{:S(2)}, u32[]{:S(2)}) collective-permute-start(bf16[2,208,768]{2,1,0:T(8,128)(2,1)S(1)} %get-tuple-element.218), channel_id=1, source_target_pairs={{0,1},{1,0},{2,3},{3,2},{4,5},{5,4},{6,7},{7,6},{8,9},{9,8},{10,11... | collective-permute-start | bytes 1916936 | tf_op jit(solution)/shard_map/ppermute | solution.py:36
  311.0 30.2 %collective-permute-start.47 = (bf16[2,192,1536]{2,1,0:T(8,128)(2,1)}, bf16[2,192,1536]{2,1,0:T(8,128)(2,1)}, u32[]{:S(2)}, u32[]{:S(2)}) collective-permute-start(bf16[2,192,1536]{2,1,0:T(8,128)(2,1)} %add_convert_fusion.6), channel_id=1, source_target_pairs={{0,18},{1,19},{2,16},{3,17},{4,22},{5,23},{6,20},{7,21},{8,26},{9,... | collective-permute-start | bytes 3538952 | tf_op jit(solution)/shard_map/ppermute | solution.py:48
  316.2 26.6 %collective-permute-start.46 = (bf16[2,192,1536]{2,1,0:T(8,128)(2,1)}, bf16[2,192,1536]{2,1,0:T(8,128)(2,1)}, u32[]{:S(2)}, u32[]{:S(2)}) collective-permute-start(bf16[2,192,1536]{2,1,0:T(8,128)(2,1)} %add_convert_fusion.7), channel_id=1, source_target_pairs={{16,17},{17,16},{18,19},{19,18},{20,21},{21,20},{22,23},{23,22},{2... | collective-permute-start | bytes 3538952 | tf_op jit(solution)/shard_map/ppermute | solution.py:42
  326.2 22.8 %collective-permute-start.48 = (bf16[512,768]{1,0:T(8,128)(2,1)S(1)}, bf16[512,768]{1,0:T(8,128)(2,1)S(1)}, u32[]{:S(2)}, u32[]{:S(2)}) collective-permute-start(bf16[512,768]{1,0:T(8,128)(2,1)S(1)} %get-tuple-element.233.own), channel_id=1, source_target_pairs={{0,16},{16,0},{1,17},{17,1},{2,18},{18,2},{3,19},{19,3},{4,20},{20... | collective-permute-start | bytes 2359304 | tf_op jit(solution)/shard_map/ppermute | solution.py:32
  328.2 35.5 %collective-permute-start.52 = (bf16[2,208,768]{2,1,0:T(8,128)(2,1)}, bf16[2,208,768]{2,1,0:T(8,128)(2,1)}, u32[]{:S(2)}, u32[]{:S(2)}) collective-permute-start(bf16[2,208,768]{2,1,0:T(8,128)(2,1)} %add_convert_fusion.14), channel_id=1, source_target_pairs={{0,18},{1,19},{2,16},{3,17},{4,22},{5,23},{6,20},{7,21},{8,26},{9,... | collective-permute-start | bytes 1916936 | tf_op jit(solution)/shard_map/ppermute | solution.py:48
  333.9 33.4 %collective-permute-start.51 = (bf16[2,208,768]{2,1,0:T(8,128)(2,1)}, bf16[2,208,768]{2,1,0:T(8,128)(2,1)}, u32[]{:S(2)}, u32[]{:S(2)}) collective-permute-start(bf16[2,208,768]{2,1,0:T(8,128)(2,1)} %add_convert_fusion.15), channel_id=1, source_target_pairs={{16,17},{17,16},{18,19},{19,18},{20,21},{21,20},{22,23},{23,22},{2... | collective-permute-start | bytes 1916936 | tf_op jit(solution)/shard_map/ppermute | solution.py:42
  341.3 31.2 %collective-permute-start.50 = (bf16[2,192,1536]{2,1,0:T(8,128)(2,1)S(1)}, bf16[2,192,1536]{2,1,0:T(8,128)(2,1)S(1)}, u32[]{:S(2)}, u32[]{:S(2)}) collective-permute-start(bf16[2,192,1536]{2,1,0:T(8,128)(2,1)S(1)} %get-tuple-element.240), channel_id=1, source_target_pairs={{0,1},{1,0},{2,3},{3,2},{4,5},{5,4},{6,7},{7,6},{8,9},{9,8},{10,11... | collective-permute-start | bytes 3538952 | tf_op jit(solution)/shard_map/ppermute | solution.py:36
  342.7 30.6 %collective-permute-start.49 = (bf16[4,192,1536]{2,1,0:T(8,128)(2,1)}, bf16[4,192,1536]{2,1,0:T(8,128)(2,1)}, u32[]{:S(2)}, u32[]{:S(2)}) collective-permute-start(bf16[4,192,1536]{2,1,0:T(8,128)(2,1)} %get-tuple-element.279), channel_id=1, source_target_pairs={{16,2},{17,3},{18,0},{19,1},{20,6},{21,7},{22,4},{23,5},{24,10},{2... | collective-permute-start | bytes 7077896 | tf_op jit(solution)/shard_map/ppermute | solution.py:48
  349.1 38.1 %collective-permute-start.58 = (bf16[2,192,1536]{2,1,0:T(8,128)(2,1)}, bf16[2,192,1536]{2,1,0:T(8,128)(2,1)}, u32[]{:S(2)}, u32[]{:S(2)}) collective-permute-start(bf16[2,192,1536]{2,1,0:T(8,128)(2,1)} %add_convert_fusion.4), channel_id=1, source_target_pairs={{16,24},{20,28},{24,16},{28,20},{17,25},{21,29},{25,17},{29,21},{1... | collective-permute-start | bytes 3538952 | tf_op jit(solution)/shard_map/ppermute | solution.py:42
  363.7 17.6 %collective-permute-start.68 = (bf16[512,768]{1,0:T(8,128)(2,1)S(1)}, bf16[512,768]{1,0:T(8,128)(2,1)S(1)}, u32[]{:S(2)}, u32[]{:S(2)}) collective-permute-start(bf16[512,768]{1,0:T(8,128)(2,1)S(1)} %get-tuple-element.256), channel_id=1, source_target_pairs={{0,16},{16,0},{1,17},{17,1},{2,18},{18,2},{3,19},{19,3},{4,20},{20... | collective-permute-start | bytes 2359304 | tf_op jit(solution)/shard_map/ppermute | solution.py:32
  369.5 42.0 %collective-permute-start.55 = (bf16[2,208,768]{2,1,0:T(8,128)(2,1)}, bf16[2,208,768]{2,1,0:T(8,128)(2,1)}, u32[]{:S(2)}, u32[]{:S(2)}) collective-permute-start(bf16[2,208,768]{2,1,0:T(8,128)(2,1)} %add_convert_fusion.12), channel_id=1, source_target_pairs={{16,24},{20,28},{24,16},{28,20},{17,25},{21,29},{25,17},{29,21},{1... | collective-permute-start | bytes 1916936 | tf_op jit(solution)/shard_map/ppermute | solution.py:42
  374.6 18.0 %collective-permute-start.57 = (bf16[2,192,1536]{2,1,0:T(8,128)(2,1)}, bf16[2,192,1536]{2,1,0:T(8,128)(2,1)}, u32[]{:S(2)}, u32[]{:S(2)}) collective-permute-start(bf16[2,192,1536]{2,1,0:T(8,128)(2,1)} %add_convert_fusion.2), channel_id=1, source_target_pairs={{16,2},{17,3},{18,0},{19,1},{20,6},{21,7},{22,4},{23,5},{24,10},{2... | collective-permute-start | bytes 3538952 | tf_op jit(solution)/shard_map/ppermute | solution.py:48
  378.7 24.8 %collective-permute-start.56 = (bf16[2,192,1536]{2,1,0:T(8,128)(2,1)}, bf16[2,192,1536]{2,1,0:T(8,128)(2,1)}, u32[]{:S(2)}, u32[]{:S(2)}) collective-permute-start(bf16[2,192,1536]{2,1,0:T(8,128)(2,1)} %add_convert_fusion.3), channel_id=1, source_target_pairs={{0,1},{1,0},{2,3},{3,2},{4,5},{5,4},{6,7},{7,6},{8,9},{9,8},{10,11... | collective-permute-start | bytes 3538952 | tf_op jit(solution)/shard_map/ppermute | solution.py:42
  385.6 32.3 %collective-permute-start.54 = (bf16[2,208,768]{2,1,0:T(8,128)(2,1)S(1)}, bf16[2,208,768]{2,1,0:T(8,128)(2,1)S(1)}, u32[]{:S(2)}, u32[]{:S(2)}) collective-permute-start(bf16[2,208,768]{2,1,0:T(8,128)(2,1)S(1)} %get-tuple-element.276), channel_id=1, source_target_pairs={{0,1},{1,0},{2,3},{3,2},{4,5},{5,4},{6,7},{7,6},{8,9},{9,8},{10,11... | collective-permute-start | bytes 1916936 | tf_op jit(solution)/shard_map/ppermute | solution.py:36
  387.1 30.8 %collective-permute-start.53 = (bf16[4,208,768]{2,1,0:T(8,128)(2,1)S(1)}, bf16[4,208,768]{2,1,0:T(8,128)(2,1)S(1)}, u32[]{:S(2)}, u32[]{:S(2)}) collective-permute-start(bf16[4,208,768]{2,1,0:T(8,128)(2,1)S(1)} %get-tuple-element.291), channel_id=1, source_target_pairs={{16,2},{17,3},{18,0},{19,1},{20,6},{21,7},{22,4},{23,5},{24,10},{2... | collective-permute-start | bytes 3833864 | tf_op jit(solution)/shard_map/ppermute | solution.py:48
  405.3 24.7 %collective-permute-start.59 = (bf16[192,1536]{1,0:T(8,128)(2,1)S(1)}, bf16[192,1536]{1,0:T(8,128)(2,1)S(1)}, u32[]{:S(2)}, u32[]{:S(2)}) collective-permute-start(bf16[192,1536]{1,0:T(8,128)(2,1)S(1)} %get-tuple-element.361), channel_id=1, source_target_pairs={{0,8},{4,12},{8,0},{12,4},{1,9},{5,13},{9,1},{13,5},{2,10},{6,14},... | collective-permute-start | bytes 1769480 | tf_op jit(solution)/shard_map/ppermute | solution.py:42
  411.4 24.5 %collective-permute-start.67 = (bf16[192,1536]{1,0:T(8,128)(2,1)S(1)}, bf16[192,1536]{1,0:T(8,128)(2,1)S(1)}, u32[]{:S(2)}, u32[]{:S(2)}) collective-permute-start(bf16[192,1536]{1,0:T(8,128)(2,1)S(1)} %get-tuple-element.360), channel_id=1, source_target_pairs={{0,12},{4,8},{8,4},{12,0},{1,13},{5,9},{9,5},{13,1},{2,14},{6,10},... | collective-permute-start | bytes 1769480 | tf_op jit(solution)/shard_map/ppermute | solution.py:42
  413.5 22.7 %collective-permute-start.66 = (bf16[192,1536]{1,0:T(8,128)(2,1)S(1)}, bf16[192,1536]{1,0:T(8,128)(2,1)S(1)}, u32[]{:S(2)}, u32[]{:S(2)}) collective-permute-start(bf16[192,1536]{1,0:T(8,128)(2,1)S(1)} %get-tuple-element.362), channel_id=1, source_target_pairs={{0,4},{4,0},{8,12},{12,8},{1,5},{5,1},{9,13},{13,9},{2,6},{6,2},{1... | collective-permute-start | bytes 1769480 | tf_op jit(solution)/shard_map/ppermute | solution.py:42
  438.3 17.4 %collective-permute-start.70 = (bf16[2,128,768]{2,1,0:T(8,128)(2,1)S(1)}, bf16[2,128,768]{2,1,0:T(8,128)(2,1)S(1)}, u32[]{:S(2)}, u32[]{:S(2)}) collective-permute-start(bf16[2,128,768]{2,1,0:T(8,128)(2,1)S(1)} %pad_maximum_fusion.8), channel_id=1, source_target_pairs={{0,2},{1,3},{2,0},{3,1},{4,6},{5,7},{6,4},{7,5},{8,10},{9,11},{10,... | collective-permute-start | bytes 1179656 | tf_op jit(solution)/shard_map/ppermute | solution.py:36
  445.6 21.4 %collective-permute-start.65 = (bf16[208,2304]{1,0:T(8,128)(2,1)S(1)}, bf16[208,2304]{1,0:T(8,128)(2,1)S(1)}, u32[]{:S(2)}, u32[]{:S(2)}) collective-permute-start(bf16[208,2304]{1,0:T(8,128)(2,1)S(1)} %fusion.1), channel_id=1, source_target_pairs={{16,20},{20,16},{24,28},{28,24},{17,21},{21,17},{25,29},{29,25},{1... | collective-permute-start | bytes 2875400 | tf_op jit(solution)/shard_map/ppermute | solution.py:42
  448.4 16.1 %collective-permute-start.64 = (bf16[208,768]{1,0:T(8,128)(2,1)S(1)}, bf16[208,768]{1,0:T(8,128)(2,1)S(1)}, u32[]{:S(2)}, u32[]{:S(2)}) collective-permute-start(bf16[208,768]{1,0:T(8,128)(2,1)S(1)} %get-tuple-element.381), channel_id=1, source_target_pairs={{0,12},{4,8},{8,4},{12,0},{1,13},{5,9},{9,5},{13,1},{2,14},{6,10},... | collective-permute-start | bytes 958472 | tf_op jit(solution)/shard_map/ppermute | solution.py:42
  451.1 16.0 %collective-permute-start.62 = (bf16[208,768]{1,0:T(8,128)(2,1)S(1)}, bf16[208,768]{1,0:T(8,128)(2,1)S(1)}, u32[]{:S(2)}, u32[]{:S(2)}) collective-permute-start(bf16[208,768]{1,0:T(8,128)(2,1)S(1)} %get-tuple-element.383), channel_id=1, source_target_pairs={{0,4},{4,0},{8,12},{12,8},{1,5},{5,1},{9,13},{13,9},{2,6},{6,2},{1... | collective-permute-start | bytes 958472 | tf_op jit(solution)/shard_map/ppermute | solution.py:42
  (111 other events, 1774.9 us)
where the time goes:
time: 480 us; the launch traced here: 473 us
  waiting for transfers between devices  148 us (31%)
  starting transfers between devices  126 us (26%)
  Pallas kernels  106 us (22%)
  other arithmetic  47.5 us (10%)
  local copies, waits for them, and re-layouts  43.2 us (9%)
    ppermute x33, waiting for transfers between devices, hop(): lax.ppermute(block, axis, [(i, i ^ flip) for i in range(lax.axis_size(axi...  62.9 us
    ppermute x33, starting transfers between devices, hop(): lax.ppermute(block, axis, [(i, i ^ flip) for i in range(lax.axis_size(axi...  57.9 us
    ppermute x13, waiting for transfers between devices, core_hop(): return lax.ppermute(block, ('section', axis), route)  35 us
    ppermute x7, waiting for transfers between devices, cross_all(): return lax.ppermute(block, ('section', 'tensor'), route)  34.9 us
    ppermute x13, starting transfers between devices, core_hop(): return lax.ppermute(block, ('section', axis), route)  31.3 us
    convert_element_type x18, other arithmetic, add_low(): return total.astype(BF16)  26.9 us
    pallas_call x2, Pallas kernels, attn_backward(): pl.pallas_call(body, out_shape=[sds((length, width), BF16), sds((length,...  25.8 us
    pallas_call x2, Pallas kernels, attn_forward(): pl.pallas_call(body, out_shape=outs, in_specs=specs, out_specs=[VM] * len...  25.2 us
  transfers between devices with their start and end apart: 71, of which 31 were waited for; matrix products, arithmetic and copies ran while one was open for 13% of the time, Pallas kernels for 13%

commit v1 on v0

--- a/solution.py
+++ b/solution.py
@@ -477,11 +477,16 @@
             cls, grad, d_cls, tok = (refs.pop(0) for _ in range(4))
         else:
             d_above, own, other = (refs.pop(0) for _ in range(3))
-        xhat, scale, gain, slope = (refs.pop(0) for _ in range(4))
+        xhat_from, scale, gain, slope_from = (refs.pop(0) for _ in range(4))
         pieces = [refs.pop(0) for _ in range(13)]
-        part_out, second_out, low_out, pre_out, vec_out, inb_out, w_i, w_f, sems = refs
+        part_out, second_out, low_out, pre_out, vec_out, inb_out, w_i, w_f, sems, xhat, slope, kept_sems = refs
+        get_hat = pltpu.make_async_copy(xhat_from, xhat, kept_sems.at[0])
+        get_slope = pltpu.make_async_copy(slope_from, slope, kept_sems.at[1])
+        get_hat.start()
+        get_slope.start()
         first, second = load_b(meta, pieces, w_i, w_f, sems)
         sums = [jnp.zeros((1, width), F32) for _ in range(3)]
+        get_hat.wait()
         for rows in chunks(length):
             if level:
                 d_out = grad[rows, :].astype(F32)
@@ -499,6 +504,7 @@
         for n in range(3):
             vec_out[n : n + 1, :] = sums[n]
         wait_all(second)
+        get_slope.wait()
         for n, rows in enumerate(chunks(length, 256)):
             for c in chunks(units, units // 4):
                 d_act = nn(low_out[rows, :], w_f[:, c])
@@ -518,7 +524,7 @@
     else:
         args, specs = [meta, *sources], [SM, VM, VM, VM]
     args += [xhat, scale, gains, slope, *pieces]
-    specs += [VM] * 4 + [ANY] * 13
+    specs += [ANY, VM, VM, ANY] + [ANY] * 13
     return pl.pallas_call(
         body,
         out_shape=[
@@ -530,6 +536,8 @@
         scratch_shapes=[
             pltpu.VMEM((width, units), BF16), pltpu.VMEM((width, units), BF16),
             pltpu.SemaphoreType.DMA((copies_of(pieces[5]),)),
+            pltpu.VMEM((length, width), BF16), pltpu.VMEM((length, units), BF16),
+            pltpu.SemaphoreType.DMA((2,)),
         ],
         compiler_params=params(),
         cost_estimate=takes(9),
@@ -933,7 +941,7 @@
     sums_b[1].third(grads_a[1])
     sums_b[0].second_direct(sums_b[1].pieces)
     sums_a[1].third(sums_b[0].sums)
-    sums_a[0].first(sums_a[1].pieces, sums_b[0].hops[1:2] if direct else sums_b[0].sums)
+    sums_a[0].first(sums_a[1].pieces, sums_b[0].hops[:1] if direct else sums_b[0].sums)
     sums_a[0].second_direct(sums_a[0].added)
     last_a1, last_b1 = last_dp([sums_a[1], sums_b[1]], sums_a[0].sums)
     total_b0 = sums_b[0].third_direct()

time: 480 us -> 474 us (0.988)
  waiting for transfers between devices: 148 us -> 139 us
  starting transfers between devices: 126 us -> 131 us
    ppermute x8, waiting for transfers between devices: 9.09 us -> 4.19 us  [cross_hop(): return lax.ppermute(block, ('section', 'tensor'), route)]
  transfers between devices with their start and end apart: 71 -> 71, of which waited for: 31 -> 29; matrix products, arithmetic and copies ran while one was open for 13% -> 13% of each run, Pallas kernels for 13% -> 14%
where the time goes in v1:
time: 474 us; the launch traced here: 467 us
  waiting for transfers between devices  139 us (29%)
  starting transfers between devices  131 us (28%)
  Pallas kernels  104 us (22%)
  other arithmetic  47.5 us (10%)
  local copies, waits for them, and re-layouts  43.2 us (9%)
    ppermute x33, waiting for transfers between devices, hop(): lax.ppermute(block, axis, [(i, i ^ flip) for i in range(lax.axis_size(axi...  60.8 us
    ppermute x33, starting transfers between devices, hop(): lax.ppermute(block, axis, [(i, i ^ flip) for i in range(lax.axis_size(axi...  58.2 us
    ppermute x13, starting transfers between devices, core_hop(): return lax.ppermute(block, ('section', axis), route)  35.5 us
    ppermute x7, waiting for transfers between devices, cross_all(): return lax.ppermute(block, ('section', 'tensor'), route)  34.9 us
    ppermute x13, waiting for transfers between devices, core_hop(): return lax.ppermute(block, ('section', axis), route)  33.3 us
    convert_element_type x18, other arithmetic, add_low(): return total.astype(BF16)  26.9 us
    pallas_call x2, Pallas kernels, attn_backward(): pl.pallas_call(body, out_shape=[sds((length, width), BF16), sds((length,...  25.8 us
    pallas_call x2, Pallas kernels, attn_forward(): pl.pallas_call(body, out_shape=outs, in_specs=specs, out_specs=[VM] * len...  25.2 us
  transfers between devices with their start and end apart: 71, of which 29 were waited for; matrix products, arithmetic and copies ran while one was open for 13% of the time, Pallas kernels for 14%

profile of v1, /device:TPU:0, one launch (start us, length us, event | category | flops | bytes accessed | tf_op | source)
XLA Modules:
  0.0 467.2 jit_solution(18043726630979876422)
XLA Ops:
  5.2 3.1 collective-permute-start
  8.3 2.6 collective-permute-start.1
  29.4 3.5 collective-permute-start.8
  34.4 9.1 %collective-permute-done.7 = bf16[192,768]{1,0:T(8,128)(2,1)S(1)} collective-permute-done((bf16[192,768]{1,0:T(8,128)(2,1)}, bf16[192,768]{1,0:T(8,128)(2,1)S(1)}, u32[]{:S(2)}, u32[]{:S(2)}) %collective-permute-start.7) | collective-permute-done | bytes 294944 | tf_op jit(solution)/shard_map/ppermute | solution.py:36
  43.5 10.2 %collective-permute-done.8 = bf16[192,768]{1,0:T(8,128)(2,1)S(1)} collective-permute-done((bf16[192,768]{1,0:T(8,128)(2,1)}, bf16[192,768]{1,0:T(8,128)(2,1)S(1)}, u32[]{:S(2)}, u32[]{:S(2)}) %collective-permute-start.8) | collective-permute-done | bytes 294944 | tf_op jit(solution)/shard_map/ppermute | solution.py:36
  58.0 6.2 %collective-permute-start.19 = (bf16[192,1536]{1,0:T(8,128)(2,1)}, bf16[192,1536]{1,0:T(8,128)(2,1)S(1)}, u32[]{:S(2)}, u32[]{:S(2)}) collective-permute-start(bf16[192,1536]{1,0:T(8,128)(2,1)} %pad_maximum_fusion.4), channel_id=1, source_target_pairs={{0,4},{4,0},{8,12},{12,8},{1,5},{5,1},{9,13},{13,9},{2,6},{6,2},{1... | collective-permute-start | bytes 1769480 | tf_op jit(solution)/shard_map/ppermute | solution.py:36
  69.1 7.0 %collective-permute-done.12.refs_8_.refs_9_.refs_12_.refs_13_.p7.p8 = bf16[3,192,768]{2,1,0:T(8,128)(2,1)} collective-permute-done((bf16[3,192,768]{2,1,0:T(8,128)(2,1)}, bf16[3,192,768]{2,1,0:T(8,128)(2,1)}, u32[]{:S(2)}, u32[]{:S(2)}) %collective-permute-start.12) | collective-permute-done | bytes 884768 | tf_op jit(solution)/shard_map/ppermute | solution.py:36
  80.5 8.8 %collective-permute-done.16.refs_4_.p3.refs_8_.refs_11_.refs_10_ = bf16[192,1152]{1,0:T(8,128)(2,1)S(1)} collective-permute-done((bf16[192,1152]{1,0:T(8,128)(2,1)}, bf16[192,1152]{1,0:T(8,128)(2,1)S(1)}, u32[]{:S(2)}, u32[]{:S(2)}) %collective-permute-start.16) | collective-permute-done | bytes 442400 | tf_op jit(solution)/shard_map/ppermute | solution.py:86
  98.5 4.6 collective-permute-done.13
  105.2 9.4 %collective-permute-start.14 = (bf16[2,128,768]{2,1,0:T(8,128)(2,1)S(1)}, bf16[2,128,768]{2,1,0:T(8,128)(2,1)S(1)}, u32[]{:S(2)}, u32[]{:S(2)}) collective-permute-start(bf16[2,128,768]{2,1,0:T(8,128)(2,1)S(1)} %pad_maximum_fusion.6), channel_id=1, source_target_pairs={{0,2},{1,3},{2,0},{3,1},{4,6},{5,7},{6,4},{7,5},{8,10},{9,11},{10,... | collective-permute-start | bytes 1179656 | tf_op jit(solution)/shard_map/ppermute | solution.py:36
  120.1 3.7 collective-permute-done.14
  130.0 7.8 %collective-permute-done.25.p7.refs_15_.refs_14_ = bf16[3,192,768]{2,1,0:T(8,128)(2,1)} collective-permute-done((bf16[3,192,768]{2,1,0:T(8,128)(2,1)}, bf16[3,192,768]{2,1,0:T(8,128)(2,1)}, u32[]{:S(2)}, u32[]{:S(2)}) %collective-permute-start.25) | collective-permute-done | bytes 884768 | tf_op jit(solution)/shard_map/ppermute | solution.py:36
  139.4 12.1 %attn_forward.2 = (bf16[512,768]{1,0:T(8,128)(2,1)S(1)}, bf16[512,1152]{1,0:T(8,128)(2,1)}, bf16[6,512,512]{2,1,0:T(8,128)(2,1)}, bf16[512,384]{1,0:T(8,128)(2,1)S(1)}) custom-call(s32[5]{0:T(128)S(1)} %get-tuple-element.426.meta, bf16[512,768]{1,0:T(8,128)(2,1)S(1)} %get-tuple-element.166.refs_0_.x, ...), custom_call_target="tpu_custom_call" | custom-call | flops 14300000256 | tf_op jit(solution)/shard_map/attn_forward/pallas_call | solution.py:382
  154.0 6.7 %collective-permute-start.23 = (bf16[512,768]{1,0:T(8,128)(2,1)S(1)}, bf16[512,768]{1,0:T(8,128)(2,1)S(1)}, u32[]{:S(2)}, u32[]{:S(2)}) collective-permute-start(bf16[512,768]{1,0:T(8,128)(2,1)S(1)} %get-tuple-element.172.own), channel_id=1, source_target_pairs={{0,16},{16,0},{1,17},{17,1},{2,18},{18,2},{3,19},{19,3},{4,20},{20... | collective-permute-start | bytes 2359304 | tf_op jit(solution)/shard_map/ppermute | solution.py:32
  160.7 7.1 %collective-permute-done.27.p9.refs_17_.refs_16_ = bf16[3,192,768]{2,1,0:T(8,128)(2,1)S(1)} collective-permute-done((bf16[3,192,768]{2,1,0:T(8,128)(2,1)}, bf16[3,192,768]{2,1,0:T(8,128)(2,1)S(1)}, u32[]{:S(2)}, u32[]{:S(2)}) %collective-permute-start.27) | collective-permute-done | bytes 884768 | tf_op jit(solution)/shard_map/ppermute | solution.py:86
  167.8 19.0 %collective-permute-done.29.p11.refs_19_.refs_18_ = bf16[3,192,768]{2,1,0:T(8,128)(2,1)S(1)} collective-permute-done((bf16[3,192,768]{2,1,0:T(8,128)(2,1)}, bf16[3,192,768]{2,1,0:T(8,128)(2,1)S(1)}, u32[]{:S(2)}, u32[]{:S(2)}) %collective-permute-start.29) | collective-permute-done | bytes 884768 | tf_op jit(solution)/shard_map/ppermute | solution.py:86
  188.6 8.9 %ffn_forward.2 = (bf16[512,768]{1,0:T(8,128)(2,1)S(1)}, f32[512,768]{1,0:T(8,128)}, bf16[512,768]{1,0:T(8,128)(2,1)S(1)}, f32[512,1]{1,0:T(8,128)S(1)}, bf16[512...) custom-call(s32[5]{0:T(128)S(1)} %get-tuple-element.426.meta, bf16[512,768]{1,0:T(8,128)(2,1)S(1)} %get-tuple-element.166.refs_0_.x, ...), custom_call_target="tpu_custom_call" | custom-call | flops 9900000256 | tf_op jit(solution)/shard_map/ffn_forward/pallas_call | solution.py:420
  202.3 13.2 %attn_forward.3 = (bf16[512,768]{1,0:T(8,128)(2,1)S(1)}, bf16[512,1152]{1,0:T(8,128)(2,1)}, bf16[6,512,512]{2,1,0:T(8,128)(2,1)}, bf16[512,384]{1,0:T(8,128)(2,1...) custom-call(s32[5]{0:T(128)S(1)} %get-tuple-element.427.meta, ...), custom_call_target="tpu_custom_call" | custom-call | flops 14300000256 | tf_op jit(solution)/shard_map/attn_forward/pallas_call | solution.py:382
  218.9 8.9 %ffn_forward.3 = (bf16[512,768]{1,0:T(8,128)(2,1)S(1)}, f32[512,768]{1,0:T(8,128)}, bf16[512,768]{1,0:T(8,128)(2,1)S(1)}, f32[512,1]{1,0:T(8,128)S(1)}, bf16[512...) custom-call(s32[5]{0:T(128)S(1)} %get-tuple-element.427.meta, bf16[512,768]{1,0:T(8,128)(2,1)S(1)} %get-tuple-element.183.x, ...), custom_call_target="tpu_custom_call" | custom-call | flops 9900000256 | tf_op jit(solution)/shard_map/ffn_forward/pallas_call | solution.py:420
  236.1 5.8 %collective-permute-start.35 = (bf16[4,768]{1,0:T(4,128)(2,1)S(1)}, bf16[4,768]{1,0:T(4,128)(2,1)}, u32[]{:S(2)}, u32[]{:S(2)}) collective-permute-start(bf16[4,768]{1,0:T(4,128)(2,1)S(1)} %get-tuple-element.190), channel_id=1, source_target_pairs={{0,8},{4,12},{8,0},{12,4},{1,9},{5,13},{9,1},{13,5},{2,10},{6,14},... | collective-permute-start | bytes 18440 | tf_op jit(solution)/shard_map/ppermute | solution.py:36
  243.7 3.8 collective-permute-done.36
  262.1 7.1 %ffn_backward.2 = (bf16[512,768]{1,0:T(8,128)(2,1)S(1)}, f32[512,768]{1,0:T(8,128)}, bf16[512,768]{1,0:T(8,128)(2,1)S(1)}, bf16[512,1536]{1,0:T(8,128)(2,1)}, f3...) custom-call(s32[5]{0:T(128)S(1)} %copy-done.17, s32[4]{0:T(128)S(1)} %copy-done.15, ...), custom_call_target="tpu_custom_call" | custom-call | flops 9900000256 | tf_op jit(solution)/shard_map/ffn_backward/pallas_call | solution.py:528
  269.3 6.0 %ffn_grads.2 = (bf16[4,192,1536]{2,1,0:T(8,128)(2,1)}, bf16[2,192,1536]{2,1,0:T(8,128)(2,1)S(1)}, bf16[2,192,1536]{2,1,0:T(8,128)(2,1)S(1)}) custom-call(s32[5]{0:T(128)S(1)} %copy-done.17, f32[512,768]{1,0:T(8,128)S(1)} %copy-done.31, bf16[512,1536]{1,0:T(8,128)(2,1)} %get-tuple-element.198.d_pre, bf16[512,768]{1,0:T(8,128)(2,1)S(1)} %get-tuple-element.199.d_ffn, ...), custom_call_target="tpu_custom_call" | custom-call | flops 7699999744 | tf_op jit(solution)/shard_map/ffn_grads/pallas_call | solution.py:579
  275.3 4.3 collective-permute-start.41
  280.4 12.9 %attn_backward.2 = (bf16[512,768]{1,0:T(8,128)(2,1)S(1)}, f32[512,768]{1,0:T(8,128)}, bf16[512,768]{1,0:T(8,128)(2,1)S(1)}, bf16[512,1152]{1,0:T(8,128)(2,1)}, f...) custom-call(s32[5]{0:T(128)S(1)} %copy-done.17, f32[512,768]{1,0:T(8,128)} %get-tuple-element.202.d_second, ...), custom_call_target="tpu_custom_call" | custom-call | flops 16499999744 | tf_op jit(solution)/shard_map/attn_backward/pallas_call | solution.py:646
  294.6 2.9 attn_grads.2
  297.5 5.1 %collective-permute-start.44 = (bf16[4,208,768]{2,1,0:T(8,128)(2,1)S(1)}, bf16[4,208,768]{2,1,0:T(8,128)(2,1)}, u32[]{:S(2)}, u32[]{:S(2)}) collective-permute-start(bf16[4,208,768]{2,1,0:T(8,128)(2,1)S(1)} %get-tuple-element.257), channel_id=1, source_target_pairs={{0,18},{1,19},{2,16},{3,17},{4,22},{5,23},{6,20},{7,21},{8,26},{9,... | collective-permute-start | bytes 3833864 | tf_op jit(solution)/shard_map/ppermute | solution.py:48
  303.2 4.9 %collective-permute-done.42 = bf16[2,192,1536]{2,1,0:T(8,128)(2,1)S(1)} collective-permute-done((bf16[2,192,1536]{2,1,0:T(8,128)(2,1)S(1)}, bf16[2,192,1536]{2,1,0:T(8,128)(2,1)S(1)}, u32[]{:S(2)}, u32[]{:S(2)}) %collective-permute-start.42) | collective-permute-done | bytes 1179680 | tf_op jit(solution)/shard_map/ppermute | solution.py:36
  316.3 7.9 %ffn_backward.3 = (bf16[512,768]{1,0:T(8,128)(2,1)S(1)}, f32[512,768]{1,0:T(8,128)}, bf16[512,768]{1,0:T(8,128)(2,1)S(1)}, bf16[512,1536]{1,0:T(8,128)(2,1)}, f3...) custom-call(s32[5]{0:T(128)S(1)} %copy-done.13, f32[512,768]{1,0:T(8,128)} %get-tuple-element.223.refs_0_, ...), custom_call_target="tpu_custom_call" | custom-call | flops 9900000256 | tf_op jit(solution)/shard_map/ffn_backward/pallas_call | solution.py:528
  326.2 3.6 collective-permute-start.52
  333.4 5.8 %ffn_grads.3 = (bf16[4,192,1536]{2,1,0:T(8,128)(2,1)}, bf16[2,192,1536]{2,1,0:T(8,128)(2,1)S(1)}, bf16[2,192,1536]{2,1,0:T(8,128)(2,1)S(1)}) custom-call(s32[5]{0:T(128)S(1)} %copy-done.13, f32[512,768]{1,0:T(8,128)S(1)} %copy-done.40, bf16[512,1536]{1,0:T(8,128)(2,1)} %get-tuple-element.229.d_pre, bf16[512,768]{1,0:T(8,128)(2,1)S(1)} %get-tuple-element.238.d_ffn, ...), custom_call_target="tpu_custom_call" | custom-call | flops 7699999744 | tf_op jit(solution)/shard_map/ffn_grads/pallas_call | solution.py:579
  342.2 2.7 add_convert_fusion.4
  348.8 12.9 %attn_backward.3 = (bf16[512,768]{1,0:T(8,128)(2,1)S(1)}, f32[512,768]{1,0:T(8,128)}, bf16[512,768]{1,0:T(8,128)(2,1)S(1)}, bf16[512,1152]{1,0:T(8,128)(2,1)}, f...) custom-call(s32[5]{0:T(128)S(1)} %copy-done.13, f32[512,768]{1,0:T(8,128)} %get-tuple-element.248.d_second, ...), custom_call_target="tpu_custom_call" | custom-call | flops 16499999744 | tf_op jit(solution)/shard_map/attn_backward/pallas_call | solution.py:646
  361.7 3.5 collective-permute-start.68
  374.1 2.6 add_convert_fusion.3
  376.7 2.7 collective-permute-start.56
  380.7 2.9 attn_grads.3
  388.0 2.7 collective-permute-done.57
  390.7 10.8 %collective-permute-done.56 = bf16[2,192,1536]{2,1,0:T(8,128)(2,1)} collective-permute-done((bf16[2,192,1536]{2,1,0:T(8,128)(2,1)}, bf16[2,192,1536]{2,1,0:T(8,128)(2,1)}, u32[]{:S(2)}, u32[]{:S(2)}) %collective-permute-start.56) | collective-permute-done | bytes 1179680 | tf_op jit(solution)/shard_map/ppermute | solution.py:42
  407.4 4.1 collective-permute-start.66
  411.5 4.1 collective-permute-start.67
  416.8 5.4 %collective-permute-done.59 = bf16[192,1536]{1,0:T(8,128)(2,1)S(1)} collective-permute-done((bf16[192,1536]{1,0:T(8,128)(2,1)S(1)}, bf16[192,1536]{1,0:T(8,128)(2,1)S(1)}, u32[]{:S(2)}, u32[]{:S(2)}) %collective-permute-start.59) | collective-permute-done | bytes 589856 | tf_op jit(solution)/shard_map/ppermute | solution.py:42
  424.6 3.5 collective-permute-start.60
  428.2 4.6 collective-permute-done.66
  438.6 7.1 %collective-permute-start.63 = (bf16[208,768]{1,0:T(8,128)(2,1)S(1)}, bf16[208,768]{1,0:T(8,128)(2,1)S(1)}, u32[]{:S(2)}, u32[]{:S(2)}) collective-permute-start(bf16[208,768]{1,0:T(8,128)(2,1)S(1)} %get-tuple-element.382), channel_id=1, source_target_pairs={{0,8},{4,12},{8,0},{12,4},{1,9},{5,13},{9,1},{13,5},{2,10},{6,14},... | collective-permute-start | bytes 958472 | tf_op jit(solution)/shard_map/ppermute | solution.py:42
  445.7 3.0 collective-permute-start.64
  450.9 6.8 %collective-permute-done.63 = bf16[208,768]{1,0:T(8,128)(2,1)S(1)} collective-permute-done((bf16[208,768]{1,0:T(8,128)(2,1)S(1)}, bf16[208,768]{1,0:T(8,128)(2,1)S(1)}, u32[]{:S(2)}, u32[]{:S(2)}) %collective-permute-start.63) | collective-permute-done | bytes 319520 | tf_op jit(solution)/shard_map/ppermute | solution.py:42
  457.7 3.3 collective-permute-done.62
  (434 shorter events, 160.2 us)
Async XLA Ops:
  25.8 27.8 %collective-permute-start.10 = (bf16[192,2304]{1,0:T(8,128)(2,1)S(1)}, bf16[192,2304]{1,0:T(8,128)(2,1)S(1)}, u32[]{:S(2)}, u32[]{:S(2)}) collective-permute-start(bf16[192,2304]{1,0:T(8,128)(2,1)S(1)} %concatenate.43.refs_1_.p0.refs_5_.refs_8_.refs_7_), channel_id=1, source_target_pairs={{0,1},{1,0},{2,3},{3,2},{4,5},{5,4},{6,7},{7,6},{8,9},{9,8},{10,11... | collective-permute-start | bytes 2654216 | tf_op jit(solution)/shard_map/ppermute | solution.py:36
  26.4 27.2 %collective-permute-start.11 = (bf16[192,2304]{1,0:T(8,128)(2,1)S(1)}, bf16[192,2304]{1,0:T(8,128)(2,1)}, u32[]{:S(2)}, u32[]{:S(2)}) collective-permute-start(bf16[192,2304]{1,0:T(8,128)(2,1)S(1)} %concatenate.43.refs_1_.p0.refs_5_.refs_8_.refs_7_), channel_id=1, source_target_pairs={{0,18},{1,19},{2,16},{3,17},{16,2},{17,3},{18,0},{19,1},{4,22},{5,... | collective-permute-start | bytes 2654216 | tf_op jit(solution)/shard_map/ppermute | solution.py:86
  28.5 15.0 %collective-permute-start.7 = (bf16[192,768]{1,0:T(8,128)(2,1)}, bf16[192,768]{1,0:T(8,128)(2,1)S(1)}, u32[]{:S(2)}, u32[]{:S(2)}) collective-permute-start(bf16[192,768]{1,0:T(8,128)(2,1)} %pad_maximum_fusion.9), channel_id=1, source_target_pairs={{0,4},{4,0},{8,12},{12,8},{1,5},{5,1},{9,13},{13,9},{2,6},{6,2},{1... | collective-permute-start | bytes 884744 | tf_op jit(solution)/shard_map/ppermute | solution.py:36
  29.4 24.3 %collective-permute-start.8 = (bf16[192,768]{1,0:T(8,128)(2,1)}, bf16[192,768]{1,0:T(8,128)(2,1)S(1)}, u32[]{:S(2)}, u32[]{:S(2)}) collective-permute-start(bf16[192,768]{1,0:T(8,128)(2,1)} %pad_maximum_fusion.9), channel_id=1, source_target_pairs={{0,8},{4,12},{8,0},{12,4},{1,9},{5,13},{9,1},{13,5},{2,10},{6,14},... | collective-permute-start | bytes 884744 | tf_op jit(solution)/shard_map/ppermute | solution.py:36
  33.7 20.0 %collective-permute-start.9 = (bf16[192,768]{1,0:T(8,128)(2,1)}, bf16[192,768]{1,0:T(8,128)(2,1)}, u32[]{:S(2)}, u32[]{:S(2)}) collective-permute-start(bf16[192,768]{1,0:T(8,128)(2,1)} %pad_maximum_fusion.9), channel_id=1, source_target_pairs={{0,12},{4,8},{8,4},{12,0},{1,13},{5,9},{9,5},{13,1},{2,14},{6,10},... | collective-permute-start | bytes 884744 | tf_op jit(solution)/shard_map/ppermute | solution.py:36
  55.9 20.2 %collective-permute-start.12 = (bf16[3,192,768]{2,1,0:T(8,128)(2,1)}, bf16[3,192,768]{2,1,0:T(8,128)(2,1)}, u32[]{:S(2)}, u32[]{:S(2)}) collective-permute-start(bf16[3,192,768]{2,1,0:T(8,128)(2,1)} %pad_maximum_fusion.refs_6_.refs_7_.refs_10_.refs_11_.p5.p6), channel_id=1, source_target_pairs={{0,1},{1,0},{2,3},{3,2},{4,5},{5,4},{6,7},{7,6},{8,9},{9,8},{10,11... | collective-permute-start | bytes 2654216 | tf_op jit(solution)/shard_map/ppermute | solution.py:36
  57.8 36.2 %collective-permute-start.18 = (bf16[3,192,768]{2,1,0:T(8,128)(2,1)}, bf16[3,192,768]{2,1,0:T(8,128)(2,1)}, u32[]{:S(2)}, u32[]{:S(2)}) collective-permute-start(bf16[3,192,768]{2,1,0:T(8,128)(2,1)} %pad_maximum_fusion.refs_6_.refs_7_.refs_10_.refs_11_.p5.p6), channel_id=1, source_target_pairs={{0,18},{1,19},{2,16},{3,17},{16,2},{17,3},{18,0},{19,1},{4,22},{5,... | collective-permute-start | bytes 2654216 | tf_op jit(solution)/shard_map/ppermute | solution.py:86
  58.0 34.3 %collective-permute-start.19 = (bf16[192,1536]{1,0:T(8,128)(2,1)}, bf16[192,1536]{1,0:T(8,128)(2,1)S(1)}, u32[]{:S(2)}, u32[]{:S(2)}) collective-permute-start(bf16[192,1536]{1,0:T(8,128)(2,1)} %pad_maximum_fusion.4), channel_id=1, source_target_pairs={{0,4},{4,0},{8,12},{12,8},{1,5},{5,1},{9,13},{13,9},{2,6},{6,2},{1... | collective-permute-start | bytes 1769480 | tf_op jit(solution)/shard_map/ppermute | solution.py:36
  64.1 29.8 %collective-permute-start.20 = (bf16[192,1536]{1,0:T(8,128)(2,1)}, bf16[192,1536]{1,0:T(8,128)(2,1)}, u32[]{:S(2)}, u32[]{:S(2)}) collective-permute-start(bf16[192,1536]{1,0:T(8,128)(2,1)} %pad_maximum_fusion.4), channel_id=1, source_target_pairs={{0,8},{4,12},{8,0},{12,4},{1,9},{5,13},{9,1},{13,5},{2,10},{6,14},... | collective-permute-start | bytes 1769480 | tf_op jit(solution)/shard_map/ppermute | solution.py:36
  65.9 23.5 %collective-permute-start.16 = (bf16[192,1152]{1,0:T(8,128)(2,1)}, bf16[192,1152]{1,0:T(8,128)(2,1)S(1)}, u32[]{:S(2)}, u32[]{:S(2)}) collective-permute-start(bf16[192,1152]{1,0:T(8,128)(2,1)} %slice.434), channel_id=1, source_target_pairs={{0,18},{1,19},{2,16},{3,17},{16,2},{17,3},{18,0},{19,1},{4,22},{5,... | collective-permute-start | bytes 1327112 | tf_op jit(solution)/shard_map/ppermute | solution.py:86
  76.1 15.6 %collective-permute-start.17 = (bf16[192,1152]{1,0:T(8,128)(2,1)}, bf16[192,1152]{1,0:T(8,128)(2,1)S(1)}, u32[]{:S(2)}, u32[]{:S(2)}) collective-permute-start(bf16[192,1152]{1,0:T(8,128)(2,1)} %slice.435), channel_id=1, source_target_pairs={{0,1},{1,0},{2,3},{3,2},{4,5},{5,4},{6,7},{7,6},{8,9},{9,8},{10,11... | collective-permute-start | bytes 1327112 | tf_op jit(solution)/shard_map/ppermute | solution.py:36
  89.3 25.3 %collective-permute-start.24 = (bf16[192,1536]{1,0:T(8,128)(2,1)}, bf16[192,1536]{1,0:T(8,128)(2,1)}, u32[]{:S(2)}, u32[]{:S(2)}) collective-permute-start(bf16[192,1536]{1,0:T(8,128)(2,1)} %pad_maximum_fusion.4), channel_id=1, source_target_pairs={{0,12},{4,8},{8,4},{12,0},{1,13},{5,9},{9,5},{13,1},{2,14},{6,10},... | collective-permute-start | bytes 1769480 | tf_op jit(solution)/shard_map/ppermute | solution.py:36
  95.8 18.9 %collective-permute-start.21 = (bf16[3,192,384]{2,1,0:T(8,128)(2,1)}, bf16[3,192,384]{2,1,0:T(8,128)(2,1)S(1)}, u32[]{:S(2)}, u32[]{:S(2)}) collective-permute-start(bf16[3,192,384]{2,1,0:T(8,128)(2,1)} %slice.343), channel_id=1, source_target_pairs={{0,18},{1,19},{2,16},{3,17},{16,2},{17,3},{18,0},{19,1},{4,22},{5,... | collective-permute-start | bytes 1327112 | tf_op jit(solution)/shard_map/ppermute | solution.py:86
  97.6 17.1 %collective-permute-start.22 = (bf16[3,192,384]{2,1,0:T(8,128)(2,1)}, bf16[3,192,384]{2,1,0:T(8,128)(2,1)S(1)}, u32[]{:S(2)}, u32[]{:S(2)}) collective-permute-start(bf16[3,192,384]{2,1,0:T(8,128)(2,1)} %slice.344), channel_id=1, source_target_pairs={{0,1},{1,0},{2,3},{3,2},{4,5},{5,4},{6,7},{7,6},{8,9},{9,8},{10,11... | collective-permute-start | bytes 1327112 | tf_op jit(solution)/shard_map/ppermute | solution.py:36
  105.2 18.5 %collective-permute-start.14 = (bf16[2,128,768]{2,1,0:T(8,128)(2,1)S(1)}, bf16[2,128,768]{2,1,0:T(8,128)(2,1)S(1)}, u32[]{:S(2)}, u32[]{:S(2)}) collective-permute-start(bf16[2,128,768]{2,1,0:T(8,128)(2,1)S(1)} %pad_maximum_fusion.6), channel_id=1, source_target_pairs={{0,2},{1,3},{2,0},{3,1},{4,6},{5,7},{6,4},{7,5},{8,10},{9,11},{10,... | collective-permute-start | bytes 1179656 | tf_op jit(solution)/shard_map/ppermute | solution.py:36
  118.6 19.2 %collective-permute-start.25 = (bf16[3,192,768]{2,1,0:T(8,128)(2,1)}, bf16[3,192,768]{2,1,0:T(8,128)(2,1)}, u32[]{:S(2)}, u32[]{:S(2)}) collective-permute-start(bf16[3,192,768]{2,1,0:T(8,128)(2,1)} %pad_maximum_fusion.1.p5.refs_13_.refs_12_), channel_id=1, source_target_pairs={{0,1},{1,0},{2,3},{3,2},{4,5},{5,4},{6,7},{7,6},{8,9},{9,8},{10,11... | collective-permute-start | bytes 2654216 | tf_op jit(solution)/shard_map/ppermute | solution.py:36
  124.8 13.0 %collective-permute-start.15 = (bf16[512,768]{1,0:T(8,128)(2,1)}, bf16[512,768]{1,0:T(8,128)(2,1)}, u32[]{:S(2)}, u32[]{:S(2)}) collective-permute-start(bf16[512,768]{1,0:T(8,128)(2,1)} %pad_maximum_fusion.3), channel_id=1, source_target_pairs={{0,16},{16,0},{1,17},{17,1},{2,18},{18,2},{3,19},{19,3},{4,20},{20... | collective-permute-start | bytes 2359304 | tf_op jit(solution)/shard_map/ppermute | solution.py:32
  127.0 24.5 %collective-permute-start.28 = (bf16[3,192,768]{2,1,0:T(8,128)(2,1)S(1)}, bf16[3,192,768]{2,1,0:T(8,128)(2,1)S(1)}, u32[]{:S(2)}, u32[]{:S(2)}) collective-permute-start(bf16[3,192,768]{2,1,0:T(8,128)(2,1)S(1)} %pad_maximum_fusion.2.p6.refs_14_.refs_13_), channel_id=1, source_target_pairs={{0,18},{1,19},{2,16},{3,17},{16,2},{17,3},{18,0},{19,1},{4,22},{5,... | collective-permute-start | bytes 2654216 | tf_op jit(solution)/shard_map/ppermute | solution.py:86
  128.3 32.3 %collective-permute-start.26 = (bf16[3,192,768]{2,1,0:T(8,128)(2,1)S(1)}, bf16[3,192,768]{2,1,0:T(8,128)(2,1)S(1)}, u32[]{:S(2)}, u32[]{:S(2)}) collective-permute-start(bf16[3,192,768]{2,1,0:T(8,128)(2,1)S(1)} %pad_maximum_fusion.2.p6.refs_14_.refs_13_), channel_id=1, source_target_pairs={{0,1},{1,0},{2,3},{3,2},{4,5},{5,4},{6,7},{7,6},{8,9},{9,8},{10,11... | collective-permute-start | bytes 2654216 | tf_op jit(solution)/shard_map/ppermute | solution.py:36
  129.6 38.2 %collective-permute-start.27 = (bf16[3,192,768]{2,1,0:T(8,128)(2,1)}, bf16[3,192,768]{2,1,0:T(8,128)(2,1)S(1)}, u32[]{:S(2)}, u32[]{:S(2)}) collective-permute-start(bf16[3,192,768]{2,1,0:T(8,128)(2,1)} %pad_maximum_fusion.1.p5.refs_13_.refs_12_), channel_id=1, source_target_pairs={{0,18},{1,19},{2,16},{3,17},{16,2},{17,3},{18,0},{19,1},{4,22},{5,... | collective-permute-start | bytes 2654216 | tf_op jit(solution)/shard_map/ppermute | solution.py:86
  137.8 48.9 %collective-permute-start.29 = (bf16[3,192,768]{2,1,0:T(8,128)(2,1)}, bf16[3,192,768]{2,1,0:T(8,128)(2,1)S(1)}, u32[]{:S(2)}, u32[]{:S(2)}) collective-permute-start(bf16[3,192,768]{2,1,0:T(8,128)(2,1)} %collective-permute-done.25.p7.refs_15_.refs_14_), channel_id=1, source_target_pairs={{0,18},{1,19},{2,16},{3,17},{16,2},{17,3},{18,0},{19,1},{4,22},{5,... | collective-permute-start | bytes 2654216 | tf_op jit(solution)/shard_map/ppermute | solution.py:86
  151.5 35.2 %collective-permute-start.30 = (bf16[3,192,768]{2,1,0:T(8,128)(2,1)S(1)}, bf16[3,192,768]{2,1,0:T(8,128)(2,1)S(1)}, u32[]{:S(2)}, u32[]{:S(2)}) collective-permute-start(bf16[3,192,768]{2,1,0:T(8,128)(2,1)S(1)} %collective-permute-done.28.p10.refs_18_.refs_17_), channel_id=1, source_target_pairs={{0,1},{1,0},{2,3},{3,2},{4,5},{5,4},{6,7},{7,6},{8,9},{9,8},{10,11... | collective-permute-start | bytes 2654216 | tf_op jit(solution)/shard_map/ppermute | solution.py:36
  154.0 32.7 %collective-permute-start.23 = (bf16[512,768]{1,0:T(8,128)(2,1)S(1)}, bf16[512,768]{1,0:T(8,128)(2,1)S(1)}, u32[]{:S(2)}, u32[]{:S(2)}) collective-permute-start(bf16[512,768]{1,0:T(8,128)(2,1)S(1)} %get-tuple-element.172.own), channel_id=1, source_target_pairs={{0,16},{16,0},{1,17},{17,1},{2,18},{18,2},{3,19},{19,3},{4,20},{20... | collective-permute-start | bytes 2359304 | tf_op jit(solution)/shard_map/ppermute | solution.py:32
  275.3 32.8 %collective-permute-start.41 = (bf16[4,192,1536]{2,1,0:T(8,128)(2,1)}, bf16[4,192,1536]{2,1,0:T(8,128)(2,1)}, u32[]{:S(2)}, u32[]{:S(2)}) collective-permute-start(bf16[4,192,1536]{2,1,0:T(8,128)(2,1)} %get-tuple-element.242), channel_id=1, source_target_pairs={{0,18},{1,19},{2,16},{3,17},{4,22},{5,23},{6,20},{7,21},{8,26},{9,... | collective-permute-start | bytes 7077896 | tf_op jit(solution)/shard_map/ppermute | solution.py:48
  279.7 28.4 %collective-permute-start.42 = (bf16[2,192,1536]{2,1,0:T(8,128)(2,1)S(1)}, bf16[2,192,1536]{2,1,0:T(8,128)(2,1)S(1)}, u32[]{:S(2)}, u32[]{:S(2)}) collective-permute-start(bf16[2,192,1536]{2,1,0:T(8,128)(2,1)S(1)} %get-tuple-element.201), channel_id=1, source_target_pairs={{0,1},{1,0},{2,3},{3,2},{4,5},{5,4},{6,7},{7,6},{8,9},{9,8},{10,11... | collective-permute-start | bytes 3538952 | tf_op jit(solution)/shard_map/ppermute | solution.py:36
  293.3 23.0 %collective-permute-start.43 = (bf16[512,768]{1,0:T(8,128)(2,1)S(1)}, bf16[512,768]{1,0:T(8,128)(2,1)S(1)}, u32[]{:S(2)}, u32[]{:S(2)}) collective-permute-start(bf16[512,768]{1,0:T(8,128)(2,1)S(1)} %get-tuple-element.224.refs_1_), channel_id=1, source_target_pairs={{0,16},{16,0},{1,17},{17,1},{2,18},{18,2},{3,19},{19,3},{4,20},{20... | collective-permute-start | bytes 2359304 | tf_op jit(solution)/shard_map/ppermute | solution.py:32
  297.5 26.8 %collective-permute-start.44 = (bf16[4,208,768]{2,1,0:T(8,128)(2,1)S(1)}, bf16[4,208,768]{2,1,0:T(8,128)(2,1)}, u32[]{:S(2)}, u32[]{:S(2)}) collective-permute-start(bf16[4,208,768]{2,1,0:T(8,128)(2,1)S(1)} %get-tuple-element.257), channel_id=1, source_target_pairs={{0,18},{1,19},{2,16},{3,17},{4,22},{5,23},{6,20},{7,21},{8,26},{9,... | collective-permute-start | bytes 3833864 | tf_op jit(solution)/shard_map/ppermute | solution.py:48
  302.6 21.7 %collective-permute-start.45 = (bf16[2,208,768]{2,1,0:T(8,128)(2,1)S(1)}, bf16[2,208,768]{2,1,0:T(8,128)(2,1)S(1)}, u32[]{:S(2)}, u32[]{:S(2)}) collective-permute-start(bf16[2,208,768]{2,1,0:T(8,128)(2,1)S(1)} %get-tuple-element.218), channel_id=1, source_target_pairs={{0,1},{1,0},{2,3},{3,2},{4,5},{5,4},{6,7},{7,6},{8,9},{9,8},{10,11... | collective-permute-start | bytes 1916936 | tf_op jit(solution)/shard_map/ppermute | solution.py:36
  309.5 29.8 %collective-permute-start.47 = (bf16[2,192,1536]{2,1,0:T(8,128)(2,1)}, bf16[2,192,1536]{2,1,0:T(8,128)(2,1)}, u32[]{:S(2)}, u32[]{:S(2)}) collective-permute-start(bf16[2,192,1536]{2,1,0:T(8,128)(2,1)} %add_convert_fusion.6), channel_id=1, source_target_pairs={{0,18},{1,19},{2,16},{3,17},{4,22},{5,23},{6,20},{7,21},{8,26},{9,... | collective-permute-start | bytes 3538952 | tf_op jit(solution)/shard_map/ppermute | solution.py:48
  314.6 26.1 %collective-permute-start.46 = (bf16[2,192,1536]{2,1,0:T(8,128)(2,1)}, bf16[2,192,1536]{2,1,0:T(8,128)(2,1)}, u32[]{:S(2)}, u32[]{:S(2)}) collective-permute-start(bf16[2,192,1536]{2,1,0:T(8,128)(2,1)} %add_convert_fusion.7), channel_id=1, source_target_pairs={{16,17},{17,16},{18,19},{19,18},{20,21},{21,20},{22,23},{23,22},{2... | collective-permute-start | bytes 3538952 | tf_op jit(solution)/shard_map/ppermute | solution.py:42
  324.2 22.8 %collective-permute-start.48 = (bf16[512,768]{1,0:T(8,128)(2,1)S(1)}, bf16[512,768]{1,0:T(8,128)(2,1)S(1)}, u32[]{:S(2)}, u32[]{:S(2)}) collective-permute-start(bf16[512,768]{1,0:T(8,128)(2,1)S(1)} %get-tuple-element.233.own), channel_id=1, source_target_pairs={{0,16},{16,0},{1,17},{17,1},{2,18},{18,2},{3,19},{19,3},{4,20},{20... | collective-permute-start | bytes 2359304 | tf_op jit(solution)/shard_map/ppermute | solution.py:32
  326.2 35.5 %collective-permute-start.52 = (bf16[2,208,768]{2,1,0:T(8,128)(2,1)}, bf16[2,208,768]{2,1,0:T(8,128)(2,1)}, u32[]{:S(2)}, u32[]{:S(2)}) collective-permute-start(bf16[2,208,768]{2,1,0:T(8,128)(2,1)} %add_convert_fusion.14), channel_id=1, source_target_pairs={{0,18},{1,19},{2,16},{3,17},{4,22},{5,23},{6,20},{7,21},{8,26},{9,... | collective-permute-start | bytes 1916936 | tf_op jit(solution)/shard_map/ppermute | solution.py:48
  331.9 33.4 %collective-permute-start.51 = (bf16[2,208,768]{2,1,0:T(8,128)(2,1)}, bf16[2,208,768]{2,1,0:T(8,128)(2,1)}, u32[]{:S(2)}, u32[]{:S(2)}) collective-permute-start(bf16[2,208,768]{2,1,0:T(8,128)(2,1)} %add_convert_fusion.15), channel_id=1, source_target_pairs={{16,17},{17,16},{18,19},{19,18},{20,21},{21,20},{22,23},{23,22},{2... | collective-permute-start | bytes 1916936 | tf_op jit(solution)/shard_map/ppermute | solution.py:42
  339.3 31.2 %collective-permute-start.50 = (bf16[2,192,1536]{2,1,0:T(8,128)(2,1)S(1)}, bf16[2,192,1536]{2,1,0:T(8,128)(2,1)S(1)}, u32[]{:S(2)}, u32[]{:S(2)}) collective-permute-start(bf16[2,192,1536]{2,1,0:T(8,128)(2,1)S(1)} %get-tuple-element.240), channel_id=1, source_target_pairs={{0,1},{1,0},{2,3},{3,2},{4,5},{5,4},{6,7},{7,6},{8,9},{9,8},{10,11... | collective-permute-start | bytes 3538952 | tf_op jit(solution)/shard_map/ppermute | solution.py:36
  340.7 30.6 %collective-permute-start.49 = (bf16[4,192,1536]{2,1,0:T(8,128)(2,1)}, bf16[4,192,1536]{2,1,0:T(8,128)(2,1)}, u32[]{:S(2)}, u32[]{:S(2)}) collective-permute-start(bf16[4,192,1536]{2,1,0:T(8,128)(2,1)} %get-tuple-element.279), channel_id=1, source_target_pairs={{16,2},{17,3},{18,0},{19,1},{20,6},{21,7},{22,4},{23,5},{24,10},{2... | collective-permute-start | bytes 7077896 | tf_op jit(solution)/shard_map/ppermute | solution.py:48
  347.1 38.1 %collective-permute-start.58 = (bf16[2,192,1536]{2,1,0:T(8,128)(2,1)}, bf16[2,192,1536]{2,1,0:T(8,128)(2,1)}, u32[]{:S(2)}, u32[]{:S(2)}) collective-permute-start(bf16[2,192,1536]{2,1,0:T(8,128)(2,1)} %add_convert_fusion.4), channel_id=1, source_target_pairs={{16,24},{20,28},{24,16},{28,20},{17,25},{21,29},{25,17},{29,21},{1... | collective-permute-start | bytes 3538952 | tf_op jit(solution)/shard_map/ppermute | solution.py:42
  361.7 17.6 %collective-permute-start.68 = (bf16[512,768]{1,0:T(8,128)(2,1)S(1)}, bf16[512,768]{1,0:T(8,128)(2,1)S(1)}, u32[]{:S(2)}, u32[]{:S(2)}) collective-permute-start(bf16[512,768]{1,0:T(8,128)(2,1)S(1)} %get-tuple-element.256), channel_id=1, source_target_pairs={{0,16},{16,0},{1,17},{17,1},{2,18},{18,2},{3,19},{19,3},{4,20},{20... | collective-permute-start | bytes 2359304 | tf_op jit(solution)/shard_map/ppermute | solution.py:32
  367.5 37.8 %collective-permute-start.55 = (bf16[2,208,768]{2,1,0:T(8,128)(2,1)}, bf16[2,208,768]{2,1,0:T(8,128)(2,1)}, u32[]{:S(2)}, u32[]{:S(2)}) collective-permute-start(bf16[2,208,768]{2,1,0:T(8,128)(2,1)} %add_convert_fusion.12), channel_id=1, source_target_pairs={{16,24},{20,28},{24,16},{28,20},{17,25},{21,29},{25,17},{29,21},{1... | collective-permute-start | bytes 1916936 | tf_op jit(solution)/shard_map/ppermute | solution.py:42
  372.6 18.0 %collective-permute-start.57 = (bf16[2,192,1536]{2,1,0:T(8,128)(2,1)}, bf16[2,192,1536]{2,1,0:T(8,128)(2,1)}, u32[]{:S(2)}, u32[]{:S(2)}) collective-permute-start(bf16[2,192,1536]{2,1,0:T(8,128)(2,1)} %add_convert_fusion.2), channel_id=1, source_target_pairs={{16,2},{17,3},{18,0},{19,1},{20,6},{21,7},{22,4},{23,5},{24,10},{2... | collective-permute-start | bytes 3538952 | tf_op jit(solution)/shard_map/ppermute | solution.py:48
  376.7 24.8 %collective-permute-start.56 = (bf16[2,192,1536]{2,1,0:T(8,128)(2,1)}, bf16[2,192,1536]{2,1,0:T(8,128)(2,1)}, u32[]{:S(2)}, u32[]{:S(2)}) collective-permute-start(bf16[2,192,1536]{2,1,0:T(8,128)(2,1)} %add_convert_fusion.3), channel_id=1, source_target_pairs={{0,1},{1,0},{2,3},{3,2},{4,5},{5,4},{6,7},{7,6},{8,9},{9,8},{10,11... | collective-permute-start | bytes 3538952 | tf_op jit(solution)/shard_map/ppermute | solution.py:42
  383.6 33.2 %collective-permute-start.54 = (bf16[2,208,768]{2,1,0:T(8,128)(2,1)S(1)}, bf16[2,208,768]{2,1,0:T(8,128)(2,1)S(1)}, u32[]{:S(2)}, u32[]{:S(2)}) collective-permute-start(bf16[2,208,768]{2,1,0:T(8,128)(2,1)S(1)} %get-tuple-element.276), channel_id=1, source_target_pairs={{0,1},{1,0},{2,3},{3,2},{4,5},{5,4},{6,7},{7,6},{8,9},{9,8},{10,11... | collective-permute-start | bytes 1916936 | tf_op jit(solution)/shard_map/ppermute | solution.py:36
  385.2 31.7 %collective-permute-start.53 = (bf16[4,208,768]{2,1,0:T(8,128)(2,1)S(1)}, bf16[4,208,768]{2,1,0:T(8,128)(2,1)S(1)}, u32[]{:S(2)}, u32[]{:S(2)}) collective-permute-start(bf16[4,208,768]{2,1,0:T(8,128)(2,1)S(1)} %get-tuple-element.291), channel_id=1, source_target_pairs={{16,2},{17,3},{18,0},{19,1},{20,6},{21,7},{22,4},{23,5},{24,10},{2... | collective-permute-start | bytes 3833864 | tf_op jit(solution)/shard_map/ppermute | solution.py:48
  405.4 16.8 %collective-permute-start.59 = (bf16[192,1536]{1,0:T(8,128)(2,1)S(1)}, bf16[192,1536]{1,0:T(8,128)(2,1)S(1)}, u32[]{:S(2)}, u32[]{:S(2)}) collective-permute-start(bf16[192,1536]{1,0:T(8,128)(2,1)S(1)} %get-tuple-element.363), channel_id=1, source_target_pairs={{0,4},{4,0},{8,12},{12,8},{1,5},{5,1},{9,13},{13,9},{2,6},{6,2},{1... | collective-permute-start | bytes 1769480 | tf_op jit(solution)/shard_map/ppermute | solution.py:42
  407.4 25.4 %collective-permute-start.66 = (bf16[192,1536]{1,0:T(8,128)(2,1)S(1)}, bf16[192,1536]{1,0:T(8,128)(2,1)S(1)}, u32[]{:S(2)}, u32[]{:S(2)}) collective-permute-start(bf16[192,1536]{1,0:T(8,128)(2,1)S(1)} %get-tuple-element.361), channel_id=1, source_target_pairs={{0,8},{4,12},{8,0},{12,4},{1,9},{5,13},{9,1},{13,5},{2,10},{6,14},... | collective-permute-start | bytes 1769480 | tf_op jit(solution)/shard_map/ppermute | solution.py:42
  411.5 21.3 %collective-permute-start.67 = (bf16[192,1536]{1,0:T(8,128)(2,1)S(1)}, bf16[192,1536]{1,0:T(8,128)(2,1)S(1)}, u32[]{:S(2)}, u32[]{:S(2)}) collective-permute-start(bf16[192,1536]{1,0:T(8,128)(2,1)S(1)} %get-tuple-element.360), channel_id=1, source_target_pairs={{0,12},{4,8},{8,4},{12,0},{1,13},{5,9},{9,5},{13,1},{2,14},{6,10},... | collective-permute-start | bytes 1769480 | tf_op jit(solution)/shard_map/ppermute | solution.py:42
  432.8 17.9 %collective-permute-start.70 = (bf16[2,128,768]{2,1,0:T(8,128)(2,1)S(1)}, bf16[2,128,768]{2,1,0:T(8,128)(2,1)S(1)}, u32[]{:S(2)}, u32[]{:S(2)}) collective-permute-start(bf16[2,128,768]{2,1,0:T(8,128)(2,1)S(1)} %pad_maximum_fusion.8), channel_id=1, source_target_pairs={{0,2},{1,3},{2,0},{3,1},{4,6},{5,7},{6,4},{7,5},{8,10},{9,11},{10,... | collective-permute-start | bytes 1179656 | tf_op jit(solution)/shard_map/ppermute | solution.py:36
  437.8 23.2 %collective-permute-start.65 = (bf16[208,2304]{1,0:T(8,128)(2,1)S(1)}, bf16[208,2304]{1,0:T(8,128)(2,1)S(1)}, u32[]{:S(2)}, u32[]{:S(2)}) collective-permute-start(bf16[208,2304]{1,0:T(8,128)(2,1)S(1)} %fusion.1), channel_id=1, source_target_pairs={{16,20},{20,16},{24,28},{28,24},{17,21},{21,17},{25,29},{29,25},{1... | collective-permute-start | bytes 2875400 | tf_op jit(solution)/shard_map/ppermute | solution.py:42
  438.6 19.1 %collective-permute-start.63 = (bf16[208,768]{1,0:T(8,128)(2,1)S(1)}, bf16[208,768]{1,0:T(8,128)(2,1)S(1)}, u32[]{:S(2)}, u32[]{:S(2)}) collective-permute-start(bf16[208,768]{1,0:T(8,128)(2,1)S(1)} %get-tuple-element.382), channel_id=1, source_target_pairs={{0,8},{4,12},{8,0},{12,4},{1,9},{5,13},{9,1},{13,5},{2,10},{6,14},... | collective-permute-start | bytes 958472 | tf_op jit(solution)/shard_map/ppermute | solution.py:42
  (111 other events, 1771.6 us)

commit v2 on v1

--- a/solution.py
+++ b/solution.py
@@ -439,7 +439,10 @@
     length, width = mid.shape
     n_cls = cls_pos.shape[0]
 
-    def body(cls, mid, own, other, gain, shift, tok, y_out, xhat_out, scale_out, cls_out):
+    def body(cls, mid_from, own, other, gain, shift, tok, y_out, xhat_out, scale_out, cls_out, mid, sem):
+        get_mid = pltpu.make_async_copy(mid_from, mid, sem.at[0])
+        get_mid.start()
+        get_mid.wait()
         for rows in chunks(length):
             z = mid[rows, :] + (own[rows, :].astype(F32) + other[rows, :].astype(F32)) + shift[2:3, :]
             xhat, scale = norm_rows(z)
@@ -458,8 +461,9 @@
             sds((length, width), BF16), sds((length, width), BF16), sds((length, 1), F32),
             sds((n_cls, width), BF16),
         ],
-        in_specs=[SM] + [VM] * 6,
+        in_specs=[SM, ANY] + [VM] * 5,
         out_specs=[VM] * 4,
+        scratch_shapes=[pltpu.VMEM((length, width), F32), pltpu.SemaphoreType.DMA((1,))],
         compiler_params=params(),
         cost_estimate=takes(2),
         name="last_norm",
@@ -721,7 +725,13 @@
     n_q, width = queries.shape
     n_p = slots.shape[0]
 
-    def body(own, perm, slots, queries, pos, loss_out, d_out):
+    def body(own, perm_from, slots, queries_from, pos, loss_out, d_out, perm, queries, sems):
+        get_perm = pltpu.make_async_copy(perm_from, perm, sems.at[0])
+        get_queries = pltpu.make_async_copy(queries_from, queries, sems.at[1])
+        get_perm.start()
+        get_queries.start()
+        get_perm.wait()
+        get_queries.wait()
         passages = nn(perm[...], slots[...]).astype(BF16)
         logits = nt(queries[...], passages)
         top = jnp.max(logits, -1, keepdims=True)
@@ -742,8 +752,11 @@
     return pl.pallas_call(
         body,
         out_shape=[sds((1, 1), F32), sds((n_own, width), F32)],
-        in_specs=[SM] + [VM] * 4,
+        in_specs=[SM, ANY, VM, ANY, VM],
         out_specs=[VM] * 2,
+        scratch_shapes=[
+            pltpu.VMEM(perm.shape, BF16), pltpu.VMEM(queries.shape, BF16), pltpu.SemaphoreType.DMA((2,)),
+        ],
         compiler_params=params(),
         cost_estimate=takes(1),
         name="contrast",
@@ -795,8 +808,8 @@
     else:
         pack = lax.all_gather(pack, "dp", axis=0, tiled=True)
         own, other_rows = pack[: width // 2], pack[width // 2 :][None]
+    near0, far0 = gather_own(after(own, message))
     message = spread_tensor(message)
-    near0, far0 = gather_own(after(own, message))
     both0 = gather_own_both(near0, far0)
     owns = [own, near0, far0, *both0]
 

time: 474 us -> 473 us (level)
  starting transfers between devices: 131 us -> 113 us
  waiting for transfers between devices: 139 us -> 156 us
    ppermute x33, waiting for transfers between devices: 60.8 us -> 78.5 us  [hop(): lax.ppermute(block, axis, [(i, i ^ flip) for i in range(lax.axis_size(axi...]
    ppermute x33, starting transfers between devices: 58.2 us -> 47.9 us  [hop(): lax.ppermute(block, axis, [(i, i ^ flip) for i in range(lax.axis_size(axi...]
    ppermute x10, starting transfers between devices: 12.7 us -> 5.35 us  [swap_cores(): return lax.ppermute(block, 'section', [(0, 1), (1, 0)])]
where the time goes in v2:
time: 473 us; the launch traced here: 466 us
  waiting for transfers between devices  156 us (33%)
  starting transfers between devices  113 us (24%)
  Pallas kernels  104 us (22%)
  other arithmetic  47.5 us (10%)
  local copies, waits for them, and re-layouts  43 us (9%)
    ppermute x33, waiting for transfers between devices, hop(): lax.ppermute(block, axis, [(i, i ^ flip) for i in range(lax.axis_size(axi...  78.5 us
    ppermute x33, starting transfers between devices, hop(): lax.ppermute(block, axis, [(i, i ^ flip) for i in range(lax.axis_size(axi...  47.9 us
    ppermute x13, starting transfers between devices, core_hop(): return lax.ppermute(block, ('section', axis), route)  36 us
    ppermute x13, waiting for transfers between devices, core_hop(): return lax.ppermute(block, ('section', axis), route)  34.1 us
    ppermute x7, waiting for transfers between devices, cross_all(): return lax.ppermute(block, ('section', 'tensor'), route)  33.8 us
    convert_element_type x18, other arithmetic, add_low(): return total.astype(BF16)  26.9 us
    pallas_call x2, Pallas kernels, attn_backward(): pl.pallas_call(body, out_shape=[sds((length, width), BF16), sds((length,...  25.8 us
    pallas_call x2, Pallas kernels, attn_forward(): pl.pallas_call(body, out_shape=outs, in_specs=specs, out_specs=[VM] * len...  25.2 us
  transfers between devices with their start and end apart: 71, of which 29 were waited for; matrix products, arithmetic and copies ran while one was open for 13% of the time, Pallas kernels for 14%

profile of v2, /device:TPU:0, one launch (start us, length us, event | category | flops | bytes accessed | tf_op | source)
XLA Modules:
  0.0 466.3 jit_solution(16778170838466579557)
XLA Ops:
  5.2 3.1 collective-permute-start
  8.3 2.6 collective-permute-start.1
  28.6 3.5 collective-permute-start.8
  33.9 9.7 %collective-permute-done.7 = bf16[192,768]{1,0:T(8,128)(2,1)S(1)} collective-permute-done((bf16[192,768]{1,0:T(8,128)(2,1)}, bf16[192,768]{1,0:T(8,128)(2,1)S(1)}, u32[]{:S(2)}, u32[]{:S(2)}) %collective-permute-start.7) | collective-permute-done | bytes 294944 | tf_op jit(solution)/shard_map/ppermute | solution.py:36
  43.6 9.3 %collective-permute-done.8 = bf16[192,768]{1,0:T(8,128)(2,1)S(1)} collective-permute-done((bf16[192,768]{1,0:T(8,128)(2,1)}, bf16[192,768]{1,0:T(8,128)(2,1)S(1)}, u32[]{:S(2)}, u32[]{:S(2)}) %collective-permute-start.8) | collective-permute-done | bytes 294944 | tf_op jit(solution)/shard_map/ppermute | solution.py:36
  56.1 6.6 %collective-permute-start.19 = (bf16[192,1536]{1,0:T(8,128)(2,1)}, bf16[192,1536]{1,0:T(8,128)(2,1)S(1)}, u32[]{:S(2)}, u32[]{:S(2)}) collective-permute-start(bf16[192,1536]{1,0:T(8,128)(2,1)} %pad_maximum_fusion.4), channel_id=1, source_target_pairs={{0,4},{4,0},{8,12},{12,8},{1,5},{5,1},{9,13},{13,9},{2,6},{6,2},{1... | collective-permute-start | bytes 1769480 | tf_op jit(solution)/shard_map/ppermute | solution.py:36
  67.7 8.5 %collective-permute-done.12.refs_8_.refs_9_.refs_12_.refs_13_.p7.p8 = bf16[3,192,768]{2,1,0:T(8,128)(2,1)} collective-permute-done((bf16[3,192,768]{2,1,0:T(8,128)(2,1)}, bf16[3,192,768]{2,1,0:T(8,128)(2,1)}, u32[]{:S(2)}, u32[]{:S(2)}) %collective-permute-start.12) | collective-permute-done | bytes 884768 | tf_op jit(solution)/shard_map/ppermute | solution.py:36
  79.6 7.2 %collective-permute-done.16.refs_4_.p3.refs_8_.refs_11_.refs_10_ = bf16[192,1152]{1,0:T(8,128)(2,1)S(1)} collective-permute-done((bf16[192,1152]{1,0:T(8,128)(2,1)}, bf16[192,1152]{1,0:T(8,128)(2,1)S(1)}, u32[]{:S(2)}, u32[]{:S(2)}) %collective-permute-start.16) | collective-permute-done | bytes 442400 | tf_op jit(solution)/shard_map/ppermute | solution.py:86
  90.7 14.3 %collective-permute-done.20 = bf16[192,1536]{1,0:T(8,128)(2,1)} collective-permute-done((bf16[192,1536]{1,0:T(8,128)(2,1)}, bf16[192,1536]{1,0:T(8,128)(2,1)}, u32[]{:S(2)}, u32[]{:S(2)}) %collective-permute-start.20) | collective-permute-done | bytes 589856 | tf_op jit(solution)/shard_map/ppermute | solution.py:36
  114.3 5.1 %collective-permute-done.21.refs_12_.refs_16_.p11 = bf16[3,192,384]{2,1,0:T(8,128)(2,1)S(1)} collective-permute-done((bf16[3,192,384]{2,1,0:T(8,128)(2,1)}, bf16[3,192,384]{2,1,0:T(8,128)(2,1)S(1)}, u32[]{:S(2)}, u32[]{:S(2)}) %collective-permute-start.21) | collective-permute-done | bytes 442400 | tf_op jit(solution)/shard_map/ppermute | solution.py:86
  119.5 3.1 collective-permute-done.22.refs_13_.refs_17_.p12
  133.2 16.0 %collective-permute-done.25.p7.refs_15_.refs_14_ = bf16[3,192,768]{2,1,0:T(8,128)(2,1)} collective-permute-done((bf16[3,192,768]{2,1,0:T(8,128)(2,1)}, bf16[3,192,768]{2,1,0:T(8,128)(2,1)}, u32[]{:S(2)}, u32[]{:S(2)}) %collective-permute-start.25) | collective-permute-done | bytes 884768 | tf_op jit(solution)/shard_map/ppermute | solution.py:36
  150.9 12.1 %attn_forward.2 = (bf16[512,768]{1,0:T(8,128)(2,1)S(1)}, bf16[512,1152]{1,0:T(8,128)(2,1)}, bf16[6,512,512]{2,1,0:T(8,128)(2,1)}, bf16[512,384]{1,0:T(8,128)(2,1)S(1)}) custom-call(s32[5]{0:T(128)S(1)} %get-tuple-element.426.meta, bf16[512,768]{1,0:T(8,128)(2,1)S(1)} %get-tuple-element.166.refs_0_.x, ...), custom_call_target="tpu_custom_call" | custom-call | flops 14300000256 | tf_op jit(solution)/shard_map/attn_forward/pallas_call | solution.py:382
  164.7 3.2 collective-permute-done.26.p8.refs_16_.refs_15_
  167.9 2.7 collective-permute-done.27.p9.refs_17_.refs_16_
  170.7 18.7 %collective-permute-done.29.p11.refs_19_.refs_18_ = bf16[3,192,768]{2,1,0:T(8,128)(2,1)S(1)} collective-permute-done((bf16[3,192,768]{2,1,0:T(8,128)(2,1)}, bf16[3,192,768]{2,1,0:T(8,128)(2,1)S(1)}, u32[]{:S(2)}, u32[]{:S(2)}) %collective-permute-start.29) | collective-permute-done | bytes 884768 | tf_op jit(solution)/shard_map/ppermute | solution.py:86
  191.2 8.9 %ffn_forward.2 = (bf16[512,768]{1,0:T(8,128)(2,1)S(1)}, f32[512,768]{1,0:T(8,128)}, bf16[512,768]{1,0:T(8,128)(2,1)S(1)}, f32[512,1]{1,0:T(8,128)S(1)}, bf16[512...) custom-call(s32[5]{0:T(128)S(1)} %get-tuple-element.426.meta, bf16[512,768]{1,0:T(8,128)(2,1)S(1)} %get-tuple-element.166.refs_0_.x, ...), custom_call_target="tpu_custom_call" | custom-call | flops 9900000256 | tf_op jit(solution)/shard_map/ffn_forward/pallas_call | solution.py:420
  205.1 13.2 %attn_forward.3 = (bf16[512,768]{1,0:T(8,128)(2,1)S(1)}, bf16[512,1152]{1,0:T(8,128)(2,1)}, bf16[6,512,512]{2,1,0:T(8,128)(2,1)}, bf16[512,384]{1,0:T(8,128)(2,1...) custom-call(s32[5]{0:T(128)S(1)} %get-tuple-element.427.meta, ...), custom_call_target="tpu_custom_call" | custom-call | flops 14300000256 | tf_op jit(solution)/shard_map/attn_forward/pallas_call | solution.py:382
  221.8 8.8 %ffn_forward.3 = (bf16[512,768]{1,0:T(8,128)(2,1)S(1)}, f32[512,768]{1,0:T(8,128)}, bf16[512,768]{1,0:T(8,128)(2,1)S(1)}, f32[512,1]{1,0:T(8,128)S(1)}, bf16[512...) custom-call(s32[5]{0:T(128)S(1)} %get-tuple-element.427.meta, bf16[512,768]{1,0:T(8,128)(2,1)S(1)} %get-tuple-element.183.x, ...), custom_call_target="tpu_custom_call" | custom-call | flops 9900000256 | tf_op jit(solution)/shard_map/ffn_forward/pallas_call | solution.py:420
  239.2 2.9 collective-permute-start.35
  244.5 3.1 collective-permute-done.36
  262.5 7.1 %ffn_backward.2 = (bf16[512,768]{1,0:T(8,128)(2,1)S(1)}, f32[512,768]{1,0:T(8,128)}, bf16[512,768]{1,0:T(8,128)(2,1)S(1)}, bf16[512,1536]{1,0:T(8,128)(2,1)}, f3...) custom-call(s32[5]{0:T(128)S(1)} %copy-done.17, s32[4]{0:T(128)S(1)} %copy-done.15, ...), custom_call_target="tpu_custom_call" | custom-call | flops 9900000256 | tf_op jit(solution)/shard_map/ffn_backward/pallas_call | solution.py:532
  269.7 6.0 %ffn_grads.2 = (bf16[4,192,1536]{2,1,0:T(8,128)(2,1)}, bf16[2,192,1536]{2,1,0:T(8,128)(2,1)S(1)}, bf16[2,192,1536]{2,1,0:T(8,128)(2,1)S(1)}) custom-call(s32[5]{0:T(128)S(1)} %copy-done.17, f32[512,768]{1,0:T(8,128)S(1)} %copy-done.31, bf16[512,1536]{1,0:T(8,128)(2,1)} %get-tuple-element.198.d_pre, bf16[512,768]{1,0:T(8,128)(2,1)S(1)} %get-tuple-element.199.d_ffn, ...), custom_call_target="tpu_custom_call" | custom-call | flops 7699999744 | tf_op jit(solution)/shard_map/ffn_grads/pallas_call | solution.py:583
  275.7 3.9 collective-permute-start.41
  280.3 12.9 %attn_backward.2 = (bf16[512,768]{1,0:T(8,128)(2,1)S(1)}, f32[512,768]{1,0:T(8,128)}, bf16[512,768]{1,0:T(8,128)(2,1)S(1)}, bf16[512,1152]{1,0:T(8,128)(2,1)}, f...) custom-call(s32[5]{0:T(128)S(1)} %copy-done.17, f32[512,768]{1,0:T(8,128)} %get-tuple-element.202.d_second, ...), custom_call_target="tpu_custom_call" | custom-call | flops 16499999744 | tf_op jit(solution)/shard_map/attn_backward/pallas_call | solution.py:650
  294.6 2.9 attn_grads.2
  297.5 4.5 collective-permute-start.44
  303.6 5.0 %collective-permute-done.42 = bf16[2,192,1536]{2,1,0:T(8,128)(2,1)S(1)} collective-permute-done((bf16[2,192,1536]{2,1,0:T(8,128)(2,1)S(1)}, bf16[2,192,1536]{2,1,0:T(8,128)(2,1)S(1)}, u32[]{:S(2)}, u32[]{:S(2)}) %collective-permute-start.42) | collective-permute-done | bytes 1179680 | tf_op jit(solution)/shard_map/ppermute | solution.py:36
  312.5 2.6 add_convert_fusion.7
  316.8 7.9 %ffn_backward.3 = (bf16[512,768]{1,0:T(8,128)(2,1)S(1)}, f32[512,768]{1,0:T(8,128)}, bf16[512,768]{1,0:T(8,128)(2,1)S(1)}, bf16[512,1536]{1,0:T(8,128)(2,1)}, f3...) custom-call(s32[5]{0:T(128)S(1)} %copy-done.13, f32[512,768]{1,0:T(8,128)} %get-tuple-element.223.refs_0_, ...), custom_call_target="tpu_custom_call" | custom-call | flops 9900000256 | tf_op jit(solution)/shard_map/ffn_backward/pallas_call | solution.py:532
  326.7 3.5 collective-permute-start.52
  333.8 5.8 %ffn_grads.3 = (bf16[4,192,1536]{2,1,0:T(8,128)(2,1)}, bf16[2,192,1536]{2,1,0:T(8,128)(2,1)S(1)}, bf16[2,192,1536]{2,1,0:T(8,128)(2,1)S(1)}) custom-call(s32[5]{0:T(128)S(1)} %copy-done.13, f32[512,768]{1,0:T(8,128)S(1)} %copy-done.40, bf16[512,1536]{1,0:T(8,128)(2,1)} %get-tuple-element.229.d_pre, bf16[512,768]{1,0:T(8,128)(2,1)S(1)} %get-tuple-element.238.d_ffn, ...), custom_call_target="tpu_custom_call" | custom-call | flops 7699999744 | tf_op jit(solution)/shard_map/ffn_grads/pallas_call | solution.py:583
  341.5 2.7 add_convert_fusion.4
  348.1 12.9 %attn_backward.3 = (bf16[512,768]{1,0:T(8,128)(2,1)S(1)}, f32[512,768]{1,0:T(8,128)}, bf16[512,768]{1,0:T(8,128)(2,1)S(1)}, bf16[512,1152]{1,0:T(8,128)(2,1)}, f...) custom-call(s32[5]{0:T(128)S(1)} %copy-done.13, f32[512,768]{1,0:T(8,128)} %get-tuple-element.248.d_second, ...), custom_call_target="tpu_custom_call" | custom-call | flops 16499999744 | tf_op jit(solution)/shard_map/attn_backward/pallas_call | solution.py:650
  361.1 3.5 collective-permute-start.68
  373.5 2.6 add_convert_fusion.3
  376.1 3.7 collective-permute-start.56
  381.2 2.9 attn_grads.3
  387.4 2.7 collective-permute-done.57
  390.1 10.6 %collective-permute-done.56 = bf16[2,192,1536]{2,1,0:T(8,128)(2,1)} collective-permute-done((bf16[2,192,1536]{2,1,0:T(8,128)(2,1)}, bf16[2,192,1536]{2,1,0:T(8,128)(2,1)}, u32[]{:S(2)}, u32[]{:S(2)}) %collective-permute-start.56) | collective-permute-done | bytes 1179680 | tf_op jit(solution)/shard_map/ppermute | solution.py:42
  404.5 3.6 collective-permute-start.59
  410.8 4.0 collective-permute-start.67
  416.0 3.8 collective-permute-done.59
  425.8 7.8 %collective-permute-done.66 = bf16[192,1536]{1,0:T(8,128)(2,1)S(1)} collective-permute-done((bf16[192,1536]{1,0:T(8,128)(2,1)S(1)}, bf16[192,1536]{1,0:T(8,128)(2,1)S(1)}, u32[]{:S(2)}, u32[]{:S(2)}) %collective-permute-start.66) | collective-permute-done | bytes 589856 | tf_op jit(solution)/shard_map/ppermute | solution.py:42
  437.2 7.8 %collective-permute-start.63 = (bf16[208,768]{1,0:T(8,128)(2,1)S(1)}, bf16[208,768]{1,0:T(8,128)(2,1)S(1)}, u32[]{:S(2)}, u32[]{:S(2)}) collective-permute-start(bf16[208,768]{1,0:T(8,128)(2,1)S(1)} %get-tuple-element.382), channel_id=1, source_target_pairs={{0,8},{4,12},{8,0},{12,4},{1,9},{5,13},{9,1},{13,5},{2,10},{6,14},... | collective-permute-start | bytes 958472 | tf_op jit(solution)/shard_map/ppermute | solution.py:42
  444.9 3.2 collective-permute-start.64
  450.3 6.6 %collective-permute-done.63 = bf16[208,768]{1,0:T(8,128)(2,1)S(1)} collective-permute-done((bf16[208,768]{1,0:T(8,128)(2,1)S(1)}, bf16[208,768]{1,0:T(8,128)(2,1)S(1)}, u32[]{:S(2)}, u32[]{:S(2)}) %collective-permute-start.63) | collective-permute-done | bytes 319520 | tf_op jit(solution)/shard_map/ppermute | solution.py:42
  456.9 3.3 collective-permute-done.62
  (434 shorter events, 157.5 us)
Async XLA Ops:
  21.6 31.2 %collective-permute-start.10 = (bf16[192,2304]{1,0:T(8,128)(2,1)S(1)}, bf16[192,2304]{1,0:T(8,128)(2,1)S(1)}, u32[]{:S(2)}, u32[]{:S(2)}) collective-permute-start(bf16[192,2304]{1,0:T(8,128)(2,1)S(1)} %concatenate.43.refs_1_.p0.refs_5_.refs_8_.refs_7_), channel_id=1, source_target_pairs={{0,1},{1,0},{2,3},{3,2},{4,5},{5,4},{6,7},{7,6},{8,9},{9,8},{10,11... | collective-permute-start | bytes 2654216 | tf_op jit(solution)/shard_map/ppermute | solution.py:36
  23.4 29.4 %collective-permute-start.11 = (bf16[192,2304]{1,0:T(8,128)(2,1)S(1)}, bf16[192,2304]{1,0:T(8,128)(2,1)}, u32[]{:S(2)}, u32[]{:S(2)}) collective-permute-start(bf16[192,2304]{1,0:T(8,128)(2,1)S(1)} %concatenate.43.refs_1_.p0.refs_5_.refs_8_.refs_7_), channel_id=1, source_target_pairs={{0,18},{1,19},{2,16},{3,17},{16,2},{17,3},{18,0},{19,1},{4,22},{5,... | collective-permute-start | bytes 2654216 | tf_op jit(solution)/shard_map/ppermute | solution.py:86
  28.0 15.6 %collective-permute-start.7 = (bf16[192,768]{1,0:T(8,128)(2,1)}, bf16[192,768]{1,0:T(8,128)(2,1)S(1)}, u32[]{:S(2)}, u32[]{:S(2)}) collective-permute-start(bf16[192,768]{1,0:T(8,128)(2,1)} %pad_maximum_fusion.9), channel_id=1, source_target_pairs={{0,4},{4,0},{8,12},{12,8},{1,5},{5,1},{9,13},{13,9},{2,6},{6,2},{1... | collective-permute-start | bytes 884744 | tf_op jit(solution)/shard_map/ppermute | solution.py:36
  28.6 24.2 %collective-permute-start.8 = (bf16[192,768]{1,0:T(8,128)(2,1)}, bf16[192,768]{1,0:T(8,128)(2,1)S(1)}, u32[]{:S(2)}, u32[]{:S(2)}) collective-permute-start(bf16[192,768]{1,0:T(8,128)(2,1)} %pad_maximum_fusion.9), channel_id=1, source_target_pairs={{0,8},{4,12},{8,0},{12,4},{1,9},{5,13},{9,1},{13,5},{2,10},{6,14},... | collective-permute-start | bytes 884744 | tf_op jit(solution)/shard_map/ppermute | solution.py:36
  32.9 19.9 %collective-permute-start.9 = (bf16[192,768]{1,0:T(8,128)(2,1)}, bf16[192,768]{1,0:T(8,128)(2,1)}, u32[]{:S(2)}, u32[]{:S(2)}) collective-permute-start(bf16[192,768]{1,0:T(8,128)(2,1)} %pad_maximum_fusion.9), channel_id=1, source_target_pairs={{0,12},{4,8},{8,4},{12,0},{1,13},{5,9},{9,5},{13,1},{2,14},{6,10},... | collective-permute-start | bytes 884744 | tf_op jit(solution)/shard_map/ppermute | solution.py:36
  55.0 21.1 %collective-permute-start.12 = (bf16[3,192,768]{2,1,0:T(8,128)(2,1)}, bf16[3,192,768]{2,1,0:T(8,128)(2,1)}, u32[]{:S(2)}, u32[]{:S(2)}) collective-permute-start(bf16[3,192,768]{2,1,0:T(8,128)(2,1)} %pad_maximum_fusion.refs_6_.refs_7_.refs_10_.refs_11_.p5.p6), channel_id=1, source_target_pairs={{0,1},{1,0},{2,3},{3,2},{4,5},{5,4},{6,7},{7,6},{8,9},{9,8},{10,11... | collective-permute-start | bytes 2654216 | tf_op jit(solution)/shard_map/ppermute | solution.py:36
  55.9 49.1 %collective-permute-start.18 = (bf16[3,192,768]{2,1,0:T(8,128)(2,1)}, bf16[3,192,768]{2,1,0:T(8,128)(2,1)}, u32[]{:S(2)}, u32[]{:S(2)}) collective-permute-start(bf16[3,192,768]{2,1,0:T(8,128)(2,1)} %pad_maximum_fusion.refs_6_.refs_7_.refs_10_.refs_11_.p5.p6), channel_id=1, source_target_pairs={{0,18},{1,19},{2,16},{3,17},{16,2},{17,3},{18,0},{19,1},{4,22},{5,... | collective-permute-start | bytes 2654216 | tf_op jit(solution)/shard_map/ppermute | solution.py:86
  56.1 34.7 %collective-permute-start.19 = (bf16[192,1536]{1,0:T(8,128)(2,1)}, bf16[192,1536]{1,0:T(8,128)(2,1)S(1)}, u32[]{:S(2)}, u32[]{:S(2)}) collective-permute-start(bf16[192,1536]{1,0:T(8,128)(2,1)} %pad_maximum_fusion.4), channel_id=1, source_target_pairs={{0,4},{4,0},{8,12},{12,8},{1,5},{5,1},{9,13},{13,9},{2,6},{6,2},{1... | collective-permute-start | bytes 1769480 | tf_op jit(solution)/shard_map/ppermute | solution.py:36
  62.7 42.3 %collective-permute-start.20 = (bf16[192,1536]{1,0:T(8,128)(2,1)}, bf16[192,1536]{1,0:T(8,128)(2,1)}, u32[]{:S(2)}, u32[]{:S(2)}) collective-permute-start(bf16[192,1536]{1,0:T(8,128)(2,1)} %pad_maximum_fusion.4), channel_id=1, source_target_pairs={{0,8},{4,12},{8,0},{12,4},{1,9},{5,13},{9,1},{13,5},{2,10},{6,14},... | collective-permute-start | bytes 1769480 | tf_op jit(solution)/shard_map/ppermute | solution.py:36
  64.4 22.3 %collective-permute-start.16 = (bf16[192,1152]{1,0:T(8,128)(2,1)}, bf16[192,1152]{1,0:T(8,128)(2,1)S(1)}, u32[]{:S(2)}, u32[]{:S(2)}) collective-permute-start(bf16[192,1152]{1,0:T(8,128)(2,1)} %slice.434), channel_id=1, source_target_pairs={{0,18},{1,19},{2,16},{3,17},{16,2},{17,3},{18,0},{19,1},{4,22},{5,... | collective-permute-start | bytes 1327112 | tf_op jit(solution)/shard_map/ppermute | solution.py:86
  86.8 27.6 %collective-permute-start.24 = (bf16[192,1536]{1,0:T(8,128)(2,1)}, bf16[192,1536]{1,0:T(8,128)(2,1)}, u32[]{:S(2)}, u32[]{:S(2)}) collective-permute-start(bf16[192,1536]{1,0:T(8,128)(2,1)} %pad_maximum_fusion.4), channel_id=1, source_target_pairs={{0,12},{4,8},{8,4},{12,0},{1,13},{5,9},{9,5},{13,1},{2,14},{6,10},... | collective-permute-start | bytes 1769480 | tf_op jit(solution)/shard_map/ppermute | solution.py:36
  89.1 22.3 %collective-permute-start.13 = (bf16[2,128,768]{2,1,0:T(8,128)(2,1)}, bf16[2,128,768]{2,1,0:T(8,128)(2,1)}, u32[]{:S(2)}, u32[]{:S(2)}) collective-permute-start(bf16[2,128,768]{2,1,0:T(8,128)(2,1)} %pad_maximum_fusion.5), channel_id=1, source_target_pairs={{0,1},{1,0},{2,3},{3,2},{4,5},{5,4},{6,7},{7,6},{8,9},{9,8},{10,11... | collective-permute-start | bytes 1179656 | tf_op jit(solution)/shard_map/ppermute | solution.py:36
  109.5 13.0 %collective-permute-start.22 = (bf16[3,192,384]{2,1,0:T(8,128)(2,1)}, bf16[3,192,384]{2,1,0:T(8,128)(2,1)S(1)}, u32[]{:S(2)}, u32[]{:S(2)}) collective-permute-start(bf16[3,192,384]{2,1,0:T(8,128)(2,1)} %slice.344), channel_id=1, source_target_pairs={{0,1},{1,0},{2,3},{3,2},{4,5},{5,4},{6,7},{7,6},{8,9},{9,8},{10,11... | collective-permute-start | bytes 1327112 | tf_op jit(solution)/shard_map/ppermute | solution.py:36
  113.6 14.4 %collective-permute-start.14 = (bf16[2,128,768]{2,1,0:T(8,128)(2,1)S(1)}, bf16[2,128,768]{2,1,0:T(8,128)(2,1)S(1)}, u32[]{:S(2)}, u32[]{:S(2)}) collective-permute-start(bf16[2,128,768]{2,1,0:T(8,128)(2,1)S(1)} %pad_maximum_fusion.6), channel_id=1, source_target_pairs={{0,2},{1,3},{2,0},{3,1},{4,6},{5,7},{6,4},{7,5},{8,10},{9,11},{10,... | collective-permute-start | bytes 1179656 | tf_op jit(solution)/shard_map/ppermute | solution.py:36
  126.4 22.8 %collective-permute-start.25 = (bf16[3,192,768]{2,1,0:T(8,128)(2,1)}, bf16[3,192,768]{2,1,0:T(8,128)(2,1)}, u32[]{:S(2)}, u32[]{:S(2)}) collective-permute-start(bf16[3,192,768]{2,1,0:T(8,128)(2,1)} %pad_maximum_fusion.1.p5.refs_13_.refs_12_), channel_id=1, source_target_pairs={{0,1},{1,0},{2,3},{3,2},{4,5},{5,4},{6,7},{7,6},{8,9},{9,8},{10,11... | collective-permute-start | bytes 2654216 | tf_op jit(solution)/shard_map/ppermute | solution.py:36
  129.0 20.3 %collective-permute-start.15 = (bf16[512,768]{1,0:T(8,128)(2,1)}, bf16[512,768]{1,0:T(8,128)(2,1)}, u32[]{:S(2)}, u32[]{:S(2)}) collective-permute-start(bf16[512,768]{1,0:T(8,128)(2,1)} %pad_maximum_fusion.3), channel_id=1, source_target_pairs={{0,16},{16,0},{1,17},{17,1},{2,18},{18,2},{3,19},{19,3},{4,20},{20... | collective-permute-start | bytes 2359304 | tf_op jit(solution)/shard_map/ppermute | solution.py:32
  130.1 32.8 %collective-permute-start.28 = (bf16[3,192,768]{2,1,0:T(8,128)(2,1)S(1)}, bf16[3,192,768]{2,1,0:T(8,128)(2,1)S(1)}, u32[]{:S(2)}, u32[]{:S(2)}) collective-permute-start(bf16[3,192,768]{2,1,0:T(8,128)(2,1)S(1)} %pad_maximum_fusion.2.p6.refs_14_.refs_13_), channel_id=1, source_target_pairs={{0,18},{1,19},{2,16},{3,17},{16,2},{17,3},{18,0},{19,1},{4,22},{5,... | collective-permute-start | bytes 2654216 | tf_op jit(solution)/shard_map/ppermute | solution.py:86
  131.6 36.3 %collective-permute-start.26 = (bf16[3,192,768]{2,1,0:T(8,128)(2,1)S(1)}, bf16[3,192,768]{2,1,0:T(8,128)(2,1)S(1)}, u32[]{:S(2)}, u32[]{:S(2)}) collective-permute-start(bf16[3,192,768]{2,1,0:T(8,128)(2,1)S(1)} %pad_maximum_fusion.2.p6.refs_14_.refs_13_), channel_id=1, source_target_pairs={{0,1},{1,0},{2,3},{3,2},{4,5},{5,4},{6,7},{7,6},{8,9},{9,8},{10,11... | collective-permute-start | bytes 2654216 | tf_op jit(solution)/shard_map/ppermute | solution.py:36
  133.2 37.5 %collective-permute-start.27 = (bf16[3,192,768]{2,1,0:T(8,128)(2,1)}, bf16[3,192,768]{2,1,0:T(8,128)(2,1)S(1)}, u32[]{:S(2)}, u32[]{:S(2)}) collective-permute-start(bf16[3,192,768]{2,1,0:T(8,128)(2,1)} %pad_maximum_fusion.1.p5.refs_13_.refs_12_), channel_id=1, source_target_pairs={{0,18},{1,19},{2,16},{3,17},{16,2},{17,3},{18,0},{19,1},{4,22},{5,... | collective-permute-start | bytes 2654216 | tf_op jit(solution)/shard_map/ppermute | solution.py:86
  149.3 40.1 %collective-permute-start.29 = (bf16[3,192,768]{2,1,0:T(8,128)(2,1)}, bf16[3,192,768]{2,1,0:T(8,128)(2,1)S(1)}, u32[]{:S(2)}, u32[]{:S(2)}) collective-permute-start(bf16[3,192,768]{2,1,0:T(8,128)(2,1)} %collective-permute-done.25.p7.refs_15_.refs_14_), channel_id=1, source_target_pairs={{0,18},{1,19},{2,16},{3,17},{16,2},{17,3},{18,0},{19,1},{4,22},{5,... | collective-permute-start | bytes 2654216 | tf_op jit(solution)/shard_map/ppermute | solution.py:86
  163.0 26.5 %collective-permute-start.30 = (bf16[3,192,768]{2,1,0:T(8,128)(2,1)S(1)}, bf16[3,192,768]{2,1,0:T(8,128)(2,1)S(1)}, u32[]{:S(2)}, u32[]{:S(2)}) collective-permute-start(bf16[3,192,768]{2,1,0:T(8,128)(2,1)S(1)} %collective-permute-done.28.p10.refs_18_.refs_17_), channel_id=1, source_target_pairs={{0,1},{1,0},{2,3},{3,2},{4,5},{5,4},{6,7},{7,6},{8,9},{9,8},{10,11... | collective-permute-start | bytes 2654216 | tf_op jit(solution)/shard_map/ppermute | solution.py:36
  164.6 24.8 %collective-permute-start.23 = (bf16[512,768]{1,0:T(8,128)(2,1)S(1)}, bf16[512,768]{1,0:T(8,128)(2,1)S(1)}, u32[]{:S(2)}, u32[]{:S(2)}) collective-permute-start(bf16[512,768]{1,0:T(8,128)(2,1)S(1)} %get-tuple-element.172.own), channel_id=1, source_target_pairs={{0,16},{16,0},{1,17},{17,1},{2,18},{18,2},{3,19},{19,3},{4,20},{20... | collective-permute-start | bytes 2359304 | tf_op jit(solution)/shard_map/ppermute | solution.py:32
  275.7 32.9 %collective-permute-start.41 = (bf16[4,192,1536]{2,1,0:T(8,128)(2,1)}, bf16[4,192,1536]{2,1,0:T(8,128)(2,1)}, u32[]{:S(2)}, u32[]{:S(2)}) collective-permute-start(bf16[4,192,1536]{2,1,0:T(8,128)(2,1)} %get-tuple-element.242), channel_id=1, source_target_pairs={{0,18},{1,19},{2,16},{3,17},{4,22},{5,23},{6,20},{7,21},{8,26},{9,... | collective-permute-start | bytes 7077896 | tf_op jit(solution)/shard_map/ppermute | solution.py:48
  279.7 28.9 %collective-permute-start.42 = (bf16[2,192,1536]{2,1,0:T(8,128)(2,1)S(1)}, bf16[2,192,1536]{2,1,0:T(8,128)(2,1)S(1)}, u32[]{:S(2)}, u32[]{:S(2)}) collective-permute-start(bf16[2,192,1536]{2,1,0:T(8,128)(2,1)S(1)} %get-tuple-element.201), channel_id=1, source_target_pairs={{0,1},{1,0},{2,3},{3,2},{4,5},{5,4},{6,7},{7,6},{8,9},{9,8},{10,11... | collective-permute-start | bytes 3538952 | tf_op jit(solution)/shard_map/ppermute | solution.py:36
  293.2 23.6 %collective-permute-start.43 = (bf16[512,768]{1,0:T(8,128)(2,1)S(1)}, bf16[512,768]{1,0:T(8,128)(2,1)S(1)}, u32[]{:S(2)}, u32[]{:S(2)}) collective-permute-start(bf16[512,768]{1,0:T(8,128)(2,1)S(1)} %get-tuple-element.224.refs_1_), channel_id=1, source_target_pairs={{0,16},{16,0},{1,17},{17,1},{2,18},{18,2},{3,19},{19,3},{4,20},{20... | collective-permute-start | bytes 2359304 | tf_op jit(solution)/shard_map/ppermute | solution.py:32
  297.5 27.4 %collective-permute-start.44 = (bf16[4,208,768]{2,1,0:T(8,128)(2,1)S(1)}, bf16[4,208,768]{2,1,0:T(8,128)(2,1)}, u32[]{:S(2)}, u32[]{:S(2)}) collective-permute-start(bf16[4,208,768]{2,1,0:T(8,128)(2,1)S(1)} %get-tuple-element.257), channel_id=1, source_target_pairs={{0,18},{1,19},{2,16},{3,17},{4,22},{5,23},{6,20},{7,21},{8,26},{9,... | collective-permute-start | bytes 3833864 | tf_op jit(solution)/shard_map/ppermute | solution.py:48
  302.0 22.8 %collective-permute-start.45 = (bf16[2,208,768]{2,1,0:T(8,128)(2,1)S(1)}, bf16[2,208,768]{2,1,0:T(8,128)(2,1)S(1)}, u32[]{:S(2)}, u32[]{:S(2)}) collective-permute-start(bf16[2,208,768]{2,1,0:T(8,128)(2,1)S(1)} %get-tuple-element.218), channel_id=1, source_target_pairs={{0,1},{1,0},{2,3},{3,2},{4,5},{5,4},{6,7},{7,6},{8,9},{9,8},{10,11... | collective-permute-start | bytes 1916936 | tf_op jit(solution)/shard_map/ppermute | solution.py:36
  310.0 29.7 %collective-permute-start.47 = (bf16[2,192,1536]{2,1,0:T(8,128)(2,1)}, bf16[2,192,1536]{2,1,0:T(8,128)(2,1)}, u32[]{:S(2)}, u32[]{:S(2)}) collective-permute-start(bf16[2,192,1536]{2,1,0:T(8,128)(2,1)} %add_convert_fusion.6), channel_id=1, source_target_pairs={{0,18},{1,19},{2,16},{3,17},{4,22},{5,23},{6,20},{7,21},{8,26},{9,... | collective-permute-start | bytes 3538952 | tf_op jit(solution)/shard_map/ppermute | solution.py:48
  315.1 25.0 %collective-permute-start.46 = (bf16[2,192,1536]{2,1,0:T(8,128)(2,1)}, bf16[2,192,1536]{2,1,0:T(8,128)(2,1)}, u32[]{:S(2)}, u32[]{:S(2)}) collective-permute-start(bf16[2,192,1536]{2,1,0:T(8,128)(2,1)} %add_convert_fusion.7), channel_id=1, source_target_pairs={{16,17},{17,16},{18,19},{19,18},{20,21},{21,20},{22,23},{23,22},{2... | collective-permute-start | bytes 3538952 | tf_op jit(solution)/shard_map/ppermute | solution.py:42
  324.8 21.7 %collective-permute-start.48 = (bf16[512,768]{1,0:T(8,128)(2,1)S(1)}, bf16[512,768]{1,0:T(8,128)(2,1)S(1)}, u32[]{:S(2)}, u32[]{:S(2)}) collective-permute-start(bf16[512,768]{1,0:T(8,128)(2,1)S(1)} %get-tuple-element.233.own), channel_id=1, source_target_pairs={{0,16},{16,0},{1,17},{17,1},{2,18},{18,2},{3,19},{19,3},{4,20},{20... | collective-permute-start | bytes 2359304 | tf_op jit(solution)/shard_map/ppermute | solution.py:32
  326.7 34.4 %collective-permute-start.52 = (bf16[2,208,768]{2,1,0:T(8,128)(2,1)}, bf16[2,208,768]{2,1,0:T(8,128)(2,1)}, u32[]{:S(2)}, u32[]{:S(2)}) collective-permute-start(bf16[2,208,768]{2,1,0:T(8,128)(2,1)} %add_convert_fusion.14), channel_id=1, source_target_pairs={{0,18},{1,19},{2,16},{3,17},{4,22},{5,23},{6,20},{7,21},{8,26},{9,... | collective-permute-start | bytes 1916936 | tf_op jit(solution)/shard_map/ppermute | solution.py:48
  332.3 32.3 %collective-permute-start.51 = (bf16[2,208,768]{2,1,0:T(8,128)(2,1)}, bf16[2,208,768]{2,1,0:T(8,128)(2,1)}, u32[]{:S(2)}, u32[]{:S(2)}) collective-permute-start(bf16[2,208,768]{2,1,0:T(8,128)(2,1)} %add_convert_fusion.15), channel_id=1, source_target_pairs={{16,17},{17,16},{18,19},{19,18},{20,21},{21,20},{22,23},{23,22},{2... | collective-permute-start | bytes 1916936 | tf_op jit(solution)/shard_map/ppermute | solution.py:42
  339.7 30.1 %collective-permute-start.50 = (bf16[2,192,1536]{2,1,0:T(8,128)(2,1)S(1)}, bf16[2,192,1536]{2,1,0:T(8,128)(2,1)S(1)}, u32[]{:S(2)}, u32[]{:S(2)}) collective-permute-start(bf16[2,192,1536]{2,1,0:T(8,128)(2,1)S(1)} %get-tuple-element.240), channel_id=1, source_target_pairs={{0,1},{1,0},{2,3},{3,2},{4,5},{5,4},{6,7},{7,6},{8,9},{9,8},{10,11... | collective-permute-start | bytes 3538952 | tf_op jit(solution)/shard_map/ppermute | solution.py:36
  340.1 30.6 %collective-permute-start.49 = (bf16[4,192,1536]{2,1,0:T(8,128)(2,1)}, bf16[4,192,1536]{2,1,0:T(8,128)(2,1)}, u32[]{:S(2)}, u32[]{:S(2)}) collective-permute-start(bf16[4,192,1536]{2,1,0:T(8,128)(2,1)} %get-tuple-element.279), channel_id=1, source_target_pairs={{16,2},{17,3},{18,0},{19,1},{20,6},{21,7},{22,4},{23,5},{24,10},{2... | collective-permute-start | bytes 7077896 | tf_op jit(solution)/shard_map/ppermute | solution.py:48
  346.4 38.1 %collective-permute-start.58 = (bf16[2,192,1536]{2,1,0:T(8,128)(2,1)}, bf16[2,192,1536]{2,1,0:T(8,128)(2,1)}, u32[]{:S(2)}, u32[]{:S(2)}) collective-permute-start(bf16[2,192,1536]{2,1,0:T(8,128)(2,1)} %add_convert_fusion.4), channel_id=1, source_target_pairs={{16,24},{20,28},{24,16},{28,20},{17,25},{21,29},{25,17},{29,21},{1... | collective-permute-start | bytes 3538952 | tf_op jit(solution)/shard_map/ppermute | solution.py:42
  361.1 18.7 %collective-permute-start.68 = (bf16[512,768]{1,0:T(8,128)(2,1)S(1)}, bf16[512,768]{1,0:T(8,128)(2,1)S(1)}, u32[]{:S(2)}, u32[]{:S(2)}) collective-permute-start(bf16[512,768]{1,0:T(8,128)(2,1)S(1)} %get-tuple-element.256), channel_id=1, source_target_pairs={{0,16},{16,0},{1,17},{17,1},{2,18},{18,2},{3,19},{19,3},{4,20},{20... | collective-permute-start | bytes 2359304 | tf_op jit(solution)/shard_map/ppermute | solution.py:32
  366.8 37.6 %collective-permute-start.55 = (bf16[2,208,768]{2,1,0:T(8,128)(2,1)}, bf16[2,208,768]{2,1,0:T(8,128)(2,1)}, u32[]{:S(2)}, u32[]{:S(2)}) collective-permute-start(bf16[2,208,768]{2,1,0:T(8,128)(2,1)} %add_convert_fusion.12), channel_id=1, source_target_pairs={{16,24},{20,28},{24,16},{28,20},{17,25},{21,29},{25,17},{29,21},{1... | collective-permute-start | bytes 1916936 | tf_op jit(solution)/shard_map/ppermute | solution.py:42
  372.0 18.0 %collective-permute-start.57 = (bf16[2,192,1536]{2,1,0:T(8,128)(2,1)}, bf16[2,192,1536]{2,1,0:T(8,128)(2,1)}, u32[]{:S(2)}, u32[]{:S(2)}) collective-permute-start(bf16[2,192,1536]{2,1,0:T(8,128)(2,1)} %add_convert_fusion.2), channel_id=1, source_target_pairs={{16,2},{17,3},{18,0},{19,1},{20,6},{21,7},{22,4},{23,5},{24,10},{2... | collective-permute-start | bytes 3538952 | tf_op jit(solution)/shard_map/ppermute | solution.py:48
  376.1 24.6 %collective-permute-start.56 = (bf16[2,192,1536]{2,1,0:T(8,128)(2,1)}, bf16[2,192,1536]{2,1,0:T(8,128)(2,1)}, u32[]{:S(2)}, u32[]{:S(2)}) collective-permute-start(bf16[2,192,1536]{2,1,0:T(8,128)(2,1)} %add_convert_fusion.3), channel_id=1, source_target_pairs={{0,1},{1,0},{2,3},{3,2},{4,5},{5,4},{6,7},{7,6},{8,9},{9,8},{10,11... | collective-permute-start | bytes 3538952 | tf_op jit(solution)/shard_map/ppermute | solution.py:42
  384.0 31.9 %collective-permute-start.54 = (bf16[2,208,768]{2,1,0:T(8,128)(2,1)S(1)}, bf16[2,208,768]{2,1,0:T(8,128)(2,1)S(1)}, u32[]{:S(2)}, u32[]{:S(2)}) collective-permute-start(bf16[2,208,768]{2,1,0:T(8,128)(2,1)S(1)} %get-tuple-element.276), channel_id=1, source_target_pairs={{0,1},{1,0},{2,3},{3,2},{4,5},{5,4},{6,7},{7,6},{8,9},{9,8},{10,11... | collective-permute-start | bytes 1916936 | tf_op jit(solution)/shard_map/ppermute | solution.py:36
  384.5 31.5 %collective-permute-start.53 = (bf16[4,208,768]{2,1,0:T(8,128)(2,1)S(1)}, bf16[4,208,768]{2,1,0:T(8,128)(2,1)S(1)}, u32[]{:S(2)}, u32[]{:S(2)}) collective-permute-start(bf16[4,208,768]{2,1,0:T(8,128)(2,1)S(1)} %get-tuple-element.291), channel_id=1, source_target_pairs={{16,2},{17,3},{18,0},{19,1},{20,6},{21,7},{22,4},{23,5},{24,10},{2... | collective-permute-start | bytes 3833864 | tf_op jit(solution)/shard_map/ppermute | solution.py:48
  404.5 15.3 %collective-permute-start.59 = (bf16[192,1536]{1,0:T(8,128)(2,1)S(1)}, bf16[192,1536]{1,0:T(8,128)(2,1)S(1)}, u32[]{:S(2)}, u32[]{:S(2)}) collective-permute-start(bf16[192,1536]{1,0:T(8,128)(2,1)S(1)} %get-tuple-element.363), channel_id=1, source_target_pairs={{0,4},{4,0},{8,12},{12,8},{1,5},{5,1},{9,13},{13,9},{2,6},{6,2},{1... | collective-permute-start | bytes 1769480 | tf_op jit(solution)/shard_map/ppermute | solution.py:42
  408.2 25.4 %collective-permute-start.66 = (bf16[192,1536]{1,0:T(8,128)(2,1)S(1)}, bf16[192,1536]{1,0:T(8,128)(2,1)S(1)}, u32[]{:S(2)}, u32[]{:S(2)}) collective-permute-start(bf16[192,1536]{1,0:T(8,128)(2,1)S(1)} %get-tuple-element.361), channel_id=1, source_target_pairs={{0,8},{4,12},{8,0},{12,4},{1,9},{5,13},{9,1},{13,5},{2,10},{6,14},... | collective-permute-start | bytes 1769480 | tf_op jit(solution)/shard_map/ppermute | solution.py:42
  410.8 22.8 %collective-permute-start.67 = (bf16[192,1536]{1,0:T(8,128)(2,1)S(1)}, bf16[192,1536]{1,0:T(8,128)(2,1)S(1)}, u32[]{:S(2)}, u32[]{:S(2)}) collective-permute-start(bf16[192,1536]{1,0:T(8,128)(2,1)S(1)} %get-tuple-element.360), channel_id=1, source_target_pairs={{0,12},{4,8},{8,4},{12,0},{1,13},{5,9},{9,5},{13,1},{2,14},{6,10},... | collective-permute-start | bytes 1769480 | tf_op jit(solution)/shard_map/ppermute | solution.py:42
  420.2 13.4 %collective-permute-start.69 = (bf16[2,128,768]{2,1,0:T(8,128)(2,1)S(1)}, bf16[2,128,768]{2,1,0:T(8,128)(2,1)S(1)}, u32[]{:S(2)}, u32[]{:S(2)}) collective-permute-start(bf16[2,128,768]{2,1,0:T(8,128)(2,1)S(1)} %pad_maximum_fusion.7), channel_id=1, source_target_pairs={{0,1},{1,0},{2,3},{3,2},{4,5},{5,4},{6,7},{7,6},{8,9},{9,8},{10,11... | collective-permute-start | bytes 1179656 | tf_op jit(solution)/shard_map/ppermute | solution.py:36
  433.7 16.5 %collective-permute-start.70 = (bf16[2,128,768]{2,1,0:T(8,128)(2,1)S(1)}, bf16[2,128,768]{2,1,0:T(8,128)(2,1)S(1)}, u32[]{:S(2)}, u32[]{:S(2)}) collective-permute-start(bf16[2,128,768]{2,1,0:T(8,128)(2,1)S(1)} %pad_maximum_fusion.8), channel_id=1, source_target_pairs={{0,2},{1,3},{2,0},{3,1},{4,6},{5,7},{6,4},{7,5},{8,10},{9,11},{10,... | collective-permute-start | bytes 1179656 | tf_op jit(solution)/shard_map/ppermute | solution.py:36
  436.4 23.8 %collective-permute-start.65 = (bf16[208,2304]{1,0:T(8,128)(2,1)S(1)}, bf16[208,2304]{1,0:T(8,128)(2,1)S(1)}, u32[]{:S(2)}, u32[]{:S(2)}) collective-permute-start(bf16[208,2304]{1,0:T(8,128)(2,1)S(1)} %fusion.1), channel_id=1, source_target_pairs={{16,20},{20,16},{24,28},{28,24},{17,21},{21,17},{25,29},{29,25},{1... | collective-permute-start | bytes 2875400 | tf_op jit(solution)/shard_map/ppermute | solution.py:42
  437.2 19.7 %collective-permute-start.63 = (bf16[208,768]{1,0:T(8,128)(2,1)S(1)}, bf16[208,768]{1,0:T(8,128)(2,1)S(1)}, u32[]{:S(2)}, u32[]{:S(2)}) collective-permute-start(bf16[208,768]{1,0:T(8,128)(2,1)S(1)} %get-tuple-element.382), channel_id=1, source_target_pairs={{0,8},{4,12},{8,0},{12,4},{1,9},{5,13},{9,1},{13,5},{2,10},{6,14},... | collective-permute-start | bytes 958472 | tf_op jit(solution)/shard_map/ppermute | solution.py:42
  (111 other events, 1846.2 us)

commit v3 on v2

--- a/solution.py
+++ b/solution.py
@@ -808,8 +808,8 @@
     else:
         pack = lax.all_gather(pack, "dp", axis=0, tiled=True)
         own, other_rows = pack[: width // 2], pack[width // 2 :][None]
+    message = spread_tensor(message)
     near0, far0 = gather_own(after(own, message))
-    message = spread_tensor(message)
     both0 = gather_own_both(near0, far0)
     owns = [own, near0, far0, *both0]
 

time: 473 us -> 474 us (level)
  starting transfers between devices: 113 us -> 130 us
  waiting for transfers between devices: 156 us -> 139 us
    ppermute x33, waiting for transfers between devices: 78.5 us -> 60.8 us  [hop(): lax.ppermute(block, axis, [(i, i ^ flip) for i in range(lax.axis_size(axi...]
    ppermute x33, starting transfers between devices: 47.9 us -> 58.2 us  [hop(): lax.ppermute(block, axis, [(i, i ^ flip) for i in range(lax.axis_size(axi...]
    ppermute x10, starting transfers between devices: 5.35 us -> 12.7 us  [swap_cores(): return lax.ppermute(block, 'section', [(0, 1), (1, 0)])]
where the time goes in v3:
time: 474 us; the launch traced here: 467 us
  waiting for transfers between devices  139 us (29%)
  starting transfers between devices  130 us (27%)
  Pallas kernels  104 us (22%)
  other arithmetic  47.5 us (10%)
  local copies, waits for them, and re-layouts  43 us (9%)
    ppermute x33, waiting for transfers between devices, hop(): lax.ppermute(block, axis, [(i, i ^ flip) for i in range(lax.axis_size(axi...  60.8 us
    ppermute x33, starting transfers between devices, hop(): lax.ppermute(block, axis, [(i, i ^ flip) for i in range(lax.axis_size(axi...  58.2 us
    ppermute x13, starting transfers between devices, core_hop(): return lax.ppermute(block, ('section', axis), route)  35.4 us
    ppermute x7, waiting for transfers between devices, cross_all(): return lax.ppermute(block, ('section', 'tensor'), route)  34.9 us
    ppermute x13, waiting for transfers between devices, core_hop(): return lax.ppermute(block, ('section', axis), route)  33.3 us
    convert_element_type x18, other arithmetic, add_low(): return total.astype(BF16)  26.9 us
    pallas_call x2, Pallas kernels, attn_backward(): pl.pallas_call(body, out_shape=[sds((length, width), BF16), sds((length,...  25.8 us
    pallas_call x2, Pallas kernels, attn_forward(): pl.pallas_call(body, out_shape=outs, in_specs=specs, out_specs=[VM] * len...  25.2 us
  transfers between devices with their start and end apart: 71, of which 29 were waited for; matrix products, arithmetic and copies ran while one was open for 13% of the time, Pallas kernels for 14%

profile of v3, /device:TPU:0, one launch (start us, length us, event | category | flops | bytes accessed | tf_op | source)
XLA Modules:
  0.0 467.3 jit_solution(14648180807662777772)
XLA Ops:
  5.2 3.1 collective-permute-start
  8.3 2.6 collective-permute-start.1
  29.4 3.5 collective-permute-start.8
  34.4 9.1 %collective-permute-done.7 = bf16[192,768]{1,0:T(8,128)(2,1)S(1)} collective-permute-done((bf16[192,768]{1,0:T(8,128)(2,1)}, bf16[192,768]{1,0:T(8,128)(2,1)S(1)}, u32[]{:S(2)}, u32[]{:S(2)}) %collective-permute-start.7) | collective-permute-done | bytes 294944 | tf_op jit(solution)/shard_map/ppermute | solution.py:36
  43.5 10.2 %collective-permute-done.8 = bf16[192,768]{1,0:T(8,128)(2,1)S(1)} collective-permute-done((bf16[192,768]{1,0:T(8,128)(2,1)}, bf16[192,768]{1,0:T(8,128)(2,1)S(1)}, u32[]{:S(2)}, u32[]{:S(2)}) %collective-permute-start.8) | collective-permute-done | bytes 294944 | tf_op jit(solution)/shard_map/ppermute | solution.py:36
  58.0 6.2 %collective-permute-start.19 = (bf16[192,1536]{1,0:T(8,128)(2,1)}, bf16[192,1536]{1,0:T(8,128)(2,1)S(1)}, u32[]{:S(2)}, u32[]{:S(2)}) collective-permute-start(bf16[192,1536]{1,0:T(8,128)(2,1)} %pad_maximum_fusion.4), channel_id=1, source_target_pairs={{0,4},{4,0},{8,12},{12,8},{1,5},{5,1},{9,13},{13,9},{2,6},{6,2},{1... | collective-permute-start | bytes 1769480 | tf_op jit(solution)/shard_map/ppermute | solution.py:36
  69.1 7.0 %collective-permute-done.12.refs_8_.refs_9_.refs_12_.refs_13_.p7.p8 = bf16[3,192,768]{2,1,0:T(8,128)(2,1)} collective-permute-done((bf16[3,192,768]{2,1,0:T(8,128)(2,1)}, bf16[3,192,768]{2,1,0:T(8,128)(2,1)}, u32[]{:S(2)}, u32[]{:S(2)}) %collective-permute-start.12) | collective-permute-done | bytes 884768 | tf_op jit(solution)/shard_map/ppermute | solution.py:36
  80.5 8.8 %collective-permute-done.16.refs_4_.p3.refs_8_.refs_11_.refs_10_ = bf16[192,1152]{1,0:T(8,128)(2,1)S(1)} collective-permute-done((bf16[192,1152]{1,0:T(8,128)(2,1)}, bf16[192,1152]{1,0:T(8,128)(2,1)S(1)}, u32[]{:S(2)}, u32[]{:S(2)}) %collective-permute-start.16) | collective-permute-done | bytes 442400 | tf_op jit(solution)/shard_map/ppermute | solution.py:86
  98.5 4.6 collective-permute-done.13
  105.2 9.4 %collective-permute-start.14 = (bf16[2,128,768]{2,1,0:T(8,128)(2,1)S(1)}, bf16[2,128,768]{2,1,0:T(8,128)(2,1)S(1)}, u32[]{:S(2)}, u32[]{:S(2)}) collective-permute-start(bf16[2,128,768]{2,1,0:T(8,128)(2,1)S(1)} %pad_maximum_fusion.6), channel_id=1, source_target_pairs={{0,2},{1,3},{2,0},{3,1},{4,6},{5,7},{6,4},{7,5},{8,10},{9,11},{10,... | collective-permute-start | bytes 1179656 | tf_op jit(solution)/shard_map/ppermute | solution.py:36
  120.1 3.7 collective-permute-done.14
  130.0 7.8 %collective-permute-done.25.p7.refs_15_.refs_14_ = bf16[3,192,768]{2,1,0:T(8,128)(2,1)} collective-permute-done((bf16[3,192,768]{2,1,0:T(8,128)(2,1)}, bf16[3,192,768]{2,1,0:T(8,128)(2,1)}, u32[]{:S(2)}, u32[]{:S(2)}) %collective-permute-start.25) | collective-permute-done | bytes 884768 | tf_op jit(solution)/shard_map/ppermute | solution.py:36
  139.4 12.1 %attn_forward.2 = (bf16[512,768]{1,0:T(8,128)(2,1)S(1)}, bf16[512,1152]{1,0:T(8,128)(2,1)}, bf16[6,512,512]{2,1,0:T(8,128)(2,1)}, bf16[512,384]{1,0:T(8,128)(2,1)S(1)}) custom-call(s32[5]{0:T(128)S(1)} %get-tuple-element.426.meta, bf16[512,768]{1,0:T(8,128)(2,1)S(1)} %get-tuple-element.166.refs_0_.x, ...), custom_call_target="tpu_custom_call" | custom-call | flops 14300000256 | tf_op jit(solution)/shard_map/attn_forward/pallas_call | solution.py:382
  154.0 6.7 %collective-permute-start.23 = (bf16[512,768]{1,0:T(8,128)(2,1)S(1)}, bf16[512,768]{1,0:T(8,128)(2,1)S(1)}, u32[]{:S(2)}, u32[]{:S(2)}) collective-permute-start(bf16[512,768]{1,0:T(8,128)(2,1)S(1)} %get-tuple-element.172.own), channel_id=1, source_target_pairs={{0,16},{16,0},{1,17},{17,1},{2,18},{18,2},{3,19},{19,3},{4,20},{20... | collective-permute-start | bytes 2359304 | tf_op jit(solution)/shard_map/ppermute | solution.py:32
  160.7 7.1 %collective-permute-done.27.p9.refs_17_.refs_16_ = bf16[3,192,768]{2,1,0:T(8,128)(2,1)S(1)} collective-permute-done((bf16[3,192,768]{2,1,0:T(8,128)(2,1)}, bf16[3,192,768]{2,1,0:T(8,128)(2,1)S(1)}, u32[]{:S(2)}, u32[]{:S(2)}) %collective-permute-start.27) | collective-permute-done | bytes 884768 | tf_op jit(solution)/shard_map/ppermute | solution.py:86
  167.8 19.0 %collective-permute-done.29.p11.refs_19_.refs_18_ = bf16[3,192,768]{2,1,0:T(8,128)(2,1)S(1)} collective-permute-done((bf16[3,192,768]{2,1,0:T(8,128)(2,1)}, bf16[3,192,768]{2,1,0:T(8,128)(2,1)S(1)}, u32[]{:S(2)}, u32[]{:S(2)}) %collective-permute-start.29) | collective-permute-done | bytes 884768 | tf_op jit(solution)/shard_map/ppermute | solution.py:86
  188.6 8.9 %ffn_forward.2 = (bf16[512,768]{1,0:T(8,128)(2,1)S(1)}, f32[512,768]{1,0:T(8,128)}, bf16[512,768]{1,0:T(8,128)(2,1)S(1)}, f32[512,1]{1,0:T(8,128)S(1)}, bf16[512...) custom-call(s32[5]{0:T(128)S(1)} %get-tuple-element.426.meta, bf16[512,768]{1,0:T(8,128)(2,1)S(1)} %get-tuple-element.166.refs_0_.x, ...), custom_call_target="tpu_custom_call" | custom-call | flops 9900000256 | tf_op jit(solution)/shard_map/ffn_forward/pallas_call | solution.py:420
  202.3 13.2 %attn_forward.3 = (bf16[512,768]{1,0:T(8,128)(2,1)S(1)}, bf16[512,1152]{1,0:T(8,128)(2,1)}, bf16[6,512,512]{2,1,0:T(8,128)(2,1)}, bf16[512,384]{1,0:T(8,128)(2,1...) custom-call(s32[5]{0:T(128)S(1)} %get-tuple-element.427.meta, ...), custom_call_target="tpu_custom_call" | custom-call | flops 14300000256 | tf_op jit(solution)/shard_map/attn_forward/pallas_call | solution.py:382
  218.9 8.9 %ffn_forward.3 = (bf16[512,768]{1,0:T(8,128)(2,1)S(1)}, f32[512,768]{1,0:T(8,128)}, bf16[512,768]{1,0:T(8,128)(2,1)S(1)}, f32[512,1]{1,0:T(8,128)S(1)}, bf16[512...) custom-call(s32[5]{0:T(128)S(1)} %get-tuple-element.427.meta, bf16[512,768]{1,0:T(8,128)(2,1)S(1)} %get-tuple-element.183.x, ...), custom_call_target="tpu_custom_call" | custom-call | flops 9900000256 | tf_op jit(solution)/shard_map/ffn_forward/pallas_call | solution.py:420
  236.3 5.8 %collective-permute-start.35 = (bf16[4,768]{1,0:T(4,128)(2,1)S(1)}, bf16[4,768]{1,0:T(4,128)(2,1)}, u32[]{:S(2)}, u32[]{:S(2)}) collective-permute-start(bf16[4,768]{1,0:T(4,128)(2,1)S(1)} %get-tuple-element.190), channel_id=1, source_target_pairs={{0,8},{4,12},{8,0},{12,4},{1,9},{5,13},{9,1},{13,5},{2,10},{6,14},... | collective-permute-start | bytes 18440 | tf_op jit(solution)/shard_map/ppermute | solution.py:36
  243.8 3.8 collective-permute-done.36
  262.2 7.1 %ffn_backward.2 = (bf16[512,768]{1,0:T(8,128)(2,1)S(1)}, f32[512,768]{1,0:T(8,128)}, bf16[512,768]{1,0:T(8,128)(2,1)S(1)}, bf16[512,1536]{1,0:T(8,128)(2,1)}, f3...) custom-call(s32[5]{0:T(128)S(1)} %copy-done.17, s32[4]{0:T(128)S(1)} %copy-done.15, ...), custom_call_target="tpu_custom_call" | custom-call | flops 9900000256 | tf_op jit(solution)/shard_map/ffn_backward/pallas_call | solution.py:532
  269.4 6.0 %ffn_grads.2 = (bf16[4,192,1536]{2,1,0:T(8,128)(2,1)}, bf16[2,192,1536]{2,1,0:T(8,128)(2,1)S(1)}, bf16[2,192,1536]{2,1,0:T(8,128)(2,1)S(1)}) custom-call(s32[5]{0:T(128)S(1)} %copy-done.17, f32[512,768]{1,0:T(8,128)S(1)} %copy-done.31, bf16[512,1536]{1,0:T(8,128)(2,1)} %get-tuple-element.198.d_pre, bf16[512,768]{1,0:T(8,128)(2,1)S(1)} %get-tuple-element.199.d_ffn, ...), custom_call_target="tpu_custom_call" | custom-call | flops 7699999744 | tf_op jit(solution)/shard_map/ffn_grads/pallas_call | solution.py:583
  275.4 4.3 collective-permute-start.41
  280.5 12.9 %attn_backward.2 = (bf16[512,768]{1,0:T(8,128)(2,1)S(1)}, f32[512,768]{1,0:T(8,128)}, bf16[512,768]{1,0:T(8,128)(2,1)S(1)}, bf16[512,1152]{1,0:T(8,128)(2,1)}, f...) custom-call(s32[5]{0:T(128)S(1)} %copy-done.17, f32[512,768]{1,0:T(8,128)} %get-tuple-element.202.d_second, ...), custom_call_target="tpu_custom_call" | custom-call | flops 16499999744 | tf_op jit(solution)/shard_map/attn_backward/pallas_call | solution.py:650
  294.8 2.9 attn_grads.2
  297.7 5.1 %collective-permute-start.44 = (bf16[4,208,768]{2,1,0:T(8,128)(2,1)S(1)}, bf16[4,208,768]{2,1,0:T(8,128)(2,1)}, u32[]{:S(2)}, u32[]{:S(2)}) collective-permute-start(bf16[4,208,768]{2,1,0:T(8,128)(2,1)S(1)} %get-tuple-element.257), channel_id=1, source_target_pairs={{0,18},{1,19},{2,16},{3,17},{4,22},{5,23},{6,20},{7,21},{8,26},{9,... | collective-permute-start | bytes 3833864 | tf_op jit(solution)/shard_map/ppermute | solution.py:48
  303.3 4.9 %collective-permute-done.42 = bf16[2,192,1536]{2,1,0:T(8,128)(2,1)S(1)} collective-permute-done((bf16[2,192,1536]{2,1,0:T(8,128)(2,1)S(1)}, bf16[2,192,1536]{2,1,0:T(8,128)(2,1)S(1)}, u32[]{:S(2)}, u32[]{:S(2)}) %collective-permute-start.42) | collective-permute-done | bytes 1179680 | tf_op jit(solution)/shard_map/ppermute | solution.py:36
  316.4 7.9 %ffn_backward.3 = (bf16[512,768]{1,0:T(8,128)(2,1)S(1)}, f32[512,768]{1,0:T(8,128)}, bf16[512,768]{1,0:T(8,128)(2,1)S(1)}, bf16[512,1536]{1,0:T(8,128)(2,1)}, f3...) custom-call(s32[5]{0:T(128)S(1)} %copy-done.13, f32[512,768]{1,0:T(8,128)} %get-tuple-element.223.refs_0_, ...), custom_call_target="tpu_custom_call" | custom-call | flops 9900000256 | tf_op jit(solution)/shard_map/ffn_backward/pallas_call | solution.py:532
  326.4 3.6 collective-permute-start.52
  333.6 5.8 %ffn_grads.3 = (bf16[4,192,1536]{2,1,0:T(8,128)(2,1)}, bf16[2,192,1536]{2,1,0:T(8,128)(2,1)S(1)}, bf16[2,192,1536]{2,1,0:T(8,128)(2,1)S(1)}) custom-call(s32[5]{0:T(128)S(1)} %copy-done.13, f32[512,768]{1,0:T(8,128)S(1)} %copy-done.40, bf16[512,1536]{1,0:T(8,128)(2,1)} %get-tuple-element.229.d_pre, bf16[512,768]{1,0:T(8,128)(2,1)S(1)} %get-tuple-element.238.d_ffn, ...), custom_call_target="tpu_custom_call" | custom-call | flops 7699999744 | tf_op jit(solution)/shard_map/ffn_grads/pallas_call | solution.py:583
  342.3 2.7 add_convert_fusion.4
  348.9 12.9 %attn_backward.3 = (bf16[512,768]{1,0:T(8,128)(2,1)S(1)}, f32[512,768]{1,0:T(8,128)}, bf16[512,768]{1,0:T(8,128)(2,1)S(1)}, bf16[512,1152]{1,0:T(8,128)(2,1)}, f...) custom-call(s32[5]{0:T(128)S(1)} %copy-done.13, f32[512,768]{1,0:T(8,128)} %get-tuple-element.248.d_second, ...), custom_call_target="tpu_custom_call" | custom-call | flops 16499999744 | tf_op jit(solution)/shard_map/attn_backward/pallas_call | solution.py:650
  361.9 3.5 collective-permute-start.68
  374.2 2.6 add_convert_fusion.3
  376.8 2.7 collective-permute-start.56
  380.9 2.9 attn_grads.3
  388.1 2.7 collective-permute-done.57
  390.8 10.9 %collective-permute-done.56 = bf16[2,192,1536]{2,1,0:T(8,128)(2,1)} collective-permute-done((bf16[2,192,1536]{2,1,0:T(8,128)(2,1)}, bf16[2,192,1536]{2,1,0:T(8,128)(2,1)}, u32[]{:S(2)}, u32[]{:S(2)}) %collective-permute-start.56) | collective-permute-done | bytes 1179680 | tf_op jit(solution)/shard_map/ppermute | solution.py:42
  407.6 4.0 collective-permute-start.66
  411.6 4.2 collective-permute-start.67
  417.0 5.3 %collective-permute-done.59 = bf16[192,1536]{1,0:T(8,128)(2,1)S(1)} collective-permute-done((bf16[192,1536]{1,0:T(8,128)(2,1)S(1)}, bf16[192,1536]{1,0:T(8,128)(2,1)S(1)}, u32[]{:S(2)}, u32[]{:S(2)}) %collective-permute-start.59) | collective-permute-done | bytes 589856 | tf_op jit(solution)/shard_map/ppermute | solution.py:42
  424.7 3.4 collective-permute-start.60
  428.2 4.7 %collective-permute-done.66 = bf16[192,1536]{1,0:T(8,128)(2,1)S(1)} collective-permute-done((bf16[192,1536]{1,0:T(8,128)(2,1)S(1)}, bf16[192,1536]{1,0:T(8,128)(2,1)S(1)}, u32[]{:S(2)}, u32[]{:S(2)}) %collective-permute-start.66) | collective-permute-done | bytes 589856 | tf_op jit(solution)/shard_map/ppermute | solution.py:42
  438.7 7.2 %collective-permute-start.63 = (bf16[208,768]{1,0:T(8,128)(2,1)S(1)}, bf16[208,768]{1,0:T(8,128)(2,1)S(1)}, u32[]{:S(2)}, u32[]{:S(2)}) collective-permute-start(bf16[208,768]{1,0:T(8,128)(2,1)S(1)} %get-tuple-element.382), channel_id=1, source_target_pairs={{0,8},{4,12},{8,0},{12,4},{1,9},{5,13},{9,1},{13,5},{2,10},{6,14},... | collective-permute-start | bytes 958472 | tf_op jit(solution)/shard_map/ppermute | solution.py:42
  446.0 2.9 collective-permute-start.64
  451.0 6.9 %collective-permute-done.63 = bf16[208,768]{1,0:T(8,128)(2,1)S(1)} collective-permute-done((bf16[208,768]{1,0:T(8,128)(2,1)S(1)}, bf16[208,768]{1,0:T(8,128)(2,1)S(1)}, u32[]{:S(2)}, u32[]{:S(2)}) %collective-permute-start.63) | collective-permute-done | bytes 319520 | tf_op jit(solution)/shard_map/ppermute | solution.py:42
  457.9 3.3 collective-permute-done.62
  (434 shorter events, 160.3 us)
Async XLA Ops:
  25.8 27.8 %collective-permute-start.10 = (bf16[192,2304]{1,0:T(8,128)(2,1)S(1)}, bf16[192,2304]{1,0:T(8,128)(2,1)S(1)}, u32[]{:S(2)}, u32[]{:S(2)}) collective-permute-start(bf16[192,2304]{1,0:T(8,128)(2,1)S(1)} %concatenate.43.refs_1_.p0.refs_5_.refs_8_.refs_7_), channel_id=1, source_target_pairs={{0,1},{1,0},{2,3},{3,2},{4,5},{5,4},{6,7},{7,6},{8,9},{9,8},{10,11... | collective-permute-start | bytes 2654216 | tf_op jit(solution)/shard_map/ppermute | solution.py:36
  26.4 27.2 %collective-permute-start.11 = (bf16[192,2304]{1,0:T(8,128)(2,1)S(1)}, bf16[192,2304]{1,0:T(8,128)(2,1)}, u32[]{:S(2)}, u32[]{:S(2)}) collective-permute-start(bf16[192,2304]{1,0:T(8,128)(2,1)S(1)} %concatenate.43.refs_1_.p0.refs_5_.refs_8_.refs_7_), channel_id=1, source_target_pairs={{0,18},{1,19},{2,16},{3,17},{16,2},{17,3},{18,0},{19,1},{4,22},{5,... | collective-permute-start | bytes 2654216 | tf_op jit(solution)/shard_map/ppermute | solution.py:86
  28.5 15.0 %collective-permute-start.7 = (bf16[192,768]{1,0:T(8,128)(2,1)}, bf16[192,768]{1,0:T(8,128)(2,1)S(1)}, u32[]{:S(2)}, u32[]{:S(2)}) collective-permute-start(bf16[192,768]{1,0:T(8,128)(2,1)} %pad_maximum_fusion.9), channel_id=1, source_target_pairs={{0,4},{4,0},{8,12},{12,8},{1,5},{5,1},{9,13},{13,9},{2,6},{6,2},{1... | collective-permute-start | bytes 884744 | tf_op jit(solution)/shard_map/ppermute | solution.py:36
  29.4 24.3 %collective-permute-start.8 = (bf16[192,768]{1,0:T(8,128)(2,1)}, bf16[192,768]{1,0:T(8,128)(2,1)S(1)}, u32[]{:S(2)}, u32[]{:S(2)}) collective-permute-start(bf16[192,768]{1,0:T(8,128)(2,1)} %pad_maximum_fusion.9), channel_id=1, source_target_pairs={{0,8},{4,12},{8,0},{12,4},{1,9},{5,13},{9,1},{13,5},{2,10},{6,14},... | collective-permute-start | bytes 884744 | tf_op jit(solution)/shard_map/ppermute | solution.py:36
  33.7 20.0 %collective-permute-start.9 = (bf16[192,768]{1,0:T(8,128)(2,1)}, bf16[192,768]{1,0:T(8,128)(2,1)}, u32[]{:S(2)}, u32[]{:S(2)}) collective-permute-start(bf16[192,768]{1,0:T(8,128)(2,1)} %pad_maximum_fusion.9), channel_id=1, source_target_pairs={{0,12},{4,8},{8,4},{12,0},{1,13},{5,9},{9,5},{13,1},{2,14},{6,10},... | collective-permute-start | bytes 884744 | tf_op jit(solution)/shard_map/ppermute | solution.py:36
  55.9 20.2 %collective-permute-start.12 = (bf16[3,192,768]{2,1,0:T(8,128)(2,1)}, bf16[3,192,768]{2,1,0:T(8,128)(2,1)}, u32[]{:S(2)}, u32[]{:S(2)}) collective-permute-start(bf16[3,192,768]{2,1,0:T(8,128)(2,1)} %pad_maximum_fusion.refs_6_.refs_7_.refs_10_.refs_11_.p5.p6), channel_id=1, source_target_pairs={{0,1},{1,0},{2,3},{3,2},{4,5},{5,4},{6,7},{7,6},{8,9},{9,8},{10,11... | collective-permute-start | bytes 2654216 | tf_op jit(solution)/shard_map/ppermute | solution.py:36
  57.8 36.2 %collective-permute-start.18 = (bf16[3,192,768]{2,1,0:T(8,128)(2,1)}, bf16[3,192,768]{2,1,0:T(8,128)(2,1)}, u32[]{:S(2)}, u32[]{:S(2)}) collective-permute-start(bf16[3,192,768]{2,1,0:T(8,128)(2,1)} %pad_maximum_fusion.refs_6_.refs_7_.refs_10_.refs_11_.p5.p6), channel_id=1, source_target_pairs={{0,18},{1,19},{2,16},{3,17},{16,2},{17,3},{18,0},{19,1},{4,22},{5,... | collective-permute-start | bytes 2654216 | tf_op jit(solution)/shard_map/ppermute | solution.py:86
  58.0 34.3 %collective-permute-start.19 = (bf16[192,1536]{1,0:T(8,128)(2,1)}, bf16[192,1536]{1,0:T(8,128)(2,1)S(1)}, u32[]{:S(2)}, u32[]{:S(2)}) collective-permute-start(bf16[192,1536]{1,0:T(8,128)(2,1)} %pad_maximum_fusion.4), channel_id=1, source_target_pairs={{0,4},{4,0},{8,12},{12,8},{1,5},{5,1},{9,13},{13,9},{2,6},{6,2},{1... | collective-permute-start | bytes 1769480 | tf_op jit(solution)/shard_map/ppermute | solution.py:36
  64.1 29.8 %collective-permute-start.20 = (bf16[192,1536]{1,0:T(8,128)(2,1)}, bf16[192,1536]{1,0:T(8,128)(2,1)}, u32[]{:S(2)}, u32[]{:S(2)}) collective-permute-start(bf16[192,1536]{1,0:T(8,128)(2,1)} %pad_maximum_fusion.4), channel_id=1, source_target_pairs={{0,8},{4,12},{8,0},{12,4},{1,9},{5,13},{9,1},{13,5},{2,10},{6,14},... | collective-permute-start | bytes 1769480 | tf_op jit(solution)/shard_map/ppermute | solution.py:36
  65.9 23.5 %collective-permute-start.16 = (bf16[192,1152]{1,0:T(8,128)(2,1)}, bf16[192,1152]{1,0:T(8,128)(2,1)S(1)}, u32[]{:S(2)}, u32[]{:S(2)}) collective-permute-start(bf16[192,1152]{1,0:T(8,128)(2,1)} %slice.434), channel_id=1, source_target_pairs={{0,18},{1,19},{2,16},{3,17},{16,2},{17,3},{18,0},{19,1},{4,22},{5,... | collective-permute-start | bytes 1327112 | tf_op jit(solution)/shard_map/ppermute | solution.py:86
  76.1 15.6 %collective-permute-start.17 = (bf16[192,1152]{1,0:T(8,128)(2,1)}, bf16[192,1152]{1,0:T(8,128)(2,1)S(1)}, u32[]{:S(2)}, u32[]{:S(2)}) collective-permute-start(bf16[192,1152]{1,0:T(8,128)(2,1)} %slice.435), channel_id=1, source_target_pairs={{0,1},{1,0},{2,3},{3,2},{4,5},{5,4},{6,7},{7,6},{8,9},{9,8},{10,11... | collective-permute-start | bytes 1327112 | tf_op jit(solution)/shard_map/ppermute | solution.py:36
  89.3 25.3 %collective-permute-start.24 = (bf16[192,1536]{1,0:T(8,128)(2,1)}, bf16[192,1536]{1,0:T(8,128)(2,1)}, u32[]{:S(2)}, u32[]{:S(2)}) collective-permute-start(bf16[192,1536]{1,0:T(8,128)(2,1)} %pad_maximum_fusion.4), channel_id=1, source_target_pairs={{0,12},{4,8},{8,4},{12,0},{1,13},{5,9},{9,5},{13,1},{2,14},{6,10},... | collective-permute-start | bytes 1769480 | tf_op jit(solution)/shard_map/ppermute | solution.py:36
  95.8 18.9 %collective-permute-start.21 = (bf16[3,192,384]{2,1,0:T(8,128)(2,1)}, bf16[3,192,384]{2,1,0:T(8,128)(2,1)S(1)}, u32[]{:S(2)}, u32[]{:S(2)}) collective-permute-start(bf16[3,192,384]{2,1,0:T(8,128)(2,1)} %slice.343), channel_id=1, source_target_pairs={{0,18},{1,19},{2,16},{3,17},{16,2},{17,3},{18,0},{19,1},{4,22},{5,... | collective-permute-start | bytes 1327112 | tf_op jit(solution)/shard_map/ppermute | solution.py:86
  97.6 17.1 %collective-permute-start.22 = (bf16[3,192,384]{2,1,0:T(8,128)(2,1)}, bf16[3,192,384]{2,1,0:T(8,128)(2,1)S(1)}, u32[]{:S(2)}, u32[]{:S(2)}) collective-permute-start(bf16[3,192,384]{2,1,0:T(8,128)(2,1)} %slice.344), channel_id=1, source_target_pairs={{0,1},{1,0},{2,3},{3,2},{4,5},{5,4},{6,7},{7,6},{8,9},{9,8},{10,11... | collective-permute-start | bytes 1327112 | tf_op jit(solution)/shard_map/ppermute | solution.py:36
  105.2 18.5 %collective-permute-start.14 = (bf16[2,128,768]{2,1,0:T(8,128)(2,1)S(1)}, bf16[2,128,768]{2,1,0:T(8,128)(2,1)S(1)}, u32[]{:S(2)}, u32[]{:S(2)}) collective-permute-start(bf16[2,128,768]{2,1,0:T(8,128)(2,1)S(1)} %pad_maximum_fusion.6), channel_id=1, source_target_pairs={{0,2},{1,3},{2,0},{3,1},{4,6},{5,7},{6,4},{7,5},{8,10},{9,11},{10,... | collective-permute-start | bytes 1179656 | tf_op jit(solution)/shard_map/ppermute | solution.py:36
  118.6 19.2 %collective-permute-start.25 = (bf16[3,192,768]{2,1,0:T(8,128)(2,1)}, bf16[3,192,768]{2,1,0:T(8,128)(2,1)}, u32[]{:S(2)}, u32[]{:S(2)}) collective-permute-start(bf16[3,192,768]{2,1,0:T(8,128)(2,1)} %pad_maximum_fusion.1.p5.refs_13_.refs_12_), channel_id=1, source_target_pairs={{0,1},{1,0},{2,3},{3,2},{4,5},{5,4},{6,7},{7,6},{8,9},{9,8},{10,11... | collective-permute-start | bytes 2654216 | tf_op jit(solution)/shard_map/ppermute | solution.py:36
  124.8 13.0 %collective-permute-start.15 = (bf16[512,768]{1,0:T(8,128)(2,1)}, bf16[512,768]{1,0:T(8,128)(2,1)}, u32[]{:S(2)}, u32[]{:S(2)}) collective-permute-start(bf16[512,768]{1,0:T(8,128)(2,1)} %pad_maximum_fusion.3), channel_id=1, source_target_pairs={{0,16},{16,0},{1,17},{17,1},{2,18},{18,2},{3,19},{19,3},{4,20},{20... | collective-permute-start | bytes 2359304 | tf_op jit(solution)/shard_map/ppermute | solution.py:32
  127.0 24.5 %collective-permute-start.28 = (bf16[3,192,768]{2,1,0:T(8,128)(2,1)S(1)}, bf16[3,192,768]{2,1,0:T(8,128)(2,1)S(1)}, u32[]{:S(2)}, u32[]{:S(2)}) collective-permute-start(bf16[3,192,768]{2,1,0:T(8,128)(2,1)S(1)} %pad_maximum_fusion.2.p6.refs_14_.refs_13_), channel_id=1, source_target_pairs={{0,18},{1,19},{2,16},{3,17},{16,2},{17,3},{18,0},{19,1},{4,22},{5,... | collective-permute-start | bytes 2654216 | tf_op jit(solution)/shard_map/ppermute | solution.py:86
  128.3 32.3 %collective-permute-start.26 = (bf16[3,192,768]{2,1,0:T(8,128)(2,1)S(1)}, bf16[3,192,768]{2,1,0:T(8,128)(2,1)S(1)}, u32[]{:S(2)}, u32[]{:S(2)}) collective-permute-start(bf16[3,192,768]{2,1,0:T(8,128)(2,1)S(1)} %pad_maximum_fusion.2.p6.refs_14_.refs_13_), channel_id=1, source_target_pairs={{0,1},{1,0},{2,3},{3,2},{4,5},{5,4},{6,7},{7,6},{8,9},{9,8},{10,11... | collective-permute-start | bytes 2654216 | tf_op jit(solution)/shard_map/ppermute | solution.py:36
  129.6 38.2 %collective-permute-start.27 = (bf16[3,192,768]{2,1,0:T(8,128)(2,1)}, bf16[3,192,768]{2,1,0:T(8,128)(2,1)S(1)}, u32[]{:S(2)}, u32[]{:S(2)}) collective-permute-start(bf16[3,192,768]{2,1,0:T(8,128)(2,1)} %pad_maximum_fusion.1.p5.refs_13_.refs_12_), channel_id=1, source_target_pairs={{0,18},{1,19},{2,16},{3,17},{16,2},{17,3},{18,0},{19,1},{4,22},{5,... | collective-permute-start | bytes 2654216 | tf_op jit(solution)/shard_map/ppermute | solution.py:86
  137.8 48.9 %collective-permute-start.29 = (bf16[3,192,768]{2,1,0:T(8,128)(2,1)}, bf16[3,192,768]{2,1,0:T(8,128)(2,1)S(1)}, u32[]{:S(2)}, u32[]{:S(2)}) collective-permute-start(bf16[3,192,768]{2,1,0:T(8,128)(2,1)} %collective-permute-done.25.p7.refs_15_.refs_14_), channel_id=1, source_target_pairs={{0,18},{1,19},{2,16},{3,17},{16,2},{17,3},{18,0},{19,1},{4,22},{5,... | collective-permute-start | bytes 2654216 | tf_op jit(solution)/shard_map/ppermute | solution.py:86
  151.5 35.2 %collective-permute-start.30 = (bf16[3,192,768]{2,1,0:T(8,128)(2,1)S(1)}, bf16[3,192,768]{2,1,0:T(8,128)(2,1)S(1)}, u32[]{:S(2)}, u32[]{:S(2)}) collective-permute-start(bf16[3,192,768]{2,1,0:T(8,128)(2,1)S(1)} %collective-permute-done.28.p10.refs_18_.refs_17_), channel_id=1, source_target_pairs={{0,1},{1,0},{2,3},{3,2},{4,5},{5,4},{6,7},{7,6},{8,9},{9,8},{10,11... | collective-permute-start | bytes 2654216 | tf_op jit(solution)/shard_map/ppermute | solution.py:36
  154.0 32.7 %collective-permute-start.23 = (bf16[512,768]{1,0:T(8,128)(2,1)S(1)}, bf16[512,768]{1,0:T(8,128)(2,1)S(1)}, u32[]{:S(2)}, u32[]{:S(2)}) collective-permute-start(bf16[512,768]{1,0:T(8,128)(2,1)S(1)} %get-tuple-element.172.own), channel_id=1, source_target_pairs={{0,16},{16,0},{1,17},{17,1},{2,18},{18,2},{3,19},{19,3},{4,20},{20... | collective-permute-start | bytes 2359304 | tf_op jit(solution)/shard_map/ppermute | solution.py:32
  275.4 32.8 %collective-permute-start.41 = (bf16[4,192,1536]{2,1,0:T(8,128)(2,1)}, bf16[4,192,1536]{2,1,0:T(8,128)(2,1)}, u32[]{:S(2)}, u32[]{:S(2)}) collective-permute-start(bf16[4,192,1536]{2,1,0:T(8,128)(2,1)} %get-tuple-element.242), channel_id=1, source_target_pairs={{0,18},{1,19},{2,16},{3,17},{4,22},{5,23},{6,20},{7,21},{8,26},{9,... | collective-permute-start | bytes 7077896 | tf_op jit(solution)/shard_map/ppermute | solution.py:48
  279.8 28.4 %collective-permute-start.42 = (bf16[2,192,1536]{2,1,0:T(8,128)(2,1)S(1)}, bf16[2,192,1536]{2,1,0:T(8,128)(2,1)S(1)}, u32[]{:S(2)}, u32[]{:S(2)}) collective-permute-start(bf16[2,192,1536]{2,1,0:T(8,128)(2,1)S(1)} %get-tuple-element.201), channel_id=1, source_target_pairs={{0,1},{1,0},{2,3},{3,2},{4,5},{5,4},{6,7},{7,6},{8,9},{9,8},{10,11... | collective-permute-start | bytes 3538952 | tf_op jit(solution)/shard_map/ppermute | solution.py:36
  293.4 23.0 %collective-permute-start.43 = (bf16[512,768]{1,0:T(8,128)(2,1)S(1)}, bf16[512,768]{1,0:T(8,128)(2,1)S(1)}, u32[]{:S(2)}, u32[]{:S(2)}) collective-permute-start(bf16[512,768]{1,0:T(8,128)(2,1)S(1)} %get-tuple-element.224.refs_1_), channel_id=1, source_target_pairs={{0,16},{16,0},{1,17},{17,1},{2,18},{18,2},{3,19},{19,3},{4,20},{20... | collective-permute-start | bytes 2359304 | tf_op jit(solution)/shard_map/ppermute | solution.py:32
  297.7 26.8 %collective-permute-start.44 = (bf16[4,208,768]{2,1,0:T(8,128)(2,1)S(1)}, bf16[4,208,768]{2,1,0:T(8,128)(2,1)}, u32[]{:S(2)}, u32[]{:S(2)}) collective-permute-start(bf16[4,208,768]{2,1,0:T(8,128)(2,1)S(1)} %get-tuple-element.257), channel_id=1, source_target_pairs={{0,18},{1,19},{2,16},{3,17},{4,22},{5,23},{6,20},{7,21},{8,26},{9,... | collective-permute-start | bytes 3833864 | tf_op jit(solution)/shard_map/ppermute | solution.py:48
  302.8 21.7 %collective-permute-start.45 = (bf16[2,208,768]{2,1,0:T(8,128)(2,1)S(1)}, bf16[2,208,768]{2,1,0:T(8,128)(2,1)S(1)}, u32[]{:S(2)}, u32[]{:S(2)}) collective-permute-start(bf16[2,208,768]{2,1,0:T(8,128)(2,1)S(1)} %get-tuple-element.218), channel_id=1, source_target_pairs={{0,1},{1,0},{2,3},{3,2},{4,5},{5,4},{6,7},{7,6},{8,9},{9,8},{10,11... | collective-permute-start | bytes 1916936 | tf_op jit(solution)/shard_map/ppermute | solution.py:36
  309.6 29.8 %collective-permute-start.47 = (bf16[2,192,1536]{2,1,0:T(8,128)(2,1)}, bf16[2,192,1536]{2,1,0:T(8,128)(2,1)}, u32[]{:S(2)}, u32[]{:S(2)}) collective-permute-start(bf16[2,192,1536]{2,1,0:T(8,128)(2,1)} %add_convert_fusion.6), channel_id=1, source_target_pairs={{0,18},{1,19},{2,16},{3,17},{4,22},{5,23},{6,20},{7,21},{8,26},{9,... | collective-permute-start | bytes 3538952 | tf_op jit(solution)/shard_map/ppermute | solution.py:48
  314.7 26.1 %collective-permute-start.46 = (bf16[2,192,1536]{2,1,0:T(8,128)(2,1)}, bf16[2,192,1536]{2,1,0:T(8,128)(2,1)}, u32[]{:S(2)}, u32[]{:S(2)}) collective-permute-start(bf16[2,192,1536]{2,1,0:T(8,128)(2,1)} %add_convert_fusion.7), channel_id=1, source_target_pairs={{16,17},{17,16},{18,19},{19,18},{20,21},{21,20},{22,23},{23,22},{2... | collective-permute-start | bytes 3538952 | tf_op jit(solution)/shard_map/ppermute | solution.py:42
  324.4 22.8 %collective-permute-start.48 = (bf16[512,768]{1,0:T(8,128)(2,1)S(1)}, bf16[512,768]{1,0:T(8,128)(2,1)S(1)}, u32[]{:S(2)}, u32[]{:S(2)}) collective-permute-start(bf16[512,768]{1,0:T(8,128)(2,1)S(1)} %get-tuple-element.233.own), channel_id=1, source_target_pairs={{0,16},{16,0},{1,17},{17,1},{2,18},{18,2},{3,19},{19,3},{4,20},{20... | collective-permute-start | bytes 2359304 | tf_op jit(solution)/shard_map/ppermute | solution.py:32
  326.4 35.5 %collective-permute-start.52 = (bf16[2,208,768]{2,1,0:T(8,128)(2,1)}, bf16[2,208,768]{2,1,0:T(8,128)(2,1)}, u32[]{:S(2)}, u32[]{:S(2)}) collective-permute-start(bf16[2,208,768]{2,1,0:T(8,128)(2,1)} %add_convert_fusion.14), channel_id=1, source_target_pairs={{0,18},{1,19},{2,16},{3,17},{4,22},{5,23},{6,20},{7,21},{8,26},{9,... | collective-permute-start | bytes 1916936 | tf_op jit(solution)/shard_map/ppermute | solution.py:48
  332.0 33.4 %collective-permute-start.51 = (bf16[2,208,768]{2,1,0:T(8,128)(2,1)}, bf16[2,208,768]{2,1,0:T(8,128)(2,1)}, u32[]{:S(2)}, u32[]{:S(2)}) collective-permute-start(bf16[2,208,768]{2,1,0:T(8,128)(2,1)} %add_convert_fusion.15), channel_id=1, source_target_pairs={{16,17},{17,16},{18,19},{19,18},{20,21},{21,20},{22,23},{23,22},{2... | collective-permute-start | bytes 1916936 | tf_op jit(solution)/shard_map/ppermute | solution.py:42
  339.4 31.2 %collective-permute-start.50 = (bf16[2,192,1536]{2,1,0:T(8,128)(2,1)S(1)}, bf16[2,192,1536]{2,1,0:T(8,128)(2,1)S(1)}, u32[]{:S(2)}, u32[]{:S(2)}) collective-permute-start(bf16[2,192,1536]{2,1,0:T(8,128)(2,1)S(1)} %get-tuple-element.240), channel_id=1, source_target_pairs={{0,1},{1,0},{2,3},{3,2},{4,5},{5,4},{6,7},{7,6},{8,9},{9,8},{10,11... | collective-permute-start | bytes 3538952 | tf_op jit(solution)/shard_map/ppermute | solution.py:36
  340.9 30.6 %collective-permute-start.49 = (bf16[4,192,1536]{2,1,0:T(8,128)(2,1)}, bf16[4,192,1536]{2,1,0:T(8,128)(2,1)}, u32[]{:S(2)}, u32[]{:S(2)}) collective-permute-start(bf16[4,192,1536]{2,1,0:T(8,128)(2,1)} %get-tuple-element.279), channel_id=1, source_target_pairs={{16,2},{17,3},{18,0},{19,1},{20,6},{21,7},{22,4},{23,5},{24,10},{2... | collective-permute-start | bytes 7077896 | tf_op jit(solution)/shard_map/ppermute | solution.py:48
  347.2 38.1 %collective-permute-start.58 = (bf16[2,192,1536]{2,1,0:T(8,128)(2,1)}, bf16[2,192,1536]{2,1,0:T(8,128)(2,1)}, u32[]{:S(2)}, u32[]{:S(2)}) collective-permute-start(bf16[2,192,1536]{2,1,0:T(8,128)(2,1)} %add_convert_fusion.4), channel_id=1, source_target_pairs={{16,24},{20,28},{24,16},{28,20},{17,25},{21,29},{25,17},{29,21},{1... | collective-permute-start | bytes 3538952 | tf_op jit(solution)/shard_map/ppermute | solution.py:42
  361.9 17.6 %collective-permute-start.68 = (bf16[512,768]{1,0:T(8,128)(2,1)S(1)}, bf16[512,768]{1,0:T(8,128)(2,1)S(1)}, u32[]{:S(2)}, u32[]{:S(2)}) collective-permute-start(bf16[512,768]{1,0:T(8,128)(2,1)S(1)} %get-tuple-element.256), channel_id=1, source_target_pairs={{0,16},{16,0},{1,17},{17,1},{2,18},{18,2},{3,19},{19,3},{4,20},{20... | collective-permute-start | bytes 2359304 | tf_op jit(solution)/shard_map/ppermute | solution.py:32
  367.6 37.8 %collective-permute-start.55 = (bf16[2,208,768]{2,1,0:T(8,128)(2,1)}, bf16[2,208,768]{2,1,0:T(8,128)(2,1)}, u32[]{:S(2)}, u32[]{:S(2)}) collective-permute-start(bf16[2,208,768]{2,1,0:T(8,128)(2,1)} %add_convert_fusion.12), channel_id=1, source_target_pairs={{16,24},{20,28},{24,16},{28,20},{17,25},{21,29},{25,17},{29,21},{1... | collective-permute-start | bytes 1916936 | tf_op jit(solution)/shard_map/ppermute | solution.py:42
  372.8 18.0 %collective-permute-start.57 = (bf16[2,192,1536]{2,1,0:T(8,128)(2,1)}, bf16[2,192,1536]{2,1,0:T(8,128)(2,1)}, u32[]{:S(2)}, u32[]{:S(2)}) collective-permute-start(bf16[2,192,1536]{2,1,0:T(8,128)(2,1)} %add_convert_fusion.2), channel_id=1, source_target_pairs={{16,2},{17,3},{18,0},{19,1},{20,6},{21,7},{22,4},{23,5},{24,10},{2... | collective-permute-start | bytes 3538952 | tf_op jit(solution)/shard_map/ppermute | solution.py:48
  376.8 24.9 %collective-permute-start.56 = (bf16[2,192,1536]{2,1,0:T(8,128)(2,1)}, bf16[2,192,1536]{2,1,0:T(8,128)(2,1)}, u32[]{:S(2)}, u32[]{:S(2)}) collective-permute-start(bf16[2,192,1536]{2,1,0:T(8,128)(2,1)} %add_convert_fusion.3), channel_id=1, source_target_pairs={{0,1},{1,0},{2,3},{3,2},{4,5},{5,4},{6,7},{7,6},{8,9},{9,8},{10,11... | collective-permute-start | bytes 3538952 | tf_op jit(solution)/shard_map/ppermute | solution.py:42
  383.8 33.2 %collective-permute-start.54 = (bf16[2,208,768]{2,1,0:T(8,128)(2,1)S(1)}, bf16[2,208,768]{2,1,0:T(8,128)(2,1)S(1)}, u32[]{:S(2)}, u32[]{:S(2)}) collective-permute-start(bf16[2,208,768]{2,1,0:T(8,128)(2,1)S(1)} %get-tuple-element.276), channel_id=1, source_target_pairs={{0,1},{1,0},{2,3},{3,2},{4,5},{5,4},{6,7},{7,6},{8,9},{9,8},{10,11... | collective-permute-start | bytes 1916936 | tf_op jit(solution)/shard_map/ppermute | solution.py:36
  385.3 31.7 %collective-permute-start.53 = (bf16[4,208,768]{2,1,0:T(8,128)(2,1)S(1)}, bf16[4,208,768]{2,1,0:T(8,128)(2,1)S(1)}, u32[]{:S(2)}, u32[]{:S(2)}) collective-permute-start(bf16[4,208,768]{2,1,0:T(8,128)(2,1)S(1)} %get-tuple-element.291), channel_id=1, source_target_pairs={{16,2},{17,3},{18,0},{19,1},{20,6},{21,7},{22,4},{23,5},{24,10},{2... | collective-permute-start | bytes 3833864 | tf_op jit(solution)/shard_map/ppermute | solution.py:48
  405.6 16.7 %collective-permute-start.59 = (bf16[192,1536]{1,0:T(8,128)(2,1)S(1)}, bf16[192,1536]{1,0:T(8,128)(2,1)S(1)}, u32[]{:S(2)}, u32[]{:S(2)}) collective-permute-start(bf16[192,1536]{1,0:T(8,128)(2,1)S(1)} %get-tuple-element.363), channel_id=1, source_target_pairs={{0,4},{4,0},{8,12},{12,8},{1,5},{5,1},{9,13},{13,9},{2,6},{6,2},{1... | collective-permute-start | bytes 1769480 | tf_op jit(solution)/shard_map/ppermute | solution.py:42
  407.6 25.4 %collective-permute-start.66 = (bf16[192,1536]{1,0:T(8,128)(2,1)S(1)}, bf16[192,1536]{1,0:T(8,128)(2,1)S(1)}, u32[]{:S(2)}, u32[]{:S(2)}) collective-permute-start(bf16[192,1536]{1,0:T(8,128)(2,1)S(1)} %get-tuple-element.361), channel_id=1, source_target_pairs={{0,8},{4,12},{8,0},{12,4},{1,9},{5,13},{9,1},{13,5},{2,10},{6,14},... | collective-permute-start | bytes 1769480 | tf_op jit(solution)/shard_map/ppermute | solution.py:42
  411.6 21.4 %collective-permute-start.67 = (bf16[192,1536]{1,0:T(8,128)(2,1)S(1)}, bf16[192,1536]{1,0:T(8,128)(2,1)S(1)}, u32[]{:S(2)}, u32[]{:S(2)}) collective-permute-start(bf16[192,1536]{1,0:T(8,128)(2,1)S(1)} %get-tuple-element.360), channel_id=1, source_target_pairs={{0,12},{4,8},{8,4},{12,0},{1,13},{5,9},{9,5},{13,1},{2,14},{6,10},... | collective-permute-start | bytes 1769480 | tf_op jit(solution)/shard_map/ppermute | solution.py:42
  433.0 17.9 %collective-permute-start.70 = (bf16[2,128,768]{2,1,0:T(8,128)(2,1)S(1)}, bf16[2,128,768]{2,1,0:T(8,128)(2,1)S(1)}, u32[]{:S(2)}, u32[]{:S(2)}) collective-permute-start(bf16[2,128,768]{2,1,0:T(8,128)(2,1)S(1)} %pad_maximum_fusion.8), channel_id=1, source_target_pairs={{0,2},{1,3},{2,0},{3,1},{4,6},{5,7},{6,4},{7,5},{8,10},{9,11},{10,... | collective-permute-start | bytes 1179656 | tf_op jit(solution)/shard_map/ppermute | solution.py:36
  437.9 23.3 %collective-permute-start.65 = (bf16[208,2304]{1,0:T(8,128)(2,1)S(1)}, bf16[208,2304]{1,0:T(8,128)(2,1)S(1)}, u32[]{:S(2)}, u32[]{:S(2)}) collective-permute-start(bf16[208,2304]{1,0:T(8,128)(2,1)S(1)} %fusion.1), channel_id=1, source_target_pairs={{16,20},{20,16},{24,28},{28,24},{17,21},{21,17},{25,29},{29,25},{1... | collective-permute-start | bytes 2875400 | tf_op jit(solution)/shard_map/ppermute | solution.py:42
  438.7 19.2 %collective-permute-start.63 = (bf16[208,768]{1,0:T(8,128)(2,1)S(1)}, bf16[208,768]{1,0:T(8,128)(2,1)S(1)}, u32[]{:S(2)}, u32[]{:S(2)}) collective-permute-start(bf16[208,768]{1,0:T(8,128)(2,1)S(1)} %get-tuple-element.382), channel_id=1, source_target_pairs={{0,8},{4,12},{8,0},{12,4},{1,9},{5,13},{9,1},{13,5},{2,10},{6,14},... | collective-permute-start | bytes 958472 | tf_op jit(solution)/shard_map/ppermute | solution.py:42
  (111 other events, 1772.7 us)
